TPU v7x, 32 devices: a whole 2x2x4 slice. The times are simulated.
32 devices in a mesh: groups: 2 (over y), req: 4 (over x, core), head: 4 (over z).
Axes of the slice: x: 2, y: 2, z: 4, core: 2. Of those that a mesh axis runs over, the one named last changes fastest.
Arguments:
- ssm_state: float32 [64, 128, 64, 128], P(('groups', 'req'), 'head'), parts along dimension 0, may hold values from -6 to 6
- conv_state: float32 [64, 3, 8, 1280], P(('groups', 'req'), None, 'head'), parts along dimension 0, may hold values from -6 to 6
- counts: int32 [8], P('groups'), parts along dimension 0, may hold values from 4 to 8, as said below
- request_slot: int32 [64], P('groups'), parts along dimension 0, may hold values from 0 to 31, as said below
- token_xbc: bfloat16 [2, 64, 8, 1280], P(None, ('groups', 'req'), 'head'), parts along dimension 1, may hold values from -6 to 6
- token_z: bfloat16 [2, 64, 8192], P(None, ('groups', 'req'), 'head'), parts along dimension 1, may hold values from -6 to 6
- token_dt: bfloat16 [2, 64, 128], P(None, ('groups', 'req'), 'head'), parts along dimension 1, may hold values from -6 to 6
- conv_weight: bfloat16 [4, 8, 1280], P(None, 'head'), may hold values from -3 to 3
- conv_bias: bfloat16 [8, 1280], P('head'), may hold values from -2 to 2
- a_log: bfloat16 [128], P('head'), may hold values from 0 to 2.5
- dt_bias: bfloat16 [128], P('head'), may hold values from -4 to -1
- d_skip: bfloat16 [128], P('head'), may hold values from 0.5 to 2
- norm_gain: bfloat16 [8192], P('head'), may hold values from 0.5 to 1.5
- out_weight: bfloat16 [8192, 8192], P('head', 'req'), may hold values from -0.0625 to 0.0625
Outputs:
- layer_out: bfloat16 [2, 64, 8192], P(None, ('groups', 'head'), 'req'), parts along dimension 1
- decode_ssm: float32 [8, 4, 4, 64, 64, 128], P(('groups', 'req'), 'head'), parts along dimension 0
- decode_conv: float32 [8, 4, 4, 3, 4, 1280], P(('groups', 'req'), 'head'), parts along dimension 0
There are 2 independent parts, one for each index of `groups`. A program takes and returns all parts, laid end to end along the dimension named above; an argument that names none is the same for every part. Nothing has to cross between parts.
Inputs may be any that keep to these rules, and one draw needn't show every extreme that they name: `counts`: some prefill group has all 8 rows live, and another has only 4. Slot s lies with index s // 8 of req. request_slot is one-to-one over all rows. The rows of one prefill group name at most 2 slots of any one index of req, and exactly 2 for some.
All inputs are finite; a program needn't handle non-finite values.
Results may differ from a plain program's by a relative error of at most 0.0049.
Values may be sent and summed in bfloat16 or wider, within the bound.
No kernel may reach another device: no remote copies, remote signals or barrier semaphores. Data moves between devices by JAX's collectives and lax.ppermute only.
A program may use at most 192 MiB of HBM per device.

v0:
```python
import jax
import jax.numpy as jnp
from jax import lax
from jax.sharding import PartitionSpec as P

H = 128
P_SIZE = 64
N = 128
G = 8
R_PF = 8


def from_partner(value, axis, bit):
    mask = 2**bit
    pairs = [(source, source ^ mask) for source in range(lax.axis_size(axis))]
    return lax.ppermute(value, axis, pairs)


def advance(
    ssm_now,
    conv_now,
    xbc_now,
    z_now,
    dt_now,
    conv_weight,
    conv_bias,
    a_log,
    dt_bias,
    d_skip,
    norm_gain,
):
    batch = ssm_now.shape[0]
    window = jnp.concatenate([conv_now, xbc_now.astype(jnp.float32)[:, None]], axis=1)
    conv_out = (
        jnp.sum(window * conv_weight.astype(jnp.float32)[None], axis=1)
        + conv_bias.astype(jnp.float32)[None]
    )
    activated = jax.nn.silu(conv_out)
    groups = activated.shape[1]
    per_group = H // G
    x_width = per_group * P_SIZE
    x_heads = activated[..., :x_width].reshape(batch, groups * per_group, P_SIZE)
    b_heads = jnp.repeat(activated[..., x_width : x_width + N], per_group, axis=1)
    c_heads = jnp.repeat(activated[..., x_width + N :], per_group, axis=1)
    step_size = jax.nn.softplus(dt_now.astype(jnp.float32) + dt_bias.astype(jnp.float32)[None])
    decay_rate = jnp.exp(-step_size * jnp.exp(a_log.astype(jnp.float32))[None])
    ssm_now = (
        decay_rate[..., None, None] * ssm_now
        + (step_size[..., None] * x_heads)[..., None] * b_heads[:, :, None, :]
    )
    readout = (
        jnp.sum(ssm_now * c_heads[:, :, None, :], axis=-1)
        + d_skip.astype(jnp.float32)[None, :, None] * x_heads
    )
    gated_y = readout.reshape(batch, -1) * jax.nn.silu(z_now.astype(jnp.float32))
    grouped = gated_y.reshape(batch, groups, x_width)
    normed = grouped * lax.rsqrt(jnp.mean(grouped * grouped, axis=-1, keepdims=True) + 1e-05)
    normed = (normed.reshape(batch, -1) * norm_gain.astype(jnp.float32)[None]).astype(jnp.bfloat16)
    return (ssm_now, window[:, 1:], normed)


def pair_join(mine, partner, parity, axis):
    first = jnp.concatenate([mine, partner], axis=axis)
    second = jnp.concatenate([partner, mine], axis=axis)
    return jnp.where(parity == 0, first, second)


def rank_rows(dest_rows, live_rows, bit_rows, group_count):
    shaped_dest = dest_rows.reshape(group_count, R_PF)
    shaped_live = live_rows.reshape(group_count, R_PF)
    shaped_bit = bit_rows.reshape(group_count, R_PF)
    order_ids = jnp.arange(R_PF, dtype=jnp.int32)
    earlier = order_ids[None, :] < order_ids[:, None]
    matches = (
        (shaped_dest[:, :, None] == shaped_dest[:, None, :])
        & (shaped_bit[:, :, None] == shaped_bit[:, None, :])
        & shaped_live[:, None, :]
        & earlier[None]
    )
    return jnp.sum(matches.astype(jnp.int32), axis=2).reshape(-1)


def pack_index(mine_dest, mine_rank, mine_mask, group_count, capacity):
    chosen = (
        (mine_dest[None, None, :] == jnp.arange(group_count, dtype=jnp.int32)[:, None, None])
        & (mine_rank[None, None, :] == jnp.arange(capacity, dtype=jnp.int32)[None, :, None])
        & mine_mask[None, None, :]
    )
    row_index = jnp.sum(
        chosen.astype(jnp.int32) * jnp.arange(R_PF, dtype=jnp.int32)[None, None, :], axis=-1
    ).reshape(-1)
    valid_row = jnp.any(chosen, axis=-1).reshape(-1).astype(jnp.float32)
    return (row_index, valid_row)


def pack_rows(values, row_index, valid_row):
    taken = jnp.take(values, row_index, axis=0)
    return taken * valid_row.reshape((-1,) + (1,) * (values.ndim - 1))


def locate(targets, request_slot, live_rows, slot_code):
    matches = (request_slot[None, :] == targets[:, None]) & live_rows[None, :]
    position = jnp.sum(matches.astype(jnp.int32) * slot_code[None, :], axis=-1)
    present = jnp.any(matches, axis=-1).astype(jnp.float32)
    return (position, present)


def on_device(
    ssm_state,
    conv_state,
    counts,
    request_slot,
    token_xbc,
    token_z,
    token_dt,
    conv_weight,
    conv_bias,
    a_log,
    dt_bias,
    d_skip,
    norm_gain,
    out_weight,
):
    req_count = lax.axis_size("req")
    my_req = lax.axis_index("req")
    parity = lax.axis_index("head") % 2
    capacity = (R_PF + req_count - 1) // req_count
    slot_dev = R_PF // 2
    step_count = token_xbc.shape[0]
    row_ids = jnp.arange(R_PF * req_count, dtype=jnp.int32)
    group_ids = row_ids // R_PF
    live_rows = row_ids % R_PF < counts[group_ids]
    dest_rows = request_slot // R_PF
    bit_rows = request_slot // slot_dev % 2
    mine_dest = lax.dynamic_slice_in_dim(dest_rows, my_req * R_PF, R_PF)
    mine_bit = lax.dynamic_slice_in_dim(bit_rows, my_req * R_PF, R_PF)
    mine_live = lax.dynamic_slice_in_dim(live_rows, my_req * R_PF, R_PF)

    def split_slots(values):
        shaped = values.reshape((step_count, 2, slot_dev) + values.shape[2:])
        kept_rows = lax.dynamic_index_in_dim(shaped, parity, 1, keepdims=False)
        given_rows = lax.dynamic_index_in_dim(shaped, 1 - parity, 1, keepdims=False)
        return (kept_rows, given_rows)

    kept_xbc, given_xbc = split_slots(token_xbc)
    kept_z, given_z = split_slots(token_z)
    kept_dt, given_dt = split_slots(token_dt)
    received = from_partner(
        (
            given_xbc,
            given_z,
            given_dt,
            conv_weight,
            conv_bias,
            a_log,
            dt_bias,
            d_skip,
            norm_gain,
            out_weight,
        ),
        "head",
        0,
    )
    xbc_pair = pair_join(kept_xbc, received[0], parity, 2)
    z_pair = pair_join(kept_z, received[1], parity, 2)
    dt_pair = pair_join(kept_dt, received[2], parity, 2)
    conv_w_pair = pair_join(conv_weight, received[3], parity, 1)
    conv_b_pair = pair_join(conv_bias, received[4], parity, 0)
    a_log_pair = pair_join(a_log, received[5], parity, 0)
    dt_bias_pair = pair_join(dt_bias, received[6], parity, 0)
    d_skip_pair = pair_join(d_skip, received[7], parity, 0)
    gain_pair = pair_join(norm_gain, received[8], parity, 0)
    w_pair = pair_join(out_weight, received[9], parity, 0)
    kept_mask = mine_live & (mine_bit == parity)
    given_mask = mine_live & (mine_bit != parity)
    kept_weight = kept_mask.astype(jnp.float32)[:, None, None, None]
    given_weight = given_mask.astype(jnp.float32)[:, None, None, None]
    partner_ssm, partner_conv = from_partner(
        (ssm_state * given_weight, conv_state * given_weight), "head", 0
    )
    joined_ssm = pair_join(ssm_state * kept_weight, partner_ssm, parity, 1)
    joined_conv = pair_join(conv_state * kept_weight, partner_conv, parity, 2)
    rank_all = rank_rows(dest_rows, live_rows, bit_rows, req_count)
    mine_rank = lax.dynamic_slice_in_dim(rank_all, my_req * R_PF, R_PF)
    row_index, valid_row = pack_index(mine_dest, mine_rank, kept_mask, req_count, capacity)
    got_ssm, got_conv = (
        lax.all_to_all(
            pack_rows(joined_ssm, row_index, valid_row),
            "req",
            split_axis=0,
            concat_axis=0,
            tiled=True,
        ),
        lax.all_to_all(
            pack_rows(joined_conv, row_index, valid_row),
            "req",
            split_axis=0,
            concat_axis=0,
            tiled=True,
        ),
    )
    targets = my_req * R_PF + parity * slot_dev + jnp.arange(slot_dev, dtype=jnp.int32)
    position, present = locate(targets, request_slot, live_rows, group_ids * capacity + rank_all)
    ssm_now = pack_rows(got_ssm, position, present)
    conv_now = pack_rows(got_conv, position, present)
    normed_steps = []
    for step_index in range(step_count):
        ssm_now, conv_now, normed = advance(
            ssm_now,
            conv_now,
            xbc_pair[step_index],
            z_pair[step_index],
            dt_pair[step_index],
            conv_w_pair,
            conv_b_pair,
            a_log_pair,
            dt_bias_pair,
            d_skip_pair,
            gain_pair,
        )
        normed_steps.append(normed)
    normed_all = jnp.stack(normed_steps)
    projected = jnp.einsum(
        "tsc,cd->tsd",
        lax.all_gather(normed_all, "req", axis=1, tiled=True),
        w_pair,
        preferred_element_type=jnp.float32,
    )
    projected = projected.reshape(step_count, req_count, slot_dev, projected.shape[-1])
    blank = jnp.zeros_like(projected)
    spread = jnp.where(
        parity == 0, jnp.stack([projected, blank], axis=2), jnp.stack([blank, projected], axis=2)
    )
    spread = spread.reshape(step_count, req_count * 2 * slot_dev, projected.shape[-1])
    layer_out = lax.psum_scatter(spread, "head", scatter_dimension=1, tiled=True).astype(
        jnp.bfloat16
    )
    return (layer_out, ssm_now[None, None], conv_now[None, None])


def solution(mesh):
    in_specs = (
        P(("groups", "req"), "head", None, None),
        P(("groups", "req"), None, "head", None),
        P("groups"),
        P("groups"),
        P(None, ("groups", "req"), "head", None),
        P(None, ("groups", "req"), "head"),
        P(None, ("groups", "req"), "head"),
        P(None, "head", None),
        P("head", None),
        P("head"),
        P("head"),
        P("head"),
        P("head"),
        P("head", "req"),
    )
    out_specs = (
        P(None, ("groups", "head"), "req"),
        P(("groups", "req"), "head", None, None, None, None),
        P(("groups", "req"), "head", None, None, None, None),
    )
    return jax.shard_map(
        on_device, mesh=mesh, in_specs=in_specs, out_specs=out_specs, check_vma=False
    )
```

profile of v0, /device:TPU:0, one launch (start us, length us, event | category | flops | bytes accessed | tf_op | source)
XLA Modules:
  0.0 550.0 jit_solution(16976998078469558591)
XLA Ops:
  7.2 1.5 fusion.57
  9.1 3.2 fusion.53
  13.1 12.5 %broadcast_multiply_fusion.1 = (f32[8,32,64,128]{3,2,1,0:T(8,128)}, f32[8,32,64,128]{3,2,1,0:T(8,128)}) fusion(f32[8,32,64,128]{3,2,1,0:T(8,128)} %param.14, f32[8]{0:T(128)S(1)} %get-tuple-element.17, f32[8]{0:T(128)S(1)} %get-tuple-element.45), kind=kLoop, calls=%fused_computation.20 | loop fusion | flops 4194304 | bytes 25165888 | tf_op jit(solution)/shard_map/mul | solution.py:181
  25.7 3.0 collective-permute-start.3
  30.5 184.1 %collective-permute-done.4 = f32[8,3,2,1280]{3,2,1,0:T(2,128)S(1)} collective-permute-done((f32[8,3,2,1280]{3,2,1,0:T(2,128)S(1)}, f32[8,3,2,1280]{3,2,1,0:T(2,128)S(1)}, u32[]{:S(2)}, u32[]{:S(2)}) %collective-permute-start.4) | collective-permute-done | bytes 245792 | tf_op jit(solution)/shard_map/ppermute | solution.py:16
  216.8 3.5 all-to-all-start.1
  220.3 19.2 %maximum_select_fusion = f32[8,64,64,128]{3,2,1,0:T(8,128)} fusion(f32[8,32,64,128]{3,2,1,0:T(8,128)} %collective-permute-done.3, f32[8,32,64,128]{3,2,1,0:T(8,128)} %get-tuple-element.19, pred[]{:T(512)S(6)} %eq.105), kind=kLoop, calls=%fused_computation.4 | loop fusion | flops 12582912 | bytes 33554432 | tf_op jit(solution)/shard_map/jit(_where)/select_n | solution.py:65
  239.5 13.5 %gather_fusion = f32[8,64,64,128]{3,2,1,0:T(8,128)} fusion(f32[8,64,64,128]{3,2,1,0:T(8,128)} %maximum_select_fusion, s32[1024]{0:T(1024)S(1)} %pad_clamp_fusion.1), kind=kCustom, calls=%fused_computation | custom fusion | bytes 33554464 | tf_op jit(solution)/shard_map/jit(_take)/gather | solution.py:97
  253.0 12.5 %select_multiply_fusion = f32[8,64,64,128]{3,2,1,0:T(8,128)} fusion(f32[8,64,64,128]{3,2,1,0:T(8,128)} %gather_fusion, f32[8]{0:T(128)S(1)} %reshape.787, pred[8]{0:T(512)(128)(4,1)S(1)} %compare_and_fusion), kind=kLoop, calls=%fused_computation.7 | loop fusion | flops 8388608 | bytes 33554472 | tf_op jit(solution)/shard_map/mul | solution.py:98
  265.6 7.1 %all-to-all-start = ((f32[8,64,64,128]{3,2,1,0:T(8,128)}), f32[8,64,64,128]{3,2,1,0:T(8,128)}, u32[]{:S(2)}, u32[]{:S(2)}) async-start(f32[8,64,64,128]{3,2,1,0:T(8,128)} %select_multiply_fusion), calls=%async_computation | async-start | bytes 33554432 | tf_op jit(solution)/shard_map/all_to_all | solution.py:187
  272.8 1.5 collective-permute-start.5
  279.1 1.5 collective-permute-done.8
  282.2 2.0 collective-permute-done.1
  285.7 2.0 collective-permute-done.2
  290.1 177.8 %collective-permute-done.10 = bf16[2048]{0:T(1024)(128)(2,1)S(1)} collective-permute-done((bf16[2048]{0:T(1024)(128)(2,1)S(1)}, bf16[2048]{0:T(1024)(128)(2,1)S(1)}, u32[]{:S(2)}, u32[]{:S(2)}) %collective-permute-start.10) | collective-permute-done | bytes 4128 | tf_op jit(solution)/shard_map/ppermute | solution.py:16
  467.9 1.7 collective-permute-start.9
  469.7 2.1 collective-permute-done.9
  473.9 10.3 %gather_fusion.1 = f32[4,64,64,128]{3,2,1,0:T(8,128)} fusion(f32[8,64,64,128]{3,2,1,0:T(8,128)} %all-to-all-done, s32[1024]{0:T(1024)S(1)} %pad_clamp_fusion), kind=kCustom, calls=%fused_computation.1 | custom fusion | bytes 16777232 | tf_op jit(solution)/shard_map/jit(_take)/gather | solution.py:97
  484.2 13.5 %multiply_reduce_fusion.1 = (f32[4,64,64]{2,1,0:T(8,128)S(1)}, f32[4,64,64]{2,1,0:T(8,128)S(1)}) fusion(f32[4,64,64,128]{3,2,1,0:T(8,128)} %gather_fusion.1, f32[4,64,128]{2,1,0:T(8,128)S(1)} %bitcast.81, f32[4,64,128]{2,1,0:T(8,128)S(1)} %bitcast.77, f32[4,64,64]{2,1,0:T(8,128)S(1)} %get-tuple-element.55, f32[4]{0:T(128)S(1)} %convert_element_type.177, ...), kind=kLoop, calls=%fused_computation.17 | loop fusion | flops 25133056 | bytes 9177108 | tf_op jit(solution)/shard_map/reduce_sum | solution.py:52
  498.7 6.3 %all_gather.3 = bf16[2,16,4096]{2,0,1:T(2,128)(2,1)S(1)} all-gather(bf16[2,4,4096]{2,0,1:T(2,128)(2,1)S(1)} %pad_maximum_fusion.2), channel_id=1, replica_groups=mesh['groups'=2,'req'=4,'head'=4] {'req'}, dimensions={1}, use_global_device_ids=true | all-gather | bytes 327680 | tf_op jit(solution)/shard_map/all_gather | solution.py:225
  505.1 12.4 %fusion.1 = f32[2,16,2048]{2,1,0:T(8,128)S(1)} fusion(bf16[2048,2048]{1,0:T(8,128)(2,1)} %collective-permute-done.11, bf16[2048,2048]{1,0:T(8,128)(2,1)} %param.27, pred[]{:T(512)S(6)} %eq.105, bf16[2,16,4096]{2,0,1:T(2,128)(2,1)S(1)} %all_gather.3), kind=kOutput, calls=%fused_computation.8 | convolution fusion | flops 612368384 | bytes 17301504 | tf_op jit(solution)/shard_map/tsc,cd->tsd/dot_general | solution.py:223
  519.4 11.1 %fusion.8 = f32[1,1,4,64,64,128]{5,4,3,2,1,0:T(8,128)} fusion(f32[4,64,64,128]{3,2,1,0:T(8,128)} %gather_fusion.1, f32[4,64,128]{2,1,0:T(8,128)S(1)} %bitcast.80, f32[4,64,64]{2,1,0:T(8,128)S(1)} %get-tuple-element.54, f32[4,64,128]{2,1,0:T(8,128)S(1)} %bitcast.78, f32[4,64,64]{2,1,0:T(8,128)S(1)} %get-tuple-element.55, f32[4]{0:T(128)S(1)} %convert_element_type.177, ...), kind=kLoop, calls=%fused_computation.15 | loop fusion | flops 16777216 | bytes 17172500 | tf_op jit(solution)/shard_map/add | solution.py:48
  530.6 11.0 %reduce-scatter.2.cloned.1.call-done = f32[2,8,2048]{2,1,0:T(8,128)} async-done(((f32[2,32,2048]{2,1,0:T(8,128)}), f32[2,8,2048]{2,1,0:T(8,128)}) %reduce-scatter.2.cloned.1.call-update) | async-done | bytes 131088 | tf_op jit(solution)/shard_map/reduce_scatter | solution.py:235
  541.6 1.5 convert_element_type.194
  (132 shorter events, 20.6 us)
Async XLA Ops:
  13.1 15.6 %copy-start = (f32[8,3,2,1280]{3,2,1,0:T(2,128)S(1)}, f32[8,3,2,1280]{3,2,1,0:T(2,128)}, u32[]{:S(2)}) copy-start(f32[8,3,2,1280]{3,2,1,0:T(2,128)} %param.15) | copy-start | bytes 737284
  25.7 194.6 %collective-permute-start.3 = (f32[8,32,64,128]{3,2,1,0:T(8,128)}, f32[8,32,64,128]{3,2,1,0:T(8,128)}, u32[]{:S(2)}, u32[]{:S(2)}) collective-permute-start(f32[8,32,64,128]{3,2,1,0:T(8,128)} %get-tuple-element.20), channel_id=1, source_target_pairs={{0,1},{1,0},{2,3},{3,2},{4,5},{5,4},{6,7},{7,6},{8,9},{9,8},{10,11... | collective-permute-start | bytes 25165832 | tf_op jit(solution)/shard_map/ppermute | solution.py:16
  28.9 185.7 %collective-permute-start.4 = (f32[8,3,2,1280]{3,2,1,0:T(2,128)S(1)}, f32[8,3,2,1280]{3,2,1,0:T(2,128)S(1)}, u32[]{:S(2)}, u32[]{:S(2)}) collective-permute-start(f32[8,3,2,1280]{3,2,1,0:T(2,128)S(1)} %get-tuple-element.22), channel_id=1, source_target_pairs={{0,1},{1,0},{2,3},{3,2},{4,5},{5,4},{6,7},{7,6},{8,9},{9,8},{10,11... | collective-permute-start | bytes 737288 | tf_op jit(solution)/shard_map/ppermute | solution.py:16
  216.8 48.7 %all-to-all-start.1 = ((f32[8,3,4,1280]{3,2,1,0:T(4,128)}), f32[8,3,4,1280]{3,2,1,0:T(4,128)S(1)}, u32[]{:S(2)}, u32[]{:S(2)}) async-start(f32[8,3,4,1280]{3,2,1,0:T(4,128)} %select_multiply_fusion.1), calls=%async_computation.1 | async-start | bytes 983040 | tf_op jit(solution)/shard_map/all_to_all | solution.py:194
  265.5 9.5 %copy-start.4 = (bf16[2,1280]{1,0:T(2,128)(2,1)S(1)}, bf16[2,1280]{1,0:T(2,128)(2,1)}, u32[]{:S(2)}) copy-start(bf16[2,1280]{1,0:T(2,128)(2,1)} %param.22) | copy-start | bytes 15364
  265.5 10.9 %copy-start.6 = (bf16[2,8,32]{2,1,0:T(8,128)(2,1)S(1)}, bf16[2,8,32]{2,1,0:T(8,128)(2,1)}, u32[]{:S(2)}) copy-start(bf16[2,8,32]{2,1,0:T(8,128)(2,1)} %param.20) | copy-start | bytes 3076
  265.5 11.6 %copy-start.10 = (bf16[32]{0:T(256)(128)(2,1)S(1)}, bf16[32]{0:T(256)(128)(2,1)}, u32[]{:S(2)}) copy-start(bf16[32]{0:T(256)(128)(2,1)} %param.25) | copy-start | bytes 196
  265.5 13.1 %copy-start.2 = (bf16[2,8,2048]{2,1,0:T(8,128)(2,1)S(1)}, bf16[2,8,2048]{2,1,0:T(8,128)(2,1)}, u32[]{:S(2)}) copy-start(bf16[2,8,2048]{2,1,0:T(8,128)(2,1)} %param.19) | copy-start | bytes 196612
  265.5 13.2 %copy-start.7 = (s32[32]{0:T(128)S(1)}, s32[32]{0:T(128)}, u32[]{:S(2)}) copy-start(s32[32]{0:T(128)} %param.17) | copy-start | bytes 388
  265.5 15.1 %copy-start.8 = (bf16[32]{0:T(256)(128)(2,1)S(1)}, bf16[32]{0:T(256)(128)(2,1)}, u32[]{:S(2)}) copy-start(bf16[32]{0:T(256)(128)(2,1)} %param.24) | copy-start | bytes 196
  265.5 18.6 %copy-start.9 = (bf16[32]{0:T(256)(128)(2,1)S(1)}, bf16[32]{0:T(256)(128)(2,1)}, u32[]{:S(2)}) copy-start(bf16[32]{0:T(256)(128)(2,1)} %param.23) | copy-start | bytes 196
  265.5 23.8 %copy-start.5 = (bf16[2048]{0:T(1024)(128)(2,1)S(1)}, bf16[2048]{0:T(1024)(128)(2,1)}, u32[]{:S(2)}) copy-start(bf16[2048]{0:T(1024)(128)(2,1)} %param.26) | copy-start | bytes 12292
  265.6 208.3 %all-to-all-start = ((f32[8,64,64,128]{3,2,1,0:T(8,128)}), f32[8,64,64,128]{3,2,1,0:T(8,128)}, u32[]{:S(2)}, u32[]{:S(2)}) async-start(f32[8,64,64,128]{3,2,1,0:T(8,128)} %select_multiply_fusion), calls=%async_computation | async-start | bytes 33554432 | tf_op jit(solution)/shard_map/all_to_all | solution.py:187
  272.7 268.9 %reduce-scatter.2.cloned.1.call-start = ((), (), s32[]{:S(2)}) async-start(), calls=%async_computation.3 | async-start | bytes 655360 | tf_op jit(solution)/shard_map/reduce_scatter | solution.py:235
  272.8 199.2 %collective-permute-start.5 = (bf16[2,4,2,1280]{3,2,1,0:T(2,128)(2,1)S(1)}, bf16[2,4,2,1280]{3,2,1,0:T(2,128)(2,1)S(1)}, u32[]{:S(2)}, u32[]{:S(2)}) collective-permute-start(bf16[2,4,2,1280]{3,2,1,0:T(2,128)(2,1)S(1)} %get-tuple-element.30), channel_id=1, source_target_pairs={{0,1},{1,0},{2,3},{3,2},{4,5},{5,4},{6,7},{7,6},{8,9},{9,8},{10,11... | collective-permute-start | bytes 122888 | tf_op jit(solution)/shard_map/ppermute | solution.py:16
  274.4 195.2 %collective-permute-start.6 = (bf16[4,2,1280]{2,1,0:T(2,128)(2,1)S(1)}, bf16[4,2,1280]{2,1,0:T(2,128)(2,1)S(1)}, u32[]{:S(2)}, u32[]{:S(2)}) collective-permute-start(bf16[4,2,1280]{2,1,0:T(2,128)(2,1)S(1)} %copy-done.3), channel_id=1, source_target_pairs={{0,1},{1,0},{2,3},{3,2},{4,5},{5,4},{6,7},{7,6},{8,9},{9,8},{10,11... | collective-permute-start | bytes 61448 | tf_op jit(solution)/shard_map/ppermute | solution.py:16
  275.0 194.6 %collective-permute-start.7 = (bf16[2,1280]{1,0:T(2,128)(2,1)S(1)}, bf16[2,1280]{1,0:T(2,128)(2,1)S(1)}, u32[]{:S(2)}, u32[]{:S(2)}) collective-permute-start(bf16[2,1280]{1,0:T(2,128)(2,1)S(1)} %copy-done.4), channel_id=1, source_target_pairs={{0,1},{1,0},{2,3},{3,2},{4,5},{5,4},{6,7},{7,6},{8,9},{9,8},{10,11... | collective-permute-start | bytes 15368 | tf_op jit(solution)/shard_map/ppermute | solution.py:16
  276.4 13.0 %collective-permute-start = (bf16[2,4,32]{2,1,0:T(4,128)(2,1)S(1)}, bf16[2,4,32]{2,1,0:T(4,128)(2,1)S(1)}, u32[]{:S(2)}, u32[]{:S(2)}) collective-permute-start(bf16[2,4,32]{2,1,0:T(4,128)(2,1)S(1)} %get-tuple-element.42), channel_id=1, source_target_pairs={{0,1},{1,0},{2,3},{3,2},{4,5},{5,4},{6,7},{7,6},{8,9},{9,8},{10,11... | collective-permute-start | bytes 1544 | tf_op jit(solution)/shard_map/ppermute | solution.py:16
  277.1 3.5 collective-permute-start.8
  280.6 3.5 collective-permute-start.1
  284.1 3.5 collective-permute-start.2
  287.7 217.4 %collective-permute-start.11 = (bf16[2048,2048]{1,0:T(8,128)(2,1)}, bf16[2048,2048]{1,0:T(8,128)(2,1)}, u32[]{:S(2)}, u32[]{:S(2)}) collective-permute-start(bf16[2048,2048]{1,0:T(8,128)(2,1)} %param.27), channel_id=1, source_target_pairs={{0,1},{1,0},{2,3},{3,2},{4,5},{5,4},{6,7},{7,6},{8,9},{9,8},{10,11... | collective-permute-start | bytes 25165832 | tf_op jit(solution)/shard_map/ppermute | solution.py:16
  289.4 178.5 %collective-permute-start.10 = (bf16[2048]{0:T(1024)(128)(2,1)S(1)}, bf16[2048]{0:T(1024)(128)(2,1)S(1)}, u32[]{:S(2)}, u32[]{:S(2)}) collective-permute-start(bf16[2048]{0:T(1024)(128)(2,1)S(1)} %copy-done.5), channel_id=1, source_target_pairs={{0,1},{1,0},{2,3},{3,2},{4,5},{5,4},{6,7},{7,6},{8,9},{9,8},{10,11... | collective-permute-start | bytes 12296 | tf_op jit(solution)/shard_map/ppermute | solution.py:16
  467.9 3.9 collective-permute-start.9
  (2 other events, 16.2 us)
Sparse Core Ops, SparseCore 0:
  518.8 22.7 reduce-scatter.1
where the time goes:
time: 551 us; the launch traced here: 550 us
  waiting for transfers between devices  381 us (69%)
  other arithmetic  79.5 us (14%)
  local copies, waits for them, and re-layouts  30.6 us (6%)
  starting transfers between devices  26 us (5%)
  between operations  14.6 us (3%)
  matrix products  12.4 us (2%)
  blocking collectives  6.34 us (1%)
    ppermute x12, waiting for transfers between devices, from_partner(): return lax.ppermute(value, axis, pairs)  370 us
    gather x4, local copies, waits for them, and re-layouts, pack_rows(): taken = jnp.take(values, row_index, axis=0)  25.3 us
    select_n x5, other arithmetic, pair_join(): return jnp.where(parity == 0, first, second)  19.8 us
    ppermute x12, starting transfers between devices, from_partner(): return lax.ppermute(value, axis, pairs)  15.4 us
    mul x3, other arithmetic, pack_rows(): return taken * valid_row.reshape((-1,) + (1,) * (values.ndim - 1))  13.6 us
    reduce_sum x1, other arithmetic, advance(): jnp.sum(ssm_now * c_heads[:, :, None, :], axis=-1)  13.5 us
    mul x1, other arithmetic, on_device(): joined_ssm = pair_join(ssm_state * kept_weight, partner_ssm, parity, 1)  12.5 us
    dot_general x1, matrix products, on_device(): jnp.einsum('tsc,cd->tsd', lax.all_gather(normed_all, 'req', axis=1, tiled...  12.4 us
  transfers between devices with their start and end apart: 15, of which 7 were waited for; matrix products, arithmetic and copies ran while one was open for 16% of the time, Pallas kernels for 0%

commit v1 on v0

v1 whole, which is shorter than its diff:
```python
import functools

import jax
import jax.numpy as jnp
from jax import lax
from jax.experimental import pallas as pl
from jax.experimental.pallas import tpu as pltpu
from jax.sharding import PartitionSpec as P

H = 128
P_SIZE = 64
N = 128
G = 8
R_PF = 8
PER_GROUP = H // G
X_WIDTH = PER_GROUP * P_SIZE
CHUNKS = 8
AHEAD = 3
VMEM_LIMIT = 48 * 1024 * 1024

ANY = pl.BlockSpec(memory_space=pl.ANY)


def split_bf16(value):
    high = value.astype(jnp.bfloat16)
    low = (value - high.astype(jnp.float32)).astype(jnp.bfloat16)
    return high, low


def pack_kernel(count, cap, _rows, *refs):
    inputs, outputs = refs[:count], refs[-(count // cap) :]
    for place in range(count):
        outputs[place // cap][place % cap] = inputs[place][0].astype(jnp.bfloat16)


def pack_chunk(ssm_state, row_of, chunk, width, cap, after):
    count = row_of.shape[0]
    block = (1, width, P_SIZE, N)
    specs = [
        pl.BlockSpec(block, functools.partial(lambda i, rows, p: (rows[p], chunk, 0, 0), p=p))
        for p in range(count)
    ]
    shape = (cap, width, P_SIZE, N)
    return pl.pallas_call(
        functools.partial(pack_kernel, count, cap),
        grid_spec=pltpu.PrefetchScalarGridSpec(
            num_scalar_prefetch=1,
            grid=(1,),
            in_specs=specs + [ANY] * len(after),
            out_specs=[pl.BlockSpec(shape, lambda i, rows: (0, 0, 0, 0))] * (count // cap),
        ),
        out_shape=[jax.ShapeDtypeStruct(shape, jnp.bfloat16)] * (count // cap),
        compiler_params=pltpu.CompilerParams(vmem_limit_bytes=VMEM_LIMIT),
        cost_estimate=pl.CostEstimate(
            flops=0, bytes_accessed=6 * count * width * P_SIZE * N, transcendentals=0
        ),
        name="pack",
    )(row_of, *([ssm_state] * count), *after)


def route_kernel(sources, cap, places, *refs):
    arrived, keep, give, sems = refs[:sources], refs[-3], refs[-2], refs[-1]
    half = keep.shape[0]

    def copy(index, source):
        target = keep if index < half else give
        rank = places[index] % cap
        return pltpu.make_async_copy(
            arrived[source].at[rank], target.at[index % half], sems.at[index]
        )

    for index in range(2 * half):
        for source in range(sources):

            @pl.when(places[index] // cap == source)
            def _():
                copy(index, source).start()

    for index in range(2 * half):
        copy(index, 0).wait()


def route_chunk(arrived, places, half, after):
    cap = arrived[0].shape[0]
    shape = (half,) + arrived[0].shape[1:]
    out = jax.ShapeDtypeStruct(shape, jnp.bfloat16)
    return pl.pallas_call(
        functools.partial(route_kernel, len(arrived), cap),
        grid_spec=pltpu.PrefetchScalarGridSpec(
            num_scalar_prefetch=1,
            grid=(1,),
            in_specs=[ANY] * (len(arrived) + len(after)),
            out_specs=[ANY, ANY],
            scratch_shapes=[pltpu.SemaphoreType.DMA((2 * half,))],
        ),
        out_shape=[out, out],
        cost_estimate=pl.CostEstimate(
            flops=0, bytes_accessed=8 * half * arrived[0][0].size, transcendentals=0
        ),
        name="route",
    )(places, *arrived, *after)


def readout_kernel(state, taps, out):
    rows = state[0].reshape(X_WIDTH, N)
    state_high, state_low = split_bf16(rows)
    both = jnp.concatenate(split_bf16(taps[0, 0]), axis=0)
    dims = (((1,), (1,)), ((), ()))
    total = lax.dot_general(both, state_high, dims, preferred_element_type=jnp.float32)
    total = total + lax.dot_general(both, state_low, dims, preferred_element_type=jnp.float32)
    out[0, 0] = total[:8] + total[8:]


def readout(ssm_state, taps):
    rows, groups = taps.shape[:2]
    return pl.pallas_call(
        readout_kernel,
        grid=(rows, groups),
        in_specs=[
            pl.BlockSpec((1, PER_GROUP, P_SIZE, N), lambda i, g: (i, g, 0, 0)),
            pl.BlockSpec((1, 1, 8, N), lambda i, g: (i, g, 0, 0)),
        ],
        out_specs=pl.BlockSpec((1, 1, 8, X_WIDTH), lambda i, g: (i, g, 0, 0)),
        out_shape=jax.ShapeDtypeStruct((rows, groups, 8, X_WIDTH), jnp.float32),
        compiler_params=pltpu.CompilerParams(vmem_limit_bytes=VMEM_LIMIT),
        cost_estimate=pl.CostEstimate(
            flops=64 * ssm_state.size, bytes_accessed=4 * ssm_state.size, transcendentals=0
        ),
        name="readout",
    )(ssm_state, taps)


def finish_kernel(width, heads, base, _half, decay, keep, got, update, taps, *refs):
    out = refs[-1]
    owner, slot = pl.program_id(0), pl.program_id(1)
    update_high, update_low = split_bf16(update[0, 0, 0])
    taps_high, taps_low = split_bf16(taps[0, 0, 0])
    added = lax.dot_general(
        jnp.concatenate([update_high, update_low, update_high, update_low], axis=0),
        jnp.concatenate([taps_high, taps_high, taps_low, taps_low], axis=0),
        (((0,), (0,)), ((), ())),
        preferred_element_type=jnp.float32,
    ).reshape(width, P_SIZE, N)
    first = (owner * pl.num_programs(1) + slot) * heads + base

    def fill(source):
        for head in range(width):
            out[0, 0, 0, head] = (
                decay[first + head] * source[0, head].astype(jnp.float32) + added[head]
            )

    pl.when(owner == 0)(lambda: fill(keep))
    pl.when(owner == 1)(lambda: fill(got))


def finish_chunk(so_far, keep, got, half_index, decay, update, taps, chunk, heads):
    slots, width = keep.shape[:2]
    per_half = heads // width
    per_group = X_WIDTH // (width * P_SIZE)
    group, part = chunk // per_group, chunk % per_group
    out_shape = jax.ShapeDtypeStruct((1, 1, slots, 2 * heads, P_SIZE, N), jnp.float32)
    block = (1, width, P_SIZE, N)
    extra = [] if so_far is None else [so_far]
    return pl.pallas_call(
        functools.partial(finish_kernel, width, heads, chunk * width),
        grid_spec=pltpu.PrefetchScalarGridSpec(
            num_scalar_prefetch=2,
            grid=(2, slots),
            in_specs=[
                pl.BlockSpec(block, lambda o, j, h, d: (jnp.where(o == 0, j, slots - 1), 0, 0, 0)),
                pl.BlockSpec(block, lambda o, j, h, d: (jnp.where(o == 0, 0, j), 0, 0, 0)),
                pl.BlockSpec((1, 1, 1, 8, width * P_SIZE), lambda o, j, h, d: (o, j, group, 0, part)),
                pl.BlockSpec((1, 1, 1, 8, N), lambda o, j, h, d: (o, j, group, 0, 0)),
            ]
            + [ANY] * len(extra),
            out_specs=pl.BlockSpec(
                (1, 1, 1, width, P_SIZE, N),
                lambda o, j, h, d: (0, 0, j, h[o] * per_half + chunk, 0, 0),
            ),
        ),
        out_shape=out_shape,
        input_output_aliases={6: 0} if extra else {},
        compiler_params=pltpu.CompilerParams(vmem_limit_bytes=VMEM_LIMIT),
        cost_estimate=pl.CostEstimate(
            flops=64 * slots * width * P_SIZE * N,
            bytes_accessed=12 * slots * width * P_SIZE * N,
            transcendentals=0,
        ),
        name="finish",
    )(half_index, decay, keep, got, update, taps, *extra)


def take_rows(values, index, axis=0):
    return jnp.take(values, index, axis=axis, mode="clip")


def on_device(
    ssm_state,
    conv_state,
    counts,
    request_slot,
    token_xbc,
    token_z,
    token_dt,
    conv_weight,
    conv_bias,
    a_log,
    dt_bias,
    d_skip,
    norm_gain,
    out_weight,
):
    f32 = jnp.float32
    req_count = lax.axis_size("req")
    head_count = lax.axis_size("head")
    my_req = lax.axis_index("req")
    parity = lax.axis_index("head") % 2
    cap = (R_PF + req_count - 1) // req_count
    slot_dev = R_PF // 2
    steps = token_xbc.shape[0]
    heads = ssm_state.shape[1]
    groups = conv_state.shape[2]
    width = heads // CHUNKS
    channels = groups * X_WIDTH
    conv_width = conv_state.shape[3]

    order = jnp.arange(R_PF, dtype=jnp.int32)
    my_slots = lax.dynamic_slice_in_dim(request_slot, my_req * R_PF, R_PF)
    my_dest = my_slots // R_PF
    my_rank = jnp.sum(
        ((my_dest[:, None] == my_dest[None, :]) & (order[None, :] < order[:, None])).astype(jnp.int32),
        axis=1,
    )
    place = jnp.arange(req_count * cap, dtype=jnp.int32)
    row_of = jnp.sum(
        jnp.where(
            ((my_dest ^ my_req) * cap + my_rank)[None, :] == place[:, None], order[None, :], 0
        ),
        axis=1,
    )
    my_live = order < lax.dynamic_index_in_dim(counts, my_req, 0, keepdims=False)

    all_dest = (request_slot // R_PF).reshape(req_count, R_PF)
    all_rank = jnp.sum(
        (
            (all_dest[:, :, None] == all_dest[:, None, :]) & (order[None, None, :] < order[None, :, None])
        ).astype(jnp.int32),
        axis=2,
    )
    row_ids = jnp.arange(req_count * R_PF, dtype=jnp.int32)
    local_slots = my_req * R_PF + order
    names = request_slot[None, :] == local_slots[:, None]
    rank_row = all_rank.reshape(-1)
    slot_place = jnp.sum(
        jnp.where(names, ((row_ids // R_PF) * cap + rank_row)[None, :], 0), axis=1
    )
    slot_shift = jnp.sum(
        jnp.where(names, ((row_ids // R_PF ^ my_req) * cap + rank_row)[None, :], 0), axis=1
    )
    mine = parity * slot_dev + jnp.arange(slot_dev, dtype=jnp.int32)
    theirs = (1 - parity) * slot_dev + jnp.arange(slot_dev, dtype=jnp.int32)
    split = jnp.concatenate([mine, theirs])
    places = slot_shift[split]

    def swap(value):
        return lax.ppermute(value, "head", [(i, i ^ 1) for i in range(head_count)])

    def exchange(value):
        return lax.all_to_all(value, "req", split_axis=0, concat_axis=0, tiled=True)

    keeps, gots = [], []
    for chunk in range(CHUNKS):
        after = [gots[chunk - AHEAD]] if chunk >= AHEAD else []
        packed = pack_chunk(ssm_state, row_of, chunk, width, cap, after)
        arrived = [packed[0]]
        for shift in range(1, req_count):
            pairs = [(i, i ^ shift) for i in range(req_count)]
            arrived.append(lax.ppermute(packed[shift], "req", pairs))
        keep, give = route_chunk(arrived, places, slot_dev, gots[chunk - 1 : chunk])
        keeps.append(keep)
        gots.append(swap(give))

    tokens = jnp.concatenate(
        [
            token_xbc.reshape(steps, R_PF, -1),
            token_z.reshape(steps, R_PF, -1),
            token_dt.reshape(steps, R_PF, -1),
        ],
        axis=2,
    )
    slot_at = jnp.sum(
        jnp.where(slot_place[None, :] == place[:, None], order[None, :], 0), axis=1
    )
    tokens = exchange(jnp.swapaxes(take_rows(tokens, slot_at, 1), 0, 1))
    my_place = my_dest * cap + my_rank
    tokens = take_rows(tokens, my_place)
    xbc_size = groups * conv_width
    row_xbc = tokens[:, :, :xbc_size].reshape(R_PF, steps, groups, conv_width).astype(f32)
    row_z = tokens[:, :, xbc_size : xbc_size + channels].astype(f32)
    row_dt = tokens[:, :, xbc_size + channels :].astype(f32)

    conv_now = jnp.where(my_live[:, None, None, None], conv_state, 0.0)
    window = jnp.concatenate([conv_now, row_xbc], axis=1)
    taps = conv_weight.shape[0]
    weight = conv_weight.astype(f32)
    act = jnp.stack(
        [
            jax.nn.silu(
                sum(window[:, t + k] * weight[k][None] for k in range(taps))
                + conv_bias.astype(f32)[None]
            )
            for t in range(steps)
        ],
        axis=1,
    )
    x = act[..., :X_WIDTH]
    b = act[..., X_WIDTH : X_WIDTH + N]
    c = act[..., X_WIDTH + N :]
    dt = jax.nn.softplus(row_dt + dt_bias.astype(f32))
    decay = jnp.exp(-dt * jnp.exp(a_log.astype(f32)))

    def spread(value):
        shape = value.shape[:-1] + (groups, PER_GROUP, P_SIZE)
        value = value.reshape(value.shape[:-1] + (groups, PER_GROUP, 1))
        return jnp.broadcast_to(value, shape).reshape(shape[:-2] + (X_WIDTH,))

    u = spread(dt) * x
    wide_decay = spread(decay)
    pad = jnp.zeros((R_PF, groups, 8 - steps, N), f32)
    read = readout(ssm_state, jnp.concatenate([jnp.swapaxes(c, 1, 2), pad], axis=2))
    read = jnp.where(my_live[:, None, None, None], read, 0.0)
    skip = spread(d_skip.astype(f32))

    def pair_sum(first, second):
        return jnp.sum(first * second, axis=-1, keepdims=True)

    y0 = wide_decay[:, 0] * read[:, :, 0] + pair_sum(b[:, 0], c[:, 0]) * u[:, 0] + skip * x[:, 0]
    y1 = (
        wide_decay[:, 1]
        * (wide_decay[:, 0] * read[:, :, 1] + pair_sum(b[:, 0], c[:, 1]) * u[:, 0])
        + pair_sum(b[:, 1], c[:, 1]) * u[:, 1]
        + skip * x[:, 1]
    )
    gated = jnp.stack([y0, y1]) * jax.nn.silu(
        jnp.swapaxes(row_z, 0, 1).reshape(steps, R_PF, groups, X_WIDTH)
    )
    normed = gated * lax.rsqrt(jnp.mean(gated * gated, axis=-1, keepdims=True) + 1e-05)
    normed = (normed.reshape(steps, R_PF, channels) * norm_gain.astype(f32)).astype(jnp.bfloat16)

    slot_row = jnp.sum(
        jnp.where(request_slot[None, :] == row_ids[:, None], row_ids[None, :], 0), axis=1
    )
    normed_all = take_rows(lax.all_gather(normed, "req", axis=1, tiled=True), slot_row, 1)
    projected = jnp.einsum("tsc,cd->tsd", normed_all, out_weight, preferred_element_type=f32)
    layer_out = lax.psum_scatter(projected, "head", scatter_dimension=1, tiled=True).astype(
        jnp.bfloat16
    )

    packet = jnp.concatenate(
        [
            (wide_decay[:, 1] * u[:, 0]).reshape(R_PF, -1),
            u[:, 1].reshape(R_PF, -1),
            b[:, 0].reshape(R_PF, -1),
            b[:, 1].reshape(R_PF, -1),
            window[:, 2].reshape(R_PF, -1),
            jnp.where(my_live[:, None], decay[:, 0] * decay[:, 1], 0.0),
        ],
        axis=1,
    )
    row_at = jnp.sum(jnp.where(my_place[None, :] == place[:, None], order[None, :], 0), axis=1)
    packet = exchange(take_rows(packet, row_at))
    local_tokens = jnp.swapaxes(token_xbc, 0, 1).reshape(R_PF, -1).astype(f32)
    by_slot = jnp.concatenate([take_rows(packet, slot_place), local_tokens], axis=1)
    by_slot = take_rows(by_slot, split)
    own, other = by_slot[:slot_dev], swap(by_slot[slot_dev:])
    both = jnp.stack([own, other])

    def cut(start, size):
        return both[:, :, start : start + size]

    at = 0
    u0, at = cut(at, channels), at + channels
    u1, at = cut(at, channels), at + channels
    b0, at = cut(at, groups * N), at + groups * N
    b1, at = cut(at, groups * N), at + groups * N
    last, at = cut(at, xbc_size), at + xbc_size
    total_decay, at = cut(at, heads), at + heads
    fresh = cut(at, steps * xbc_size)

    def pile(first, second, size):
        shape = (2, slot_dev, groups, 1, size)
        zero = jnp.zeros((2, slot_dev, groups, 8 - steps, size), f32)
        return jnp.concatenate([first.reshape(shape), second.reshape(shape), zero], axis=3)

    update = pile(u0, u1, X_WIDTH)
    update_taps = pile(b0, b1, N)
    half_index = jnp.stack([parity, 1 - parity])
    flat_decay = total_decay.reshape(-1)
    out_ssm = None
    for chunk in range(CHUNKS):
        out_ssm = finish_chunk(
            out_ssm, keeps[chunk], gots[chunk], half_index, flat_decay, update, update_taps, chunk, heads
        )

    conv_rows = jnp.concatenate([last, fresh], axis=2).reshape(
        2, slot_dev, 1 + steps, groups, conv_width
    )
    conv_rows = jnp.where(parity == 0, conv_rows, conv_rows[::-1])
    out_conv = jnp.moveaxis(conv_rows, 0, 2).reshape(
        1, 1, slot_dev, 1 + steps, 2 * groups, conv_width
    )
    return (layer_out, out_ssm, out_conv)


def solution(mesh):
    in_specs = (
        P(("groups", "req"), "head", None, None),
        P(("groups", "req"), None, "head", None),
        P("groups"),
        P("groups"),
        P(None, ("groups", "req"), "head", None),
        P(None, ("groups", "req"), "head"),
        P(None, ("groups", "req"), "head"),
        P(None, "head", None),
        P("head", None),
        P("head"),
        P("head"),
        P("head"),
        P("head"),
        P("head", "req"),
    )
    out_specs = (
        P(None, ("groups", "head"), "req"),
        P(("groups", "req"), "head", None, None, None, None),
        P(("groups", "req"), "head", None, None, None, None),
    )
    return jax.shard_map(
        on_device, mesh=mesh, in_specs=in_specs, out_specs=out_specs, check_vma=False
    )
```

time: 551 us -> 336 us (0.61)
  waiting for transfers between devices: 381 us -> 23.5 us
  Pallas kernels: 0 us -> 202 us
  other arithmetic: 79.5 us -> 12.5 us
  starting transfers between devices: 26 us -> 36.1 us
  matrix products: 12.4 us -> 5.75 us
    ppermute x12 -> x33, waiting for transfers between devices: 370 us -> 23.5 us  [the longest x24 12.7 us: on_device(): arrived.append(lax.ppermute(packed[shift], 'req', pairs))]
    pallas_call x0 -> x25, Pallas kernels: none -> 202 us  [the longest x8 142 us: route_chunk(): pl.pallas_call(functools.partial(route_kernel, len(arrived), cap), grid_s...]
    mul x9 -> x4, other arithmetic: 26.7 us -> 2 us  [the longest x1 0.99 us: on_device(): wide_decay[:, 1] * u[:, 0]]
    gather x7, local copies, waits for them, and re-layouts: 27.3 us -> 6.92 us  [the longest x6 5.75 us: take_rows(): return jnp.take(values, index, axis=axis, mode='clip')]
    select_n x9 -> x5, other arithmetic: 20.7 us -> 1.75 us  [the longest x1 0.73 us: on_device(): my_dest = my_slots // R_PF]
    unnamed x22 -> x136, local copies, waits for them, and re-layouts: 0.06 us -> 14.3 us
    ppermute x12 -> x33, starting transfers between devices: 15.4 us -> 28.5 us  [the longest x24 17.9 us: on_device(): arrived.append(lax.ppermute(packed[shift], 'req', pairs))]
    reduce_sum x6 -> x8, other arithmetic: 14.4 us -> 2.09 us  [the longest x1 0.87 us: on_device(): jnp.sum(jnp.where(names, ((row_ids // R_PF ^ my_req) * cap + rank_row)[No...]
  transfers between devices with their start and end apart: 15 -> 36, of which waited for: 7 -> 7; matrix products, arithmetic and copies ran while one was open for 16% -> 9% of each run, Pallas kernels for 0% -> 59%
where the time goes in v1:
time: 336 us; the launch traced here: 335 us
  Pallas kernels  202 us (60%)
  starting transfers between devices  36.1 us (11%)
  local copies, waits for them, and re-layouts  33.2 us (10%)
  waiting for transfers between devices  23.5 us (7%)
  between operations  15.2 us (5%)
  other arithmetic  12.5 us (4%)
  blocking collectives  5.97 us (2%)
  matrix products  5.75 us (2%)
    pallas_call x8, Pallas kernels, route_chunk(): pl.pallas_call(functools.partial(route_kernel, len(arrived), cap), grid_s...  142 us
    pallas_call x8, Pallas kernels, finish_chunk(): pl.pallas_call(functools.partial(finish_kernel, width, heads, chunk * wid...  34.6 us
    ppermute x24, starting transfers between devices, on_device(): arrived.append(lax.ppermute(packed[shift], 'req', pairs))  17.9 us
    pallas_call x8, Pallas kernels, pack_chunk(): pl.pallas_call(functools.partial(pack_kernel, count, cap), grid_spec=pltp...  15.1 us
    unnamed x136, local copies, waits for them, and re-layouts  14.3 us
    ppermute x24, waiting for transfers between devices, on_device(): arrived.append(lax.ppermute(packed[shift], 'req', pairs))  12.7 us
    pallas_call x1, Pallas kernels, readout(): pl.pallas_call(readout_kernel, grid=(rows, groups), in_specs=[pl.BlockSpe...  10.9 us
    ppermute x9, waiting for transfers between devices, swap(): return lax.ppermute(value, 'head', [(i, i ^ 1) for i in range(head_count)])  10.8 us
  transfers between devices with their start and end apart: 36, of which 7 were waited for; matrix products, arithmetic and copies ran while one was open for 9% of the time, Pallas kernels for 59%

profile of v1, /device:TPU:0, one launch (start us, length us, event | category | flops | bytes accessed | tf_op | source)
XLA Modules:
  0.0 334.6 jit_solution(6402852259375420104)
XLA Ops:
  13.5 4.2 %all-to-all-start = ((bf16[8,2,4640]{2,1,0:T(2,128)(2,1)}), bf16[8,2,4640]{2,1,0:T(2,128)(2,1)S(1)}, u32[]{:S(2)}, u32[]{:S(2)}) async-start(bf16[8,2,4640]{2,1,0:T(2,128)(2,1)} %gather_fusion), calls=%async_computation | async-start | bytes 303104 | tf_op jit(solution)/shard_map/all_to_all | solution.py:269
  43.9 3.4 %all-to-all-start.1 = ((f32[4,2,7200]{2,1,0:T(2,128)}), f32[4,2,7200]{2,1,0:T(2,128)S(1)}, u32[]{:S(2)}, u32[]{:S(2)}) async-start(f32[4,2,7200]{2,1,0:T(2,128)} %all_to_all.12), calls=%async_computation.2 | async-start | bytes 466944 | tf_op jit(solution)/shard_map/all_to_all | solution.py:269
  47.7 10.9 %readout.1 = f32[8,2,8,1024]{3,2,1,0:T(8,128)S(1)} custom-call(f32[8,32,64,128]{3,2,1,0:T(8,128)} %refs_7_.15, f32[8,2,8,128]{3,2,1,0:T(8,128)S(1)} %concatenate.51.taps), custom_call_target="tpu_custom_call" | custom-call | flops 134217728 | bytes 8388608 | tf_op jit(solution)/shard_map/readout/pallas_call | solution.py:116
  66.7 17.7 %route.8 = (bf16[4,4,64,128]{3,2,1,0:T(8,128)(2,1)}, bf16[4,4,64,128]{3,2,1,0:T(8,128)(2,1)}) custom-call(s32[8]{0:T(128)} %gather_fusion.6, bf16[2,4,64,128]{3,2,1,0:T(8,128)(2,1)} %copy-done.25, bf16[2,4,64,128]{3,2,1,0:T(8,128)(2,1)} %collective-permute-done.4.refs_1_, bf16[2,4,64,128]{3,2,1,0:T(8,128)(2,1)} %collective-permute-done.5.refs_2_, ...), custom_call_target="tpu_custom_call" | custom-call | bytes 1048576 | tf_op jit(solution)/shard_map/route/pallas_call | solution.py:87
  86.9 6.0 %all_gather.3 = bf16[2,32,2048]{2,0,1:T(2,128)(2,1)S(1)} all-gather(bf16[2,8,2048]{2,0,1:T(2,128)(2,1)S(1)} %copy.125), channel_id=1, replica_groups=mesh['groups'=2,'req'=4,'head'=4] {'req'}, dimensions={1}, use_global_device_ids=true | all-gather | bytes 327680 | tf_op jit(solution)/shard_map/all_gather | solution.py:353
  97.6 17.7 %route.9 = (bf16[4,4,64,128]{3,2,1,0:T(8,128)(2,1)}, bf16[4,4,64,128]{3,2,1,0:T(8,128)(2,1)}) custom-call(s32[8]{0:T(128)} %gather_fusion.6, bf16[2,4,64,128]{3,2,1,0:T(8,128)(2,1)} %copy-done.26, bf16[2,4,64,128]{3,2,1,0:T(8,128)(2,1)} %copy-done.35, bf16[2,4,64,128]{3,2,1,0:T(8,128)(2,1)} %copy-done.36, bf16[2,4,64,128]{3,2,1,0:T(8,128)(2,1)} %copy-done.39, ...), custom_call_target="tpu_custom_call" | custom-call | bytes 1048576 | tf_op jit(solution)/shard_map/route/pallas_call | solution.py:87
  125.0 17.7 %route.10 = (bf16[4,4,64,128]{3,2,1,0:T(8,128)(2,1)}, bf16[4,4,64,128]{3,2,1,0:T(8,128)(2,1)}) custom-call(s32[8]{0:T(128)} %gather_fusion.6, bf16[2,4,64,128]{3,2,1,0:T(8,128)(2,1)} %copy-done.27, bf16[2,4,64,128]{3,2,1,0:T(8,128)(2,1)} %copy-done.37, bf16[2,4,64,128]{3,2,1,0:T(8,128)(2,1)} %collective-permute-done.16.refs_2_, ...), custom_call_target="tpu_custom_call" | custom-call | bytes 1048576 | tf_op jit(solution)/shard_map/route/pallas_call | solution.py:87
  152.9 17.7 %route.11 = (bf16[4,4,64,128]{3,2,1,0:T(8,128)(2,1)}, bf16[4,4,64,128]{3,2,1,0:T(8,128)(2,1)}) custom-call(s32[8]{0:T(128)} %gather_fusion.6, bf16[2,4,64,128]{3,2,1,0:T(8,128)(2,1)} %copy-done.29, bf16[2,4,64,128]{3,2,1,0:T(8,128)(2,1)} %copy-done.38, bf16[2,4,64,128]{3,2,1,0:T(8,128)(2,1)} %copy-done.41, bf16[2,4,64,128]{3,2,1,0:T(8,128)(2,1)} %copy-done.43, ...), custom_call_target="tpu_custom_call" | custom-call | bytes 1048576 | tf_op jit(solution)/shard_map/route/pallas_call | solution.py:87
  171.0 5.8 %fusion = f32[2,32,2048]{2,1,0:T(8,128)} fusion(bf16[2048,2048]{1,0:T(8,128)(2,1)} %param.27, bf16[2,32,2048]{2,0,1:T(2,128)(2,1)S(1)} %bitcast.106), kind=kOutput, calls=%fused_computation.7 | convolution fusion | flops 536870912 | bytes 9175040 | tf_op jit(solution)/shard_map/tsc,cd->tsd/dot_general | solution.py:354
  181.9 17.7 %route.12 = (bf16[4,4,64,128]{3,2,1,0:T(8,128)(2,1)}, bf16[4,4,64,128]{3,2,1,0:T(8,128)(2,1)}) custom-call(s32[8]{0:T(128)} %gather_fusion.6, bf16[2,4,64,128]{3,2,1,0:T(8,128)(2,1)} %copy-done.28, bf16[2,4,64,128]{3,2,1,0:T(8,128)(2,1)} %copy-done.44, bf16[2,4,64,128]{3,2,1,0:T(8,128)(2,1)} %copy-done.40, bf16[2,4,64,128]{3,2,1,0:T(8,128)(2,1)} %copy-done.42, ...), custom_call_target="tpu_custom_call" | custom-call | bytes 1048576 | tf_op jit(solution)/shard_map/route/pallas_call | solution.py:87
  201.9 6.6 %collective-permute-done.20.refs_8_.refs_4_.got = bf16[4,4,64,128]{3,2,1,0:T(8,128)(2,1)S(1)} collective-permute-done((bf16[4,4,64,128]{3,2,1,0:T(8,128)(2,1)}, bf16[4,4,64,128]{3,2,1,0:T(8,128)(2,1)S(1)}, u32[]{:S(2)}, u32[]{:S(2)}) %collective-permute-start.20) | collective-permute-done | bytes 262176 | tf_op jit(solution)/shard_map/ppermute | solution.py:266
  209.2 17.7 %route.13 = (bf16[4,4,64,128]{3,2,1,0:T(8,128)(2,1)}, bf16[4,4,64,128]{3,2,1,0:T(8,128)(2,1)}) custom-call(s32[8]{0:T(128)} %gather_fusion.6, bf16[2,4,64,128]{3,2,1,0:T(8,128)(2,1)} %copy-done.30, bf16[2,4,64,128]{3,2,1,0:T(8,128)(2,1)} %copy-done.45, bf16[2,4,64,128]{3,2,1,0:T(8,128)(2,1)} %copy-done.46, bf16[2,4,64,128]{3,2,1,0:T(8,128)(2,1)} %copy-done.47, ...), custom_call_target="tpu_custom_call" | custom-call | bytes 1048576 | tf_op jit(solution)/shard_map/route/pallas_call | solution.py:87
  233.7 4.4 %collective-permute-done.25.refs_2_ = bf16[2,4,64,128]{3,2,1,0:T(8,128)(2,1)S(1)} collective-permute-done((bf16[2,4,64,128]{3,2,1,0:T(8,128)(2,1)S(1)}, bf16[2,4,64,128]{3,2,1,0:T(8,128)(2,1)S(1)}, u32[]{:S(2)}, u32[]{:S(2)}) %collective-permute-start.25) | collective-permute-done | bytes 131104 | tf_op jit(solution)/shard_map/ppermute | solution.py:278
  240.8 17.7 %route.14 = (bf16[4,4,64,128]{3,2,1,0:T(8,128)(2,1)}, bf16[4,4,64,128]{3,2,1,0:T(8,128)(2,1)}) custom-call(s32[8]{0:T(128)} %gather_fusion.6, bf16[2,4,64,128]{3,2,1,0:T(8,128)(2,1)} %copy-done.32, bf16[2,4,64,128]{3,2,1,0:T(8,128)(2,1)} %copy-done.49, bf16[2,4,64,128]{3,2,1,0:T(8,128)(2,1)} %copy-done.51, bf16[2,4,64,128]{3,2,1,0:T(8,128)(2,1)} %copy-done.53, ...), custom_call_target="tpu_custom_call" | custom-call | bytes 1048576 | tf_op jit(solution)/shard_map/route/pallas_call | solution.py:87
  263.5 4.4 %collective-permute-done.22.refs_2_ = bf16[2,4,64,128]{3,2,1,0:T(8,128)(2,1)S(1)} collective-permute-done((bf16[2,4,64,128]{3,2,1,0:T(8,128)(2,1)S(1)}, bf16[2,4,64,128]{3,2,1,0:T(8,128)(2,1)S(1)}, u32[]{:S(2)}, u32[]{:S(2)}) %collective-permute-start.22) | collective-permute-done | bytes 131104 | tf_op jit(solution)/shard_map/ppermute | solution.py:278
  270.6 17.7 %route.15 = (bf16[4,4,64,128]{3,2,1,0:T(8,128)(2,1)}, bf16[4,4,64,128]{3,2,1,0:T(8,128)(2,1)}) custom-call(s32[8]{0:T(128)} %gather_fusion.6, bf16[2,4,64,128]{3,2,1,0:T(8,128)(2,1)} %copy-done.31, bf16[2,4,64,128]{3,2,1,0:T(8,128)(2,1)} %copy-done.48, bf16[2,4,64,128]{3,2,1,0:T(8,128)(2,1)} %copy-done.50, bf16[2,4,64,128]{3,2,1,0:T(8,128)(2,1)} %copy-done.52, ...), custom_call_target="tpu_custom_call" | custom-call | bytes 1048576 | tf_op jit(solution)/shard_map/route/pallas_call | solution.py:87
  291.6 4.3 %finish.8.refs_0_ = f32[1,1,4,64,64,128]{5,4,3,2,1,0:T(8,128)} custom-call(s32[2]{0:T(128)S(1)} %pad_add_fusion._half, f32[256]{0:T(256)S(1)} %reshape.439.decay, bf16[4,4,64,128]{3,2,1,0:T(8,128)(2,1)S(1)} %copy-done.24, bf16[4,4,64,128]{3,2,1,0:T(8,128)(2,1)S(1)} %copy-done.12, f32[2,4,2,8,1024]{4,3,2,1,0:T(8,128)S(1)} %maximum_maximum_fusion.update, ...), custom_call_target="tpu_custom_call" | custom-call | flops 8388608 | bytes 1572864 | tf_op jit(solution)/shard_map/finish/pallas_call | solution.py:164
  295.9 4.3 %finish.9.refs_0_ = f32[1,1,4,64,64,128]{5,4,3,2,1,0:T(8,128)} custom-call(s32[2]{0:T(128)S(1)} %pad_add_fusion._half, f32[256]{0:T(256)S(1)} %reshape.439.decay, bf16[4,4,64,128]{3,2,1,0:T(8,128)(2,1)S(1)} %copy-done.17, bf16[4,4,64,128]{3,2,1,0:T(8,128)(2,1)S(1)} %copy-done.2, ...), custom_call_target="tpu_custom_call", output_to_operand_aliasing={{}: (6, {})} | custom-call | flops 8388608 | bytes 1572864 | tf_op jit(solution)/shard_map/finish/pallas_call | solution.py:164
  300.2 4.3 %finish.10.refs_0_ = f32[1,1,4,64,64,128]{5,4,3,2,1,0:T(8,128)} custom-call(s32[2]{0:T(128)S(1)} %pad_add_fusion._half, f32[256]{0:T(256)S(1)} %reshape.439.decay, bf16[4,4,64,128]{3,2,1,0:T(8,128)(2,1)S(1)} %copy-done.18, bf16[4,4,64,128]{3,2,1,0:T(8,128)(2,1)S(1)} %copy-done.4, ...), custom_call_target="tpu_custom_call", output_to_operand_aliasing={{}: (6, {})} | custom-call | flops 8388608 | bytes 1572864 | tf_op jit(solution)/shard_map/finish/pallas_call | solution.py:164
  306.1 4.3 %finish.11.refs_0_ = f32[1,1,4,64,64,128]{5,4,3,2,1,0:T(8,128)} custom-call(s32[2]{0:T(128)S(1)} %pad_add_fusion._half, f32[256]{0:T(256)S(1)} %reshape.439.decay, bf16[4,4,64,128]{3,2,1,0:T(8,128)(2,1)S(1)} %copy-done.19, bf16[4,4,64,128]{3,2,1,0:T(8,128)(2,1)S(1)} %copy-done.7, ...), custom_call_target="tpu_custom_call", output_to_operand_aliasing={{}: (6, {})} | custom-call | flops 8388608 | bytes 1572864 | tf_op jit(solution)/shard_map/finish/pallas_call | solution.py:164
  310.4 4.3 %finish.12.refs_0_ = f32[1,1,4,64,64,128]{5,4,3,2,1,0:T(8,128)} custom-call(s32[2]{0:T(128)S(1)} %pad_add_fusion._half, f32[256]{0:T(256)S(1)} %reshape.439.decay, bf16[4,4,64,128]{3,2,1,0:T(8,128)(2,1)S(1)} %copy-done.20, bf16[4,4,64,128]{3,2,1,0:T(8,128)(2,1)S(1)} %copy-done.9, ...), custom_call_target="tpu_custom_call", output_to_operand_aliasing={{}: (6, {})} | custom-call | flops 8388608 | bytes 1572864 | tf_op jit(solution)/shard_map/finish/pallas_call | solution.py:164
  314.7 4.3 %finish.13.refs_0_ = f32[1,1,4,64,64,128]{5,4,3,2,1,0:T(8,128)} custom-call(s32[2]{0:T(128)S(1)} %pad_add_fusion._half, f32[256]{0:T(256)S(1)} %reshape.439.decay, bf16[4,4,64,128]{3,2,1,0:T(8,128)(2,1)S(1)} %copy-done.21, bf16[4,4,64,128]{3,2,1,0:T(8,128)(2,1)S(1)} %copy-done.14, ...), custom_call_target="tpu_custom_call", output_to_operand_aliasing={{}: (6, {})} | custom-call | flops 8388608 | bytes 1572864 | tf_op jit(solution)/shard_map/finish/pallas_call | solution.py:164
  319.1 4.3 %finish.14.refs_0_ = f32[1,1,4,64,64,128]{5,4,3,2,1,0:T(8,128)} custom-call(s32[2]{0:T(128)S(1)} %pad_add_fusion._half, f32[256]{0:T(256)S(1)} %reshape.439.decay, bf16[4,4,64,128]{3,2,1,0:T(8,128)(2,1)S(1)} %copy-done.22, bf16[4,4,64,128]{3,2,1,0:T(8,128)(2,1)S(1)} %copy-done.16, ...), custom_call_target="tpu_custom_call", output_to_operand_aliasing={{}: (6, {})} | custom-call | flops 8388608 | bytes 1572864 | tf_op jit(solution)/shard_map/finish/pallas_call | solution.py:164
  323.4 4.3 %finish.15 = f32[1,1,4,64,64,128]{5,4,3,2,1,0:T(8,128)} custom-call(s32[2]{0:T(128)S(1)} %pad_add_fusion._half, f32[256]{0:T(256)S(1)} %reshape.439.decay, bf16[4,4,64,128]{3,2,1,0:T(8,128)(2,1)S(1)} %copy-done.23, bf16[4,4,64,128]{3,2,1,0:T(8,128)(2,1)S(1)} %collective-permute-done.32.got, ...), custom_call_target="tpu_custom_call", output_to_operand_aliasing={{}: (6, {})} | custom-call | flops 8388608 | bytes 1572864 | tf_op jit(solution)/shard_map/finish/pallas_call | solution.py:164
  (335 shorter events, 97.3 us)
Async XLA Ops:
  13.5 24.1 %all-to-all-start = ((bf16[8,2,4640]{2,1,0:T(2,128)(2,1)}), bf16[8,2,4640]{2,1,0:T(2,128)(2,1)S(1)}, u32[]{:S(2)}, u32[]{:S(2)}) async-start(bf16[8,2,4640]{2,1,0:T(2,128)(2,1)} %gather_fusion), calls=%async_computation | async-start | bytes 303104 | tf_op jit(solution)/shard_map/all_to_all | solution.py:269
  22.1 42.5 %collective-permute-start.4 = (bf16[2,4,64,128]{3,2,1,0:T(8,128)(2,1)S(1)}, bf16[2,4,64,128]{3,2,1,0:T(8,128)(2,1)}, u32[]{:S(2)}, u32[]{:S(2)}) collective-permute-start(bf16[2,4,64,128]{3,2,1,0:T(8,128)(2,1)S(1)} %get-tuple-element.56), channel_id=1, source_target_pairs={{0,4},{4,0},{8,12},{12,8},{1,5},{5,1},{9,13},{13,9},{2,6},{6,2},{1... | collective-permute-start | bytes 393224 | tf_op jit(solution)/shard_map/ppermute | solution.py:278
  22.6 43.8 %collective-permute-start.5 = (bf16[2,4,64,128]{3,2,1,0:T(8,128)(2,1)S(1)}, bf16[2,4,64,128]{3,2,1,0:T(8,128)(2,1)}, u32[]{:S(2)}, u32[]{:S(2)}) collective-permute-start(bf16[2,4,64,128]{3,2,1,0:T(8,128)(2,1)S(1)} %get-tuple-element.57), channel_id=1, source_target_pairs={{0,8},{4,12},{8,0},{12,4},{1,9},{5,13},{9,1},{13,5},{2,10},{6,14},... | collective-permute-start | bytes 393224 | tf_op jit(solution)/shard_map/ppermute | solution.py:278
  24.2 42.5 %collective-permute-start.6 = (bf16[2,4,64,128]{3,2,1,0:T(8,128)(2,1)S(1)}, bf16[2,4,64,128]{3,2,1,0:T(8,128)(2,1)}, u32[]{:S(2)}, u32[]{:S(2)}) collective-permute-start(bf16[2,4,64,128]{3,2,1,0:T(8,128)(2,1)S(1)} %get-tuple-element.58), channel_id=1, source_target_pairs={{0,12},{4,8},{8,4},{12,0},{1,13},{5,9},{9,5},{13,1},{2,14},{6,10},... | collective-permute-start | bytes 393224 | tf_op jit(solution)/shard_map/ppermute | solution.py:278
  26.8 68.2 %collective-permute-start.1 = (bf16[2,4,64,128]{3,2,1,0:T(8,128)(2,1)S(1)}, bf16[2,4,64,128]{3,2,1,0:T(8,128)(2,1)S(1)}, u32[]{:S(2)}, u32[]{:S(2)}) collective-permute-start(bf16[2,4,64,128]{3,2,1,0:T(8,128)(2,1)S(1)} %get-tuple-element.52), channel_id=1, source_target_pairs={{0,4},{4,0},{8,12},{12,8},{1,5},{5,1},{9,13},{13,9},{2,6},{6,2},{1... | collective-permute-start | bytes 393224 | tf_op jit(solution)/shard_map/ppermute | solution.py:278
  27.3 68.3 %collective-permute-start.2 = (bf16[2,4,64,128]{3,2,1,0:T(8,128)(2,1)S(1)}, bf16[2,4,64,128]{3,2,1,0:T(8,128)(2,1)S(1)}, u32[]{:S(2)}, u32[]{:S(2)}) collective-permute-start(bf16[2,4,64,128]{3,2,1,0:T(8,128)(2,1)S(1)} %get-tuple-element.53), channel_id=1, source_target_pairs={{0,8},{4,12},{8,0},{12,4},{1,9},{5,13},{9,1},{13,5},{2,10},{6,14},... | collective-permute-start | bytes 393224 | tf_op jit(solution)/shard_map/ppermute | solution.py:278
  43.9 50.1 %all-to-all-start.1 = ((f32[4,2,7200]{2,1,0:T(2,128)}), f32[4,2,7200]{2,1,0:T(2,128)S(1)}, u32[]{:S(2)}, u32[]{:S(2)}) async-start(f32[4,2,7200]{2,1,0:T(2,128)} %all_to_all.12), calls=%async_computation.2 | async-start | bytes 466944 | tf_op jit(solution)/shard_map/all_to_all | solution.py:269
  47.3 257.2 %reduce-scatter.2.cloned.1.call-start = ((), (), s32[]{:S(2)}) async-start(), calls=%async_computation.3 | async-start | bytes 655360 | tf_op jit(solution)/shard_map/reduce_scatter | solution.py:355
  64.6 32.2 %collective-permute-start.3 = (bf16[2,4,64,128]{3,2,1,0:T(8,128)(2,1)S(1)}, bf16[2,4,64,128]{3,2,1,0:T(8,128)(2,1)S(1)}, u32[]{:S(2)}, u32[]{:S(2)}) collective-permute-start(bf16[2,4,64,128]{3,2,1,0:T(8,128)(2,1)S(1)} %get-tuple-element.54), channel_id=1, source_target_pairs={{0,12},{4,8},{8,4},{12,0},{1,13},{5,9},{9,5},{13,1},{2,14},{6,10},... | collective-permute-start | bytes 393224 | tf_op jit(solution)/shard_map/ppermute | solution.py:278
  66.4 53.9 %collective-permute-start.15 = (bf16[2,4,64,128]{3,2,1,0:T(8,128)(2,1)S(1)}, bf16[2,4,64,128]{3,2,1,0:T(8,128)(2,1)S(1)}, u32[]{:S(2)}, u32[]{:S(2)}) collective-permute-start(bf16[2,4,64,128]{3,2,1,0:T(8,128)(2,1)S(1)} %get-tuple-element.70), channel_id=1, source_target_pairs={{0,4},{4,0},{8,12},{12,8},{1,5},{5,1},{9,13},{13,9},{2,6},{6,2},{1... | collective-permute-start | bytes 393224 | tf_op jit(solution)/shard_map/ppermute | solution.py:278
  95.0 25.8 %collective-permute-start.16 = (bf16[2,4,64,128]{3,2,1,0:T(8,128)(2,1)S(1)}, bf16[2,4,64,128]{3,2,1,0:T(8,128)(2,1)}, u32[]{:S(2)}, u32[]{:S(2)}) collective-permute-start(bf16[2,4,64,128]{3,2,1,0:T(8,128)(2,1)S(1)} %get-tuple-element.71), channel_id=1, source_target_pairs={{0,8},{4,12},{8,0},{12,4},{1,9},{5,13},{9,1},{13,5},{2,10},{6,14},... | collective-permute-start | bytes 393224 | tf_op jit(solution)/shard_map/ppermute | solution.py:278
  95.6 26.1 %collective-permute-start.17 = (bf16[2,4,64,128]{3,2,1,0:T(8,128)(2,1)S(1)}, bf16[2,4,64,128]{3,2,1,0:T(8,128)(2,1)}, u32[]{:S(2)}, u32[]{:S(2)}) collective-permute-start(bf16[2,4,64,128]{3,2,1,0:T(8,128)(2,1)S(1)} %get-tuple-element.72), channel_id=1, source_target_pairs={{0,12},{4,8},{8,4},{12,0},{1,13},{5,9},{9,5},{13,1},{2,14},{6,10},... | collective-permute-start | bytes 393224 | tf_op jit(solution)/shard_map/ppermute | solution.py:278
  119.8 28.6 %collective-permute-start.12 = (bf16[2,4,64,128]{3,2,1,0:T(8,128)(2,1)S(1)}, bf16[2,4,64,128]{3,2,1,0:T(8,128)(2,1)S(1)}, u32[]{:S(2)}, u32[]{:S(2)}) collective-permute-start(bf16[2,4,64,128]{3,2,1,0:T(8,128)(2,1)S(1)} %get-tuple-element.66), channel_id=1, source_target_pairs={{0,4},{4,0},{8,12},{12,8},{1,5},{5,1},{9,13},{13,9},{2,6},{6,2},{1... | collective-permute-start | bytes 393224 | tf_op jit(solution)/shard_map/ppermute | solution.py:278
  120.3 28.7 %collective-permute-start.13 = (bf16[2,4,64,128]{3,2,1,0:T(8,128)(2,1)S(1)}, bf16[2,4,64,128]{3,2,1,0:T(8,128)(2,1)S(1)}, u32[]{:S(2)}, u32[]{:S(2)}) collective-permute-start(bf16[2,4,64,128]{3,2,1,0:T(8,128)(2,1)S(1)} %get-tuple-element.67), channel_id=1, source_target_pairs={{0,8},{4,12},{8,0},{12,4},{1,9},{5,13},{9,1},{13,5},{2,10},{6,14},... | collective-permute-start | bytes 393224 | tf_op jit(solution)/shard_map/ppermute | solution.py:278
  120.8 28.2 %collective-permute-start.14 = (bf16[2,4,64,128]{3,2,1,0:T(8,128)(2,1)S(1)}, bf16[2,4,64,128]{3,2,1,0:T(8,128)(2,1)S(1)}, u32[]{:S(2)}, u32[]{:S(2)}) collective-permute-start(bf16[2,4,64,128]{3,2,1,0:T(8,128)(2,1)S(1)} %get-tuple-element.68), channel_id=1, source_target_pairs={{0,12},{4,8},{8,4},{12,0},{1,13},{5,9},{9,5},{13,1},{2,14},{6,10},... | collective-permute-start | bytes 393224 | tf_op jit(solution)/shard_map/ppermute | solution.py:278
  143.1 58.4 %collective-permute-start = (f32[4,12320]{1,0:T(4,128)S(1)}, f32[4,12320]{1,0:T(4,128)S(1)}, u32[]{:S(2)}, u32[]{:S(2)}) collective-permute-start(f32[4,12320]{1,0:T(4,128)S(1)} %get-tuple-element.124), channel_id=1, source_target_pairs={{0,1},{1,0},{2,3},{3,2},{4,5},{5,4},{6,7},{7,6},{8,9},{9,8},{10,11... | collective-permute-start | bytes 591368 | tf_op jit(solution)/shard_map/ppermute | solution.py:266
  148.4 30.9 %collective-permute-start.10 = (bf16[2,4,64,128]{3,2,1,0:T(8,128)(2,1)S(1)}, bf16[2,4,64,128]{3,2,1,0:T(8,128)(2,1)S(1)}, u32[]{:S(2)}, u32[]{:S(2)}) collective-permute-start(bf16[2,4,64,128]{3,2,1,0:T(8,128)(2,1)S(1)} %get-tuple-element.63), channel_id=1, source_target_pairs={{0,8},{4,12},{8,0},{12,4},{1,9},{5,13},{9,1},{13,5},{2,10},{6,14},... | collective-permute-start | bytes 393224 | tf_op jit(solution)/shard_map/ppermute | solution.py:278
  149.0 30.3 %collective-permute-start.11 = (bf16[2,4,64,128]{3,2,1,0:T(8,128)(2,1)S(1)}, bf16[2,4,64,128]{3,2,1,0:T(8,128)(2,1)S(1)}, u32[]{:S(2)}, u32[]{:S(2)}) collective-permute-start(bf16[2,4,64,128]{3,2,1,0:T(8,128)(2,1)S(1)} %get-tuple-element.64), channel_id=1, source_target_pairs={{0,12},{4,8},{8,4},{12,0},{1,13},{5,9},{9,5},{13,1},{2,14},{6,10},... | collective-permute-start | bytes 393224 | tf_op jit(solution)/shard_map/ppermute | solution.py:278
  149.0 31.0 %collective-permute-start.9 = (bf16[2,4,64,128]{3,2,1,0:T(8,128)(2,1)S(1)}, bf16[2,4,64,128]{3,2,1,0:T(8,128)(2,1)S(1)}, u32[]{:S(2)}, u32[]{:S(2)}) collective-permute-start(bf16[2,4,64,128]{3,2,1,0:T(8,128)(2,1)S(1)} %get-tuple-element.62), channel_id=1, source_target_pairs={{0,4},{4,0},{8,12},{12,8},{1,5},{5,1},{9,13},{13,9},{2,6},{6,2},{1... | collective-permute-start | bytes 393224 | tf_op jit(solution)/shard_map/ppermute | solution.py:278
  179.3 22.6 %collective-permute-start.27 = (bf16[2,4,64,128]{3,2,1,0:T(8,128)(2,1)S(1)}, bf16[2,4,64,128]{3,2,1,0:T(8,128)(2,1)S(1)}, u32[]{:S(2)}, u32[]{:S(2)}) collective-permute-start(bf16[2,4,64,128]{3,2,1,0:T(8,128)(2,1)S(1)} %get-tuple-element.85), channel_id=1, source_target_pairs={{0,4},{4,0},{8,12},{12,8},{1,5},{5,1},{9,13},{13,9},{2,6},{6,2},{1... | collective-permute-start | bytes 393224 | tf_op jit(solution)/shard_map/ppermute | solution.py:278
  179.3 22.6 %collective-permute-start.28 = (bf16[2,4,64,128]{3,2,1,0:T(8,128)(2,1)S(1)}, bf16[2,4,64,128]{3,2,1,0:T(8,128)(2,1)S(1)}, u32[]{:S(2)}, u32[]{:S(2)}) collective-permute-start(bf16[2,4,64,128]{3,2,1,0:T(8,128)(2,1)S(1)} %get-tuple-element.86), channel_id=1, source_target_pairs={{0,8},{4,12},{8,0},{12,4},{1,9},{5,13},{9,1},{13,5},{2,10},{6,14},... | collective-permute-start | bytes 393224 | tf_op jit(solution)/shard_map/ppermute | solution.py:278
  180.0 22.0 %collective-permute-start.29 = (bf16[2,4,64,128]{3,2,1,0:T(8,128)(2,1)S(1)}, bf16[2,4,64,128]{3,2,1,0:T(8,128)(2,1)S(1)}, u32[]{:S(2)}, u32[]{:S(2)}) collective-permute-start(bf16[2,4,64,128]{3,2,1,0:T(8,128)(2,1)S(1)} %get-tuple-element.87), channel_id=1, source_target_pairs={{0,12},{4,8},{8,4},{12,0},{1,13},{5,9},{9,5},{13,1},{2,14},{6,10},... | collective-permute-start | bytes 393224 | tf_op jit(solution)/shard_map/ppermute | solution.py:278
  227.0 13.1 %collective-permute-start.30 = (bf16[4,4,64,128]{3,2,1,0:T(8,128)(2,1)}, bf16[4,4,64,128]{3,2,1,0:T(8,128)(2,1)S(1)}, u32[]{:S(2)}, u32[]{:S(2)}) collective-permute-start(bf16[4,4,64,128]{3,2,1,0:T(8,128)(2,1)} %get-tuple-element.88), channel_id=1, source_target_pairs={{0,1},{1,0},{2,3},{3,2},{4,5},{5,4},{6,7},{7,6},{8,9},{9,8},{10,11... | collective-permute-start | bytes 786440 | tf_op jit(solution)/shard_map/ppermute | solution.py:266
  288.4 35.1 %collective-permute-start.32 = (bf16[4,4,64,128]{3,2,1,0:T(8,128)(2,1)}, bf16[4,4,64,128]{3,2,1,0:T(8,128)(2,1)S(1)}, u32[]{:S(2)}, u32[]{:S(2)}) collective-permute-start(bf16[4,4,64,128]{3,2,1,0:T(8,128)(2,1)} %get-tuple-element.91), channel_id=1, source_target_pairs={{0,1},{1,0},{2,3},{3,2},{4,5},{5,4},{6,7},{7,6},{8,9},{9,8},{10,11... | collective-permute-start | bytes 786440 | tf_op jit(solution)/shard_map/ppermute | solution.py:266
  (75 other events, 431.9 us)
Sparse Core Ops, SparseCore 0:
  176.9 22.1 reduce-scatter.1

commit v2 on v1

v2 whole, which is shorter than its diff:
```python
import functools

import jax
import jax.numpy as jnp
from jax import lax
from jax.experimental import pallas as pl
from jax.experimental.pallas import tpu as pltpu
from jax.sharding import PartitionSpec as P

H = 128
P_SIZE = 64
N = 128
G = 8
R_PF = 8
PER_GROUP = H // G
X_WIDTH = PER_GROUP * P_SIZE
CHUNKS = 4
AHEAD = 2
LANES = 128
VMEM_LIMIT = 48 * 1024 * 1024

ANY = pl.BlockSpec(memory_space=pl.ANY)


def split_bf16(value):
    high = value.astype(jnp.bfloat16)
    low = (value - high.astype(jnp.float32)).astype(jnp.bfloat16)
    return high, low


class Plan:
    def __init__(self, req_count):
        self.cap = (R_PF + req_count - 1) // req_count
        self.places = req_count * self.cap
        self.rows = req_count * R_PF
        self.row_of = 0
        self.row_place = self.row_of + self.places
        self.slot_place = self.row_place + R_PF
        self.split_place = self.slot_place + R_PF
        self.live = self.split_place + R_PF
        self.parity = self.live + 1
        self.slot_row = self.parity + 1
        self.size = self.slot_row + self.rows


def plan_kernel(plan, request_slot, counts, out):
    me = lax.axis_index("req")
    parity = lax.axis_index("head") % 2
    half = R_PF // 2
    out[plan.live] = counts[me]
    out[plan.parity] = parity
    for place in range(plan.places):
        out[plan.row_of + place] = 0

    dests = [request_slot[me * R_PF + row] // R_PF for row in range(R_PF)]
    for row in range(R_PF):
        rank = sum([(dests[row] == dests[other]).astype(jnp.int32) for other in range(row)], 0)
        out[plan.row_place + row] = dests[row] * plan.cap + rank
        out[plan.row_of + (dests[row] ^ me) * plan.cap + rank] = row

    @pl.loop(0, plan.rows // R_PF)
    def _(group):
        seen = jnp.int32(0)
        for row in range(R_PF):
            slot = request_slot[group * R_PF + row]
            out[plan.slot_row + slot] = group * R_PF + row
            here = slot // R_PF == me
            local = slot % R_PF

            @pl.when(here)
            def _():
                out[plan.slot_place + local] = group * plan.cap + seen
                out[plan.split_place + (local + parity * half) % R_PF] = (
                    group ^ me
                ) * plan.cap + seen

            seen = seen + here.astype(jnp.int32)


def make_plan(plan, request_slot, counts):
    smem = pl.BlockSpec(memory_space=pltpu.SMEM)
    return pl.pallas_call(
        functools.partial(plan_kernel, plan),
        in_specs=[smem, smem],
        out_specs=smem,
        out_shape=jax.ShapeDtypeStruct((plan.size,), jnp.int32),
        name="plan",
    )(request_slot, counts)


def one_hot(shape, pairs):
    rows = lax.broadcasted_iota(jnp.int32, shape, 0)
    columns = lax.broadcasted_iota(jnp.int32, shape, 1)
    total = jnp.zeros(shape, jnp.float32)
    for row, column in pairs:
        total = jnp.where((rows == row) & (columns == column), 1.0, total)
    return total.astype(jnp.bfloat16)


def pick(matrix, values):
    return jnp.dot(matrix, values, preferred_element_type=jnp.float32)


def tokens_kernel(plan, table, xbc, z, dt, out):
    steps, groups = xbc.shape[:2]
    matrix = one_hot(
        (plan.places, R_PF), [(table[plan.slot_place + slot], slot) for slot in range(R_PF)]
    )

    def put(values, start):
        picked = pick(matrix, values)
        size = values.shape[1]
        for source in range(plan.places // plan.cap):
            rows = picked[source * plan.cap : (source + 1) * plan.cap]
            out[source, :, start : start + size] = rows.astype(jnp.bfloat16)

    at = 0
    for step in range(steps):
        for group in range(groups):
            put(xbc[step, group], at)
            at += xbc.shape[3]
        put(z[step], at)
        at += z.shape[2]
        put(dt[step], at)
        at += LANES


def pack_tokens(plan, table, xbc, z, dt):
    steps, groups = xbc.shape[:2]
    size = steps * (groups * xbc.shape[3] + z.shape[2] + LANES)
    return pl.pallas_call(
        functools.partial(tokens_kernel, plan),
        grid_spec=pltpu.PrefetchScalarGridSpec(
            num_scalar_prefetch=1,
            grid=(1,),
            in_specs=[whole(xbc), whole(z), whole(dt)],
            out_specs=pl.BlockSpec((plan.places // plan.cap, plan.cap, size), lambda i, t: (0, 0, 0)),
        ),
        out_shape=jax.ShapeDtypeStruct((plan.places // plan.cap, plan.cap, size), jnp.bfloat16),
        name="tokens",
    )(table, xbc, z, dt)


def whole(array):
    return pl.BlockSpec(array.shape, lambda *_: (0,) * array.ndim)


def silu(value):
    return value / (1.0 + jnp.exp(-value))


def rows_kernel(plan, table, tokens, conv, weight, bias, small, gain, state, *refs):
    normed, packet, read, read_taps, acts, wide, gates, lines = refs
    steps = 2
    taps, groups, conv_width = weight.shape
    heads = state.shape[1]
    channels = groups * X_WIDTH
    index = pl.program_id(0)
    row_ids = lax.broadcasted_iota(jnp.int32, (R_PF, 1), 0)
    live = row_ids < table[plan.live]
    f32, bf16 = jnp.float32, jnp.bfloat16
    update_at = 0
    taps_at = update_at + steps * channels
    last_at = taps_at + steps * groups * N
    decay_at = last_at + groups * conv_width

    @pl.when(index == 0)
    def _():
        matrix = one_hot(
            (R_PF, plan.places), [(row, table[plan.row_place + row]) for row in range(R_PF)]
        )
        stride = tokens.shape[2] // steps

        def rows_of(start, size):
            parts = [tokens[source, :, start : start + size] for source in range(tokens.shape[0])]
            parts = jnp.concatenate([part.astype(f32) for part in parts], axis=0)
            return pick(matrix, parts.astype(bf16))

        for group in range(groups):
            window = [
                jnp.where(live, conv[tap, group], 0.0) for tap in range(taps - 1)
            ] + [
                rows_of(step * stride + group * conv_width, conv_width) for step in range(steps)
            ]
            kernel = [weight[tap].astype(f32)[group : group + 1] for tap in range(taps)]
            offset = bias[...].astype(f32)[group : group + 1]
            parts = []
            for step in range(steps):
                total = sum(window[step + tap] * kernel[tap] for tap in range(taps)) + offset
                act = silu(total)
                acts[step, group] = act
                parts.append(act[:, X_WIDTH + N :])
            high = [part.astype(bf16).astype(f32) for part in parts]
            low = [part - near for part, near in zip(parts, high)]
            read_taps[group] = jnp.concatenate(high + low, axis=0).astype(bf16)
            start = last_at + group * conv_width
            lines[:, start : start + conv_width] = window[taps - 2]

        dts, decays = [], []
        rate = jnp.exp(small[0:1, :heads])
        for step in range(steps):
            base = step * stride + groups * conv_width
            gates[step] = silu(rows_of(base, channels))
            raw = rows_of(base + channels, LANES)[:, :heads] + small[1:2, :heads]
            dts.append(jnp.maximum(raw, 0.0) + jnp.log1p(jnp.exp(-jnp.abs(raw))))
            decays.append(jnp.exp(-dts[-1] * rate))
        lines[:, decay_at : decay_at + LANES] = jnp.concatenate(
            [jnp.where(live, decays[0] * decays[1], 0.0), jnp.zeros((R_PF, LANES - heads), f32)],
            axis=1,
        )
        skip = jnp.broadcast_to(small[2:3, :heads], (R_PF, heads))
        narrow = jnp.concatenate(dts + decays + [skip], axis=0)
        high = narrow.astype(bf16).astype(f32)
        middle = (narrow - high).astype(bf16).astype(f32)
        narrow = jnp.concatenate([high, middle, narrow - high - middle], axis=1).astype(bf16)
        head_ids = lax.broadcasted_iota(jnp.int32, (3 * heads, channels), 0) % heads
        channel_ids = lax.broadcasted_iota(jnp.int32, (3 * heads, channels), 1) // P_SIZE
        spread = pick(narrow, (head_ids == channel_ids).astype(bf16))
        for part in range(5):
            wide[part] = spread[part * R_PF : (part + 1) * R_PF]

    for group in range(groups):
        rows = state[0, group * PER_GROUP : (group + 1) * PER_GROUP].reshape(X_WIDTH, N)
        state_high, state_low = split_bf16(rows)
        dims = (((1,), (1,)), ((), ()))
        total = lax.dot_general(read_taps[group], state_high, dims, preferred_element_type=f32)
        rest = lax.dot_general(
            read_taps[group, : steps * R_PF], state_low, dims, preferred_element_type=f32
        )
        total = total[: steps * R_PF] + total[steps * R_PF :] + rest
        for step in range(steps):
            part = total[step * R_PF : (step + 1) * R_PF]
            read[group, step] = jnp.where(row_ids == index, part, read[group, step])

    @pl.when(index == R_PF - 1)
    def _():
        for group in range(groups):
            span = slice(group * X_WIDTH, (group + 1) * X_WIDTH)
            x = [acts[step, group, :, :X_WIDTH] for step in range(steps)]
            b = [acts[step, group, :, X_WIDTH : X_WIDTH + N] for step in range(steps)]
            c = [acts[step, group, :, X_WIDTH + N :] for step in range(steps)]
            u = [wide[step, :, span] * x[step] for step in range(steps)]
            first_decay, second_decay, skip = wide[2, :, span], wide[3, :, span], wide[4, :, span]
            held = [jnp.where(live, read[group, step], 0.0) for step in range(steps)]

            def pair_sum(one, two):
                return jnp.sum(one * two, axis=1, keepdims=True)

            later = second_decay * u[0]
            y = [
                first_decay * held[0] + pair_sum(b[0], c[0]) * u[0] + skip * x[0],
                second_decay * first_decay * held[1]
                + pair_sum(b[0], c[1]) * later
                + pair_sum(b[1], c[1]) * u[1]
                + skip * x[1],
            ]
            result = []
            for step in range(steps):
                gated = y[step] * gates[step, :, span]
                scale = lax.rsqrt(jnp.mean(gated * gated, axis=1, keepdims=True) + 1e-05)
                result.append(gated * scale * gain[0:1, span])
            normed[:, span] = jnp.concatenate(result, axis=0).astype(bf16)
            lines[:, span] = later
            lines[:, channels + group * X_WIDTH : channels + (group + 1) * X_WIDTH] = u[1]
            for step in range(steps):
                start = taps_at + (step * groups + group) * N
                lines[:, start : start + N] = b[step]
        for row in range(R_PF):
            packet[table[plan.row_place + row]] = lines[row : row + 1]


def run_rows(plan, table, tokens, conv, weight, bias, small, gain, ssm_state):
    taps, groups, conv_width = weight.shape
    steps = 2
    heads = ssm_state.shape[1]
    channels = groups * X_WIDTH
    size = steps * channels + steps * groups * N + groups * conv_width + LANES
    f32 = jnp.float32
    return pl.pallas_call(
        functools.partial(rows_kernel, plan),
        grid_spec=pltpu.PrefetchScalarGridSpec(
            num_scalar_prefetch=1,
            grid=(R_PF,),
            in_specs=[
                whole(tokens),
                whole(conv),
                whole(weight),
                whole(bias),
                whole(small),
                whole(gain),
                pl.BlockSpec((1, heads, P_SIZE, N), lambda i, t: (i, 0, 0, 0)),
            ],
            out_specs=[
                pl.BlockSpec((steps * R_PF, channels), lambda i, t: (0, 0)),
                pl.BlockSpec((plan.places, 1, size), lambda i, t: (0, 0, 0)),
            ],
            scratch_shapes=[
                pltpu.VMEM((groups, steps, R_PF, X_WIDTH), f32),
                pltpu.VMEM((groups, 2 * steps * R_PF, N), jnp.bfloat16),
                pltpu.VMEM((steps, groups, R_PF, conv_width), f32),
                pltpu.VMEM((5, R_PF, channels), f32),
                pltpu.VMEM((steps, R_PF, channels), f32),
                pltpu.VMEM((R_PF, size), f32),
            ],
        ),
        out_shape=[
            jax.ShapeDtypeStruct((steps * R_PF, channels), jnp.bfloat16),
            jax.ShapeDtypeStruct((plan.places, 1, size), f32),
        ],
        compiler_params=pltpu.CompilerParams(vmem_limit_bytes=VMEM_LIMIT),
        cost_estimate=pl.CostEstimate(
            flops=64 * ssm_state.size, bytes_accessed=4 * ssm_state.size, transcendentals=0
        ),
        name="rows",
    )(table, tokens, conv, weight, bias, small, gain, ssm_state)


def project_kernel(plan, share, table, normed, weight, out, picked):
    steps = 2

    @pl.when(pl.program_id(0) == 0)
    def _():
        shape = (steps * plan.rows, steps * plan.rows)
        rows = lax.broadcasted_iota(jnp.int32, shape, 0)
        columns = lax.broadcasted_iota(jnp.int32, shape, 1)

        def add(slot, total):
            row = table[plan.slot_row + slot]
            target = (slot // share) * steps * share + slot % share
            source = (row // R_PF) * steps * R_PF + row % R_PF
            for step in range(steps):
                hit = (rows == target + step * share) & (columns == source + step * R_PF)
                total = jnp.where(hit, 1.0, total)
            return total

        matrix = lax.fori_loop(0, plan.rows, add, jnp.zeros(shape, jnp.float32), unroll=8)
        picked[...] = pick(matrix.astype(jnp.bfloat16), normed[...]).astype(jnp.bfloat16)

    out[...] = pick(picked[...], weight[...])


def project(plan, share, table, normed, weight):
    rows, depth = normed.shape
    columns = weight.shape[1]
    block = min(512, columns)
    return pl.pallas_call(
        functools.partial(project_kernel, plan, share),
        grid_spec=pltpu.PrefetchScalarGridSpec(
            num_scalar_prefetch=1,
            grid=(columns // block,),
            in_specs=[whole(normed), pl.BlockSpec((depth, block), lambda i, t: (0, i))],
            out_specs=pl.BlockSpec((rows, block), lambda i, t: (0, i)),
            scratch_shapes=[pltpu.VMEM((rows, depth), jnp.bfloat16)],
        ),
        out_shape=jax.ShapeDtypeStruct((rows, columns), jnp.float32),
        compiler_params=pltpu.CompilerParams(vmem_limit_bytes=VMEM_LIMIT),
        cost_estimate=pl.CostEstimate(
            flops=2 * rows * weight.size, bytes_accessed=2 * weight.size, transcendentals=0
        ),
        name="project",
    )(table, normed, weight)


def slots_kernel(plan, table, packet, tokens, own, other):
    half = R_PF // 2
    size = packet.shape[2]
    for local in range(R_PF):
        target = own if local < half else other
        slot = (local + table[plan.parity] * half) % R_PF
        target[local % half, :, :size] = packet[table[plan.slot_place + slot]]
        target[local % half, :, size:] = tokens[slot]


def split_slots(plan, table, packet, tokens):
    shape = (R_PF // 2, 1, packet.shape[2] + tokens.shape[2])
    out = jax.ShapeDtypeStruct(shape, jnp.float32)
    return pl.pallas_call(
        functools.partial(slots_kernel, plan),
        grid_spec=pltpu.PrefetchScalarGridSpec(
            num_scalar_prefetch=1,
            grid=(1,),
            in_specs=[whole(packet), whole(tokens)],
            out_specs=[whole(out)] * 2,
        ),
        out_shape=[out, out],
        name="slots",
    )(table, packet, tokens)


def windows_kernel(plan, groups, conv_width, starts, table, own, got, out):
    parity = table[plan.parity]
    for owner, packet in enumerate((own, got)):
        side = jnp.where(parity == owner, 0, groups)
        for slot in range(R_PF // 2):
            for row, start in enumerate(starts):
                for group in range(groups):
                    first = start + group * conv_width
                    out[0, 0, slot, row, pl.ds(side + group, 1)] = packet[
                        slot, :, first : first + conv_width
                    ]


def write_windows(plan, table, own, got, groups, conv_width, starts):
    shape = (1, 1, R_PF // 2, len(starts), 2 * groups, conv_width)
    out = jax.ShapeDtypeStruct(shape, jnp.float32)
    return pl.pallas_call(
        functools.partial(windows_kernel, plan, groups, conv_width, starts),
        grid_spec=pltpu.PrefetchScalarGridSpec(
            num_scalar_prefetch=1,
            grid=(1,),
            in_specs=[whole(own), whole(got)],
            out_specs=whole(out),
        ),
        out_shape=out,
        name="windows",
    )(table, own, got)


def pack_kernel(count, cap, _rows, *refs):
    inputs, outputs = refs[:count], refs[-(count // cap) :]
    for place in range(count):
        outputs[place // cap][place % cap] = inputs[place][0].astype(jnp.bfloat16)


def pack_chunk(plan, table, ssm_state, chunk, width, after):
    count, cap = plan.places, plan.cap
    block = (1, width, P_SIZE, N)
    specs = [
        pl.BlockSpec(block, functools.partial(lambda i, rows, p: (rows[plan.row_of + p], chunk, 0, 0), p=p))
        for p in range(count)
    ]
    shape = (cap, width, P_SIZE, N)
    return pl.pallas_call(
        functools.partial(pack_kernel, count, cap),
        grid_spec=pltpu.PrefetchScalarGridSpec(
            num_scalar_prefetch=1,
            grid=(1,),
            in_specs=specs + [ANY] * len(after),
            out_specs=[pl.BlockSpec(shape, lambda i, rows: (0, 0, 0, 0))] * (count // cap),
        ),
        out_shape=[jax.ShapeDtypeStruct(shape, jnp.bfloat16)] * (count // cap),
        compiler_params=pltpu.CompilerParams(vmem_limit_bytes=VMEM_LIMIT),
        cost_estimate=pl.CostEstimate(
            flops=0, bytes_accessed=6 * count * width * P_SIZE * N, transcendentals=0
        ),
        name="pack",
    )(table, *([ssm_state] * count), *after)


def route_kernel(plan, sources, table, *refs):
    cap = plan.cap
    arrived, keep, give = refs[:sources], refs[-2], refs[-1]
    half = keep.shape[0]
    for index in range(2 * half):
        target = keep if index < half else give
        place = table[plan.split_place + index]
        for source in range(sources):

            @pl.when(place // cap == source)
            def _():
                target[index % half] = arrived[source][place % cap]


def route_chunk(plan, table, arrived, half, after):
    shape = (half,) + arrived[0].shape[1:]
    out = jax.ShapeDtypeStruct(shape, jnp.bfloat16)
    return pl.pallas_call(
        functools.partial(route_kernel, plan, len(arrived)),
        grid_spec=pltpu.PrefetchScalarGridSpec(
            num_scalar_prefetch=1,
            grid=(1,),
            in_specs=[whole(one) for one in arrived] + [ANY] * len(after),
            out_specs=[whole(out)] * 2,
        ),
        out_shape=[out, out],
        compiler_params=pltpu.CompilerParams(vmem_limit_bytes=VMEM_LIMIT),
        cost_estimate=pl.CostEstimate(
            flops=0, bytes_accessed=8 * half * arrived[0][0].size, transcendentals=0
        ),
        name="route",
    )(table, *arrived, *after)


def finish_kernel(plan, width, heads, base, table, decay, keep, got, *refs):
    parts, out, done = refs[:8], refs[-2], refs[-1]
    owner = pl.program_id(0)
    slots = keep.shape[0]
    done[...] = jnp.zeros_like(done)

    def stack(first, second, slot):
        rows = jnp.concatenate([first[slot], second[slot]], axis=0)
        high = rows.astype(jnp.bfloat16).astype(jnp.float32)
        return high, rows - high

    def fill(source, first_update, second_update, first_taps, second_taps):
        for slot in range(slots):
            update_high, update_low = stack(first_update, second_update, slot)
            taps_high, taps_low = stack(first_taps, second_taps, slot)
            updates = jnp.concatenate([update_high, update_low, update_high, update_low], axis=0)
            taps = jnp.concatenate([taps_high, taps_high, taps_low, taps_low], axis=0)
            added = lax.dot_general(
                updates.astype(jnp.bfloat16),
                taps.astype(jnp.bfloat16),
                (((0,), (0,)), ((), ())),
                preferred_element_type=jnp.float32,
            ).reshape(width, P_SIZE, N)
            for head in range(width):
                factor = decay[(owner * slots + slot) * heads + base + head]
                out[0, 0, slot, head] = (
                    factor * source[slot, head].astype(jnp.float32) + added[head]
                )

    pl.when(owner == 0)(lambda: fill(keep, *parts[:4]))
    pl.when(owner == 1)(lambda: fill(got, *parts[4:]))


def finish_chunk(plan, table, so_far, keep, got, decay, own, other, chunk, heads):
    slots, width = keep.shape[:2]
    per_half = heads // width
    span = width * P_SIZE
    channels = heads * P_SIZE
    groups = heads // PER_GROUP
    group = chunk * width // PER_GROUP
    taps_at = 2 * channels // N
    out_shape = jax.ShapeDtypeStruct((1, 1, slots, 2 * heads, P_SIZE, N), jnp.float32)
    extra = [] if so_far is None else [so_far]

    def part(size, place):
        return pl.BlockSpec((slots, 1, size), lambda o, t, d: (0, 0, place))

    parts = [
        part(span, chunk),
        part(span, channels // span + chunk),
        part(N, taps_at + group),
        part(N, taps_at + groups + group),
    ]
    side = lambda o, t: (o + t[plan.parity]) % 2
    return pl.pallas_call(
        functools.partial(finish_kernel, plan, width, heads, chunk * width),
        grid_spec=pltpu.PrefetchScalarGridSpec(
            num_scalar_prefetch=2,
            grid=(2,),
            in_specs=[whole(keep), whole(got)] + parts + parts + [ANY] * len(extra),
            out_specs=[
                pl.BlockSpec(
                    (1, 1, slots, width, P_SIZE, N),
                    lambda o, t, d: (0, 0, 0, side(o, t) * per_half + chunk, 0, 0),
                ),
                pl.BlockSpec((8, 128), lambda o, t, d: (0, 0)),
            ],
        ),
        out_shape=[out_shape, jax.ShapeDtypeStruct((8, 128), jnp.float32)],
        input_output_aliases={12: 0} if extra else {},
        compiler_params=pltpu.CompilerParams(vmem_limit_bytes=VMEM_LIMIT),
        cost_estimate=pl.CostEstimate(
            flops=64 * slots * width * P_SIZE * N,
            bytes_accessed=12 * slots * width * P_SIZE * N,
            transcendentals=0,
        ),
        name="finish",
    )(table, decay, keep, got, *([own] * 4), *([other] * 4), *extra)


def on_device(
    ssm_state,
    conv_state,
    counts,
    request_slot,
    token_xbc,
    token_z,
    token_dt,
    conv_weight,
    conv_bias,
    a_log,
    dt_bias,
    d_skip,
    norm_gain,
    out_weight,
):
    f32 = jnp.float32
    req_count = lax.axis_size("req")
    head_count = lax.axis_size("head")
    plan = Plan(req_count)
    slot_dev = R_PF // 2
    steps = token_xbc.shape[0]
    heads = ssm_state.shape[1]
    groups = conv_state.shape[2]
    conv_width = conv_state.shape[3]
    width = heads // CHUNKS
    channels = groups * X_WIDTH

    def swap(value):
        return lax.ppermute(value, "head", [(i, i ^ 1) for i in range(head_count)])

    def exchange(value):
        return lax.all_to_all(value, "req", split_axis=0, concat_axis=0, tiled=True)

    table = make_plan(plan, request_slot, counts)

    tokens = exchange(
        pack_tokens(plan, table, jnp.swapaxes(token_xbc, 1, 2), token_z, token_dt)
    )
    small = jnp.stack([a_log, dt_bias, d_skip]).astype(f32)
    normed, packet = run_rows(
        plan,
        table,
        tokens,
        jnp.moveaxis(conv_state, 0, 2),
        conv_weight,
        conv_bias,
        small,
        norm_gain.astype(f32)[None],
        ssm_state,
    )

    share = plan.rows // head_count
    projected = project(
        plan, share, table, lax.all_gather(normed, "req", axis=0, tiled=True), out_weight
    ).reshape(head_count, -1, out_weight.shape[1])
    layer_out = lax.psum_scatter(projected, "head", scatter_dimension=0, tiled=True)
    layer_out = layer_out.astype(jnp.bfloat16).reshape(steps, share, -1)

    local_tokens = jnp.swapaxes(token_xbc, 0, 1).reshape(R_PF, 1, -1).astype(f32)
    own, other = split_slots(plan, table, exchange(packet), local_tokens)
    other = swap(other)
    taps_at = steps * channels
    last_at = taps_at + steps * groups * N
    decay_at = last_at + groups * conv_width
    fresh_at = decay_at + LANES
    starts = [last_at] + [fresh_at + step * groups * conv_width for step in range(steps)]
    out_conv = write_windows(plan, table, own, other, groups, conv_width, starts)
    decay = jnp.stack([own, other])[:, :, 0, decay_at : decay_at + heads].reshape(-1)

    gives, gots, dones, out_ssm = [], [], [], None
    for chunk in range(CHUNKS):
        packed = pack_chunk(plan, table, ssm_state, chunk, width, gives[: chunk - AHEAD + 1][-1:])
        arrived = [packed[0]]
        for shift in range(1, req_count):
            pairs = [(i, i ^ shift) for i in range(req_count)]
            arrived.append(lax.ppermute(packed[shift], "req", pairs))
        keep, give = route_chunk(
            plan, table, arrived, slot_dev, gots[-1:] + dones[: chunk - 1][-1:]
        )
        gives.append(give)
        gots.append(swap(give))
        out_ssm, done = finish_chunk(
            plan, table, out_ssm, keep, gots[-1], decay, own, other, chunk, heads
        )
        dones.append(done)
    return (layer_out, out_ssm, out_conv)


def solution(mesh):
    in_specs = (
        P(("groups", "req"), "head", None, None),
        P(("groups", "req"), None, "head", None),
        P("groups"),
        P("groups"),
        P(None, ("groups", "req"), "head", None),
        P(None, ("groups", "req"), "head"),
        P(None, ("groups", "req"), "head"),
        P(None, "head", None),
        P("head", None),
        P("head"),
        P("head"),
        P("head"),
        P("head"),
        P("head", "req"),
    )
    out_specs = (
        P(None, ("groups", "head"), "req"),
        P(("groups", "req"), "head", None, None, None, None),
        P(("groups", "req"), "head", None, None, None, None),
    )
    return jax.shard_map(
        on_device, mesh=mesh, in_specs=in_specs, out_specs=out_specs, check_vma=False
    )
```

time: 336 us -> 151 us (0.45)
  Pallas kernels: 202 us -> 49.2 us
  local copies, waits for them, and re-layouts: 33.2 us -> 9.19 us
  waiting for transfers between devices: 23.5 us -> 44.2 us
  starting transfers between devices: 36.1 us -> 22.7 us
  other arithmetic: 12.5 us -> 2.32 us
  matrix products: 5.75 us -> 0 us
    pallas_call x17 -> x14, Pallas kernels: 187 us -> 39 us  [the longest x4 9.5 us: finish_chunk(): pl.pallas_call(functools.partial(finish_kernel, plan, width, heads, chunk...]
    ppermute x9 -> x5, waiting for transfers between devices: 10.8 us -> 22.5 us  [swap(): return lax.ppermute(value, 'head', [(i, i ^ 1) for i in range(head_count)])]
    ppermute x24 -> x12, waiting for transfers between devices: 12.7 us -> 21.7 us  [on_device(): arrived.append(lax.ppermute(packed[shift], 'req', pairs))]
    ppermute x24 -> x12, starting transfers between devices: 17.9 us -> 9.34 us  [on_device(): arrived.append(lax.ppermute(packed[shift], 'req', pairs))]
    gather x7 -> x0, local copies, waits for them, and re-layouts: 6.92 us -> none  [the longest x6 5.75 us: take_rows(): return jnp.take(values, index, axis=axis, mode='clip')]
    unnamed x136 -> x54, local copies, waits for them, and re-layouts: 14.3 us -> 8.18 us
    dot_general x1 -> x0, matrix products: 5.75 us -> none  [on_device(): jnp.einsum('tsc,cd->tsd', normed_all, out_weight, preferred_element_type=...]
    pallas_call x8 -> x4, Pallas kernels: 15.1 us -> 10.2 us  [pack_chunk(): pl.pallas_call(functools.partial(pack_kernel, count, cap), grid_spec=pltp...]
  transfers between devices with their start and end apart: 36 -> 20, of which waited for: 7 -> 6; matrix products, arithmetic and copies ran while one was open for 9% -> 3% of each run, Pallas kernels for 59% -> 28%
where the time goes in v2:
time: 151 us; the launch traced here: 150 us
  Pallas kernels  49.2 us (33%)
  waiting for transfers between devices  44.2 us (29%)
  starting transfers between devices  22.7 us (15%)
  between operations  14.4 us (10%)
  local copies, waits for them, and re-layouts  9.19 us (6%)
  blocking collectives  7.88 us (5%)
  other arithmetic  2.32 us (2%)
    ppermute x5, waiting for transfers between devices, swap(): return lax.ppermute(value, 'head', [(i, i ^ 1) for i in range(head_count)])  22.5 us
    ppermute x12, waiting for transfers between devices, on_device(): arrived.append(lax.ppermute(packed[shift], 'req', pairs))  21.7 us
    pallas_call x4, Pallas kernels, pack_chunk(): pl.pallas_call(functools.partial(pack_kernel, count, cap), grid_spec=pltp...  10.2 us
    pallas_call x4, Pallas kernels, finish_chunk(): pl.pallas_call(functools.partial(finish_kernel, plan, width, heads, chunk...  9.5 us
    ppermute x12, starting transfers between devices, on_device(): arrived.append(lax.ppermute(packed[shift], 'req', pairs))  9.34 us
    pallas_call x1, Pallas kernels, run_rows(): pl.pallas_call(functools.partial(rows_kernel, plan), grid_spec=pltpu.Pref...  9.25 us
    unnamed x54, local copies, waits for them, and re-layouts  8.18 us
    all_gather x1, blocking collectives, on_device(): lax.all_gather(normed, 'req', axis=0, tiled=True)  7.88 us
  transfers between devices with their start and end apart: 20, of which 6 were waited for; matrix products, arithmetic and copies ran while one was open for 3% of the time, Pallas kernels for 28%

profile of v2, /device:TPU:0, one launch (start us, length us, event | category | flops | bytes accessed | tf_op | source)
XLA Modules:
  0.0 149.8 jit_solution(6528361724995824693)
XLA Ops:
  9.5 2.1 %pack.5 = (bf16[2,8,64,128]{3,2,1,0:T(8,128)(2,1)S(1)}, bf16[2,8,64,128]{3,2,1,0:T(8,128)(2,1)S(1)}, bf16[2,8,64,128]{3,2,1,0:T(8,128)(2,1)S(1)}, bf16[2,8,64,128]{3,2,1,0:T(8,128)(2,1)S(1)}) custom-call(s32[66]{0:T(128)S(1)} %copy-done.13, f32[8,32,64,128]{3,2,1,0:T(8,128)} %refs_7_.7, f32[8,32,64,128]{3,2,1,0:T(8,128)} %refs_7_.7, ...), custom_call_target="tpu_custom_call" | custom-call | bytes 3145728 | tf_op jit(solution)/shard_map/pack/pallas_call | solution.py:433
  12.2 2.6 %collective-permute-start.5 = (bf16[2,8,64,128]{3,2,1,0:T(8,128)(2,1)S(1)}, bf16[2,8,64,128]{3,2,1,0:T(8,128)(2,1)S(1)}, u32[]{:S(2)}, u32[]{:S(2)}) collective-permute-start(bf16[2,8,64,128]{3,2,1,0:T(8,128)(2,1)S(1)} %get-tuple-element.47), channel_id=1, source_target_pairs={{0,8},{4,12},{8,0},{12,4},{1,9},{5,13},{9,1},{13,5},{2,10},{6,14},... | collective-permute-start | bytes 786440 | tf_op jit(solution)/shard_map/ppermute | solution.py:640
  14.8 7.1 %collective-permute-done.5.refs_2_ = bf16[2,8,64,128]{3,2,1,0:T(8,128)(2,1)S(1)} collective-permute-done((bf16[2,8,64,128]{3,2,1,0:T(8,128)(2,1)S(1)}, bf16[2,8,64,128]{3,2,1,0:T(8,128)(2,1)S(1)}, u32[]{:S(2)}, u32[]{:S(2)}) %collective-permute-start.5) | collective-permute-done | bytes 262176 | tf_op jit(solution)/shard_map/ppermute | solution.py:640
  21.9 5.1 %collective-permute-done.6.refs_3_ = bf16[2,8,64,128]{3,2,1,0:T(8,128)(2,1)S(1)} collective-permute-done((bf16[2,8,64,128]{3,2,1,0:T(8,128)(2,1)S(1)}, bf16[2,8,64,128]{3,2,1,0:T(8,128)(2,1)S(1)}, u32[]{:S(2)}, u32[]{:S(2)}) %collective-permute-start.6) | collective-permute-done | bytes 262176 | tf_op jit(solution)/shard_map/ppermute | solution.py:640
  30.2 2.5 %tokens.1 = bf16[4,2,9472]{2,1,0:T(2,128)(2,1)} custom-call(s32[66]{0:T(128)} %plan.1.table._rows, bf16[2,2,8,1280]{3,2,1,0:T(8,128)(2,1)} %bitcast.21, bf16[2,8,2048]{2,1,0:T(8,128)(2,1)} %z.1, bf16[2,8,32]{2,1,0:T(8,128)(2,1)} %dt.1), custom_call_target="tpu_custom_call" | custom-call | tf_op jit(solution)/shard_map/tokens/pallas_call | solution.py:131
  32.7 3.3 %all-to-all-start = ((bf16[4,2,9472]{2,1,0:T(2,128)(2,1)}), bf16[4,2,9472]{2,1,0:T(2,128)(2,1)S(1)}, u32[]{:S(2)}, u32[]{:S(2)}) async-start(bf16[4,2,9472]{2,1,0:T(2,128)(2,1)} %tokens.1), calls=%async_computation | async-start | bytes 303104 | tf_op jit(solution)/shard_map/all_to_all | solution.py:596
  36.1 2.9 %pack.4 = (bf16[2,8,64,128]{3,2,1,0:T(8,128)(2,1)S(1)}, bf16[2,8,64,128]{3,2,1,0:T(8,128)(2,1)}, bf16[2,8,64,128]{3,2,1,0:T(8,128)(2,1)}, bf16[2,8,64,128]{3,2,1,0:T(8,128)(2,1)S(1)}) custom-call(s32[66]{0:T(128)S(1)} %copy-done.14, f32[8,32,64,128]{3,2,1,0:T(8,128)} %refs_7_.7, f32[8,32,64,128]{3,2,1,0:T(8,128)} %refs_7_.7, f32[8,32,64,128]{3,2,1,0:T(8,128)} %refs_7_.7, ...), custom_call_target="tpu_custom_call" | custom-call | bytes 3145728 | tf_op jit(solution)/shard_map/pack/pallas_call | solution.py:433
  41.2 9.3 %rows.1 = (bf16[16,2048]{1,0:T(8,128)(2,1)S(1)}, f32[8,1,7296]{2,1,0:T(1,128)}) custom-call(s32[66]{0:T(128)S(1)} %copy-done.14, bf16[4,2,9472]{2,1,0:T(2,128)(2,1)S(1)} %all-to-all-done.tokens, f32[3,2,8,1280]{3,2,1,0:T(8,128)S(1)} %bitcast.19, bf16[4,2,1280]{2,1,0:T(2,128)(2,1)S(1)} %copy-done.17, bf16[2,1280]{1,0:T(2,128)(2,1)S(1)} %copy-done.18, ...), custom_call_target="tpu_custom_call" | custom-call | flops 134217728 | bytes 8388608 | tf_op jit(solution)/shard_map/rows/pallas_call | solution.py:279
  50.5 4.0 %all-to-all-start.1 = ((f32[8,1,7296]{2,1,0:T(1,128)}), f32[8,1,7296]{2,1,0:T(1,128)}, u32[]{:S(2)}, u32[]{:S(2)}) async-start(f32[8,1,7296]{2,1,0:T(1,128)} %get-tuple-element.38), calls=%async_computation.2 | async-start | bytes 466944 | tf_op jit(solution)/shard_map/all_to_all | solution.py:596
  54.6 7.9 %all_gather.3.normed = bf16[64,2048]{1,0:T(8,128)(2,1)S(1)} all-gather(bf16[16,2048]{1,0:T(8,128)(2,1)S(1)} %get-tuple-element.37), channel_id=1, replica_groups=mesh['groups'=2,'req'=4,'head'=4] {'req'}, dimensions={0}, use_global_device_ids=true | all-gather | bytes 327680 | tf_op jit(solution)/shard_map/all_gather | solution.py:618
  62.4 6.9 %project.1 = f32[64,2048]{1,0:T(8,128)} custom-call(s32[66]{0:T(128)S(1)} %copy-done.14, bf16[64,2048]{1,0:T(8,128)(2,1)S(1)} %all_gather.3.normed, bf16[2048,2048]{1,0:T(8,128)(2,1)} %weight.3), custom_call_target="tpu_custom_call" | custom-call | flops 536870912 | bytes 8388608 | tf_op jit(solution)/shard_map/project/pallas_call | solution.py:346
  69.4 3.0 %pack.7 = (bf16[2,8,64,128]{3,2,1,0:T(8,128)(2,1)S(1)}, bf16[2,8,64,128]{3,2,1,0:T(8,128)(2,1)}, bf16[2,8,64,128]{3,2,1,0:T(8,128)(2,1)}, bf16[2,8,64,128]{3,2,1,0:T(8,128)(2,1)}) custom-call(s32[66]{0:T(128)S(1)} %copy-done.14, f32[8,32,64,128]{3,2,1,0:T(8,128)} %refs_7_.7, f32[8,32,64,128]{3,2,1,0:T(8,128)} %refs_7_.7, f32[8,32,64,128]{3,2,1,0:T(8,128)} %refs_7_.7, ...), custom_call_target="tpu_custom_call" | custom-call | bytes 3145728 | tf_op jit(solution)/shard_map/pack/pallas_call | solution.py:433
  81.5 2.5 %slots.1 = (f32[4,1,12416]{2,1,0:T(1,128)}, f32[4,1,12416]{2,1,0:T(1,128)}) custom-call(s32[66]{0:T(128)} %plan.1.table._rows, f32[8,1,7296]{2,1,0:T(1,128)} %all-to-all-done.1.packet, f32[8,1,5120]{2,1,0:T(1,128)} %reshape.30.tokens), custom_call_target="tpu_custom_call" | custom-call | tf_op jit(solution)/shard_map/slots/pallas_call | solution.py:377
  85.6 16.2 %collective-permute-done.refs_4_.refs_5_.refs_6_.refs_7_.got = f32[4,1,12416]{2,1,0:T(1,128)S(1)} collective-permute-done((f32[4,1,12416]{2,1,0:T(1,128)}, f32[4,1,12416]{2,1,0:T(1,128)S(1)}, u32[]{:S(2)}, u32[]{:S(2)}) %collective-permute-start) | collective-permute-done | bytes 198688 | tf_op jit(solution)/shard_map/ppermute | solution.py:593
  103.6 2.4 %finish.4 = (f32[1,1,4,64,64,128]{5,4,3,2,1,0:T(8,128)}, f32[8,128]{1,0:T(8,128)S(1)}) custom-call(s32[66]{0:T(128)S(1)} %copy-done.15, f32[256]{0:T(256)S(1)} %reshape_squeeze.3.decay, bf16[4,8,64,128]{3,2,1,0:T(8,128)(2,1)S(1)} %get-tuple-element.59.keep, bf16[4,8,64,128]{3,2,1,0:T(8,128)(2,1)S(1)} %collective-permute-done.7.refs_4_.got, ...), custom_call_target="tpu_custom_call" | custom-call | flops 16777216 | bytes 3145728 | tf_op jit(solution)/shard_map/finish/pallas_call | solution.py:538
  106.0 1.8 %route.6 = (bf16[4,8,64,128]{3,2,1,0:T(8,128)(2,1)S(1)}, bf16[4,8,64,128]{3,2,1,0:T(8,128)(2,1)S(1)}) custom-call(s32[66]{0:T(128)S(1)} %copy-done.15, bf16[2,8,64,128]{3,2,1,0:T(8,128)(2,1)S(1)} %get-tuple-element.55.refs_0_, bf16[2,8,64,128]{3,2,1,0:T(8,128)(2,1)S(1)} %collective-permute-done.11.refs_1_, ...), custom_call_target="tpu_custom_call" | custom-call | bytes 2097152 | tf_op jit(solution)/shard_map/route/pallas_call | solution.py:467
  109.5 2.2 %pack.6 = (bf16[2,8,64,128]{3,2,1,0:T(8,128)(2,1)S(1)}, bf16[2,8,64,128]{3,2,1,0:T(8,128)(2,1)S(1)}, bf16[2,8,64,128]{3,2,1,0:T(8,128)(2,1)S(1)}, bf16[2,8,64,128]{3,2,1,0:T(8,128)(2,1)S(1)}) custom-call(s32[66]{0:T(128)S(1)} %copy-done.15, f32[8,32,64,128]{3,2,1,0:T(8,128)} %refs_7_.7, f32[8,32,64,128]{3,2,1,0:T(8,128)} %refs_7_.7, ...), custom_call_target="tpu_custom_call" | custom-call | bytes 3145728 | tf_op jit(solution)/shard_map/pack/pallas_call | solution.py:433
  113.9 2.4 %finish.5 = (f32[1,1,4,64,64,128]{5,4,3,2,1,0:T(8,128)}, f32[8,128]{1,0:T(8,128)S(1)}) custom-call(s32[66]{0:T(128)S(1)} %copy-done.15, f32[256]{0:T(256)S(1)} %reshape_squeeze.3.decay, bf16[4,8,64,128]{3,2,1,0:T(8,128)(2,1)S(1)} %get-tuple-element.62.keep, ...), custom_call_target="tpu_custom_call", output_to_operand_aliasing={{0}: (12, {})} | custom-call | flops 16777216 | bytes 3145728 | tf_op jit(solution)/shard_map/finish/pallas_call | solution.py:538
  116.2 4.1 %collective-permute-done.10.refs_3_ = bf16[2,8,64,128]{3,2,1,0:T(8,128)(2,1)S(1)} collective-permute-done((bf16[2,8,64,128]{3,2,1,0:T(8,128)(2,1)S(1)}, bf16[2,8,64,128]{3,2,1,0:T(8,128)(2,1)S(1)}, u32[]{:S(2)}, u32[]{:S(2)}) %collective-permute-start.10) | collective-permute-done | bytes 262176 | tf_op jit(solution)/shard_map/ppermute | solution.py:640
  120.3 5.4 %collective-permute-done.9.refs_2_ = bf16[2,8,64,128]{3,2,1,0:T(8,128)(2,1)S(1)} collective-permute-done((bf16[2,8,64,128]{3,2,1,0:T(8,128)(2,1)S(1)}, bf16[2,8,64,128]{3,2,1,0:T(8,128)(2,1)S(1)}, u32[]{:S(2)}, u32[]{:S(2)}) %collective-permute-start.9) | collective-permute-done | bytes 262176 | tf_op jit(solution)/shard_map/ppermute | solution.py:640
  127.1 2.4 %windows.1 = f32[1,1,4,3,4,1280]{5,4,3,2,1,0:T(4,128)} custom-call(s32[66]{0:T(128)} %plan.1.table._rows, f32[4,1,12416]{2,1,0:T(1,128)} %get-tuple-element.39.refs_0_.refs_1_.refs_2_.refs_3_.own, f32[4,1,12416]{2,1,0:T(1,128)} %copy-done.3), custom_call_target="tpu_custom_call" | custom-call | tf_op jit(solution)/shard_map/windows/pallas_call | solution.py:406
  132.0 2.4 %finish.6 = (f32[1,1,4,64,64,128]{5,4,3,2,1,0:T(8,128)}, f32[8,128]{1,0:T(8,128)}) custom-call(s32[66]{0:T(128)S(1)} %copy-done.16, f32[256]{0:T(256)S(1)} %reshape_squeeze.3.decay, bf16[4,8,64,128]{3,2,1,0:T(8,128)(2,1)S(1)} %get-tuple-element.67.keep, ...), custom_call_target="tpu_custom_call", output_to_operand_aliasing={{0}: (12, {})} | custom-call | flops 16777216 | bytes 3145728 | tf_op jit(solution)/shard_map/finish/pallas_call | solution.py:538
  134.3 6.3 %collective-permute-done.16.got = bf16[4,8,64,128]{3,2,1,0:T(8,128)(2,1)S(1)} collective-permute-done((bf16[4,8,64,128]{3,2,1,0:T(8,128)(2,1)S(1)}, bf16[4,8,64,128]{3,2,1,0:T(8,128)(2,1)S(1)}, u32[]{:S(2)}, u32[]{:S(2)}) %collective-permute-start.16) | collective-permute-done | bytes 524320 | tf_op jit(solution)/shard_map/ppermute | solution.py:593
  140.6 2.4 %finish.7 = (f32[1,1,4,64,64,128]{5,4,3,2,1,0:T(8,128)}, f32[8,128]{1,0:T(8,128)}) custom-call(s32[66]{0:T(128)S(1)} %copy-done.16, f32[256]{0:T(256)S(1)} %reshape_squeeze.3.decay, bf16[4,8,64,128]{3,2,1,0:T(8,128)(2,1)S(1)} %get-tuple-element.65.keep, bf16[4,8,64,128]{3,2,1,0:T(8,128)(2,1)S(1)} %collective-permute-done.16.got, ...), custom_call_target="tpu_custom_call", output_to_operand_aliasing={{0}: (12, {})} | custom-call | flops 16777216 | bytes 3145728 | tf_op jit(solution)/shard_map/finish/pallas_call | solution.py:538
  (98 shorter events, 28.5 us)
Async XLA Ops:
  9.5 20.1 %copy-start.19 = (bf16[2,8,2,1280]{3,2,1,0:T(2,128)(2,1)S(1)}, bf16[2,8,2,1280]{3,2,1,0:T(2,128)(2,1)}, u32[]{:S(2)}) copy-start(bf16[2,8,2,1280]{3,2,1,0:T(2,128)(2,1)} %param.18) | copy-start | bytes 245764
  9.5 26.5 %copy-start.14 = (s32[66]{0:T(128)S(1)}, s32[66]{0:T(128)}, u32[]{:S(2)}) copy-start(s32[66]{0:T(128)} %plan.1.table._rows) | copy-start | bytes 796
  11.6 3.2 %collective-permute-start.4 = (bf16[2,8,64,128]{3,2,1,0:T(8,128)(2,1)S(1)}, bf16[2,8,64,128]{3,2,1,0:T(8,128)(2,1)S(1)}, u32[]{:S(2)}, u32[]{:S(2)}) collective-permute-start(bf16[2,8,64,128]{3,2,1,0:T(8,128)(2,1)S(1)} %get-tuple-element.46), channel_id=1, source_target_pairs={{0,4},{4,0},{8,12},{12,8},{1,5},{5,1},{9,13},{13,9},{2,6},{6,2},{1... | collective-permute-start | bytes 786440 | tf_op jit(solution)/shard_map/ppermute | solution.py:640
  12.2 9.7 %collective-permute-start.5 = (bf16[2,8,64,128]{3,2,1,0:T(8,128)(2,1)S(1)}, bf16[2,8,64,128]{3,2,1,0:T(8,128)(2,1)S(1)}, u32[]{:S(2)}, u32[]{:S(2)}) collective-permute-start(bf16[2,8,64,128]{3,2,1,0:T(8,128)(2,1)S(1)} %get-tuple-element.47), channel_id=1, source_target_pairs={{0,8},{4,12},{8,0},{12,4},{1,9},{5,13},{9,1},{13,5},{2,10},{6,14},... | collective-permute-start | bytes 786440 | tf_op jit(solution)/shard_map/ppermute | solution.py:640
  14.7 12.3 %collective-permute-start.6 = (bf16[2,8,64,128]{3,2,1,0:T(8,128)(2,1)S(1)}, bf16[2,8,64,128]{3,2,1,0:T(8,128)(2,1)S(1)}, u32[]{:S(2)}, u32[]{:S(2)}) collective-permute-start(bf16[2,8,64,128]{3,2,1,0:T(8,128)(2,1)S(1)} %get-tuple-element.48), channel_id=1, source_target_pairs={{0,12},{4,8},{8,4},{12,0},{1,13},{5,9},{9,5},{13,1},{2,14},{6,10},... | collective-permute-start | bytes 786440 | tf_op jit(solution)/shard_map/ppermute | solution.py:640
  27.8 48.5 %collective-permute-start.7 = (bf16[4,8,64,128]{3,2,1,0:T(8,128)(2,1)S(1)}, bf16[4,8,64,128]{3,2,1,0:T(8,128)(2,1)S(1)}, u32[]{:S(2)}, u32[]{:S(2)}) collective-permute-start(bf16[4,8,64,128]{3,2,1,0:T(8,128)(2,1)S(1)} %get-tuple-element.49.refs_8_), channel_id=1, source_target_pairs={{0,1},{1,0},{2,3},{3,2},{4,5},{5,4},{6,7},{7,6},{8,9},{9,8},{10,11... | collective-permute-start | bytes 1572872 | tf_op jit(solution)/shard_map/ppermute | solution.py:593
  32.7 8.5 %all-to-all-start = ((bf16[4,2,9472]{2,1,0:T(2,128)(2,1)}), bf16[4,2,9472]{2,1,0:T(2,128)(2,1)S(1)}, u32[]{:S(2)}, u32[]{:S(2)}) async-start(bf16[4,2,9472]{2,1,0:T(2,128)(2,1)} %tokens.1), calls=%async_computation | async-start | bytes 303104 | tf_op jit(solution)/shard_map/all_to_all | solution.py:596
  39.0 33.7 %collective-permute-start.1 = (bf16[2,8,64,128]{3,2,1,0:T(8,128)(2,1)}, bf16[2,8,64,128]{3,2,1,0:T(8,128)(2,1)S(1)}, u32[]{:S(2)}, u32[]{:S(2)}) collective-permute-start(bf16[2,8,64,128]{3,2,1,0:T(8,128)(2,1)} %get-tuple-element.42), channel_id=1, source_target_pairs={{0,4},{4,0},{8,12},{12,8},{1,5},{5,1},{9,13},{13,9},{2,6},{6,2},{1... | collective-permute-start | bytes 786440 | tf_op jit(solution)/shard_map/ppermute | solution.py:640
  39.4 34.4 %collective-permute-start.2 = (bf16[2,8,64,128]{3,2,1,0:T(8,128)(2,1)}, bf16[2,8,64,128]{3,2,1,0:T(8,128)(2,1)S(1)}, u32[]{:S(2)}, u32[]{:S(2)}) collective-permute-start(bf16[2,8,64,128]{3,2,1,0:T(8,128)(2,1)} %get-tuple-element.43), channel_id=1, source_target_pairs={{0,8},{4,12},{8,0},{12,4},{1,9},{5,13},{9,1},{13,5},{2,10},{6,14},... | collective-permute-start | bytes 786440 | tf_op jit(solution)/shard_map/ppermute | solution.py:640
  41.1 34.6 %collective-permute-start.3 = (bf16[2,8,64,128]{3,2,1,0:T(8,128)(2,1)S(1)}, bf16[2,8,64,128]{3,2,1,0:T(8,128)(2,1)S(1)}, u32[]{:S(2)}, u32[]{:S(2)}) collective-permute-start(bf16[2,8,64,128]{3,2,1,0:T(8,128)(2,1)S(1)} %get-tuple-element.44), channel_id=1, source_target_pairs={{0,12},{4,8},{8,4},{12,0},{1,13},{5,9},{9,5},{13,1},{2,14},{6,10},... | collective-permute-start | bytes 786440 | tf_op jit(solution)/shard_map/ppermute | solution.py:640
  50.5 31.0 %all-to-all-start.1 = ((f32[8,1,7296]{2,1,0:T(1,128)}), f32[8,1,7296]{2,1,0:T(1,128)}, u32[]{:S(2)}, u32[]{:S(2)}) async-start(f32[8,1,7296]{2,1,0:T(1,128)} %get-tuple-element.38), calls=%async_computation.2 | async-start | bytes 466944 | tf_op jit(solution)/shard_map/all_to_all | solution.py:596
  54.5 75.0 %reduce-scatter.2.cloned.1.call-start = ((), (), s32[]{:S(2)}) async-start(), calls=%async_computation.3 | async-start | bytes 655360 | tf_op jit(solution)/shard_map/reduce_scatter | solution.py:620
  69.4 33.3 %copy-start.15 = (s32[66]{0:T(128)S(1)}, s32[66]{0:T(128)}, u32[]{:S(2)}) copy-start(s32[66]{0:T(128)} %plan.1.table._rows) | copy-start | bytes 796
  72.4 33.6 %collective-permute-start.11 = (bf16[2,8,64,128]{3,2,1,0:T(8,128)(2,1)}, bf16[2,8,64,128]{3,2,1,0:T(8,128)(2,1)S(1)}, u32[]{:S(2)}, u32[]{:S(2)}) collective-permute-start(bf16[2,8,64,128]{3,2,1,0:T(8,128)(2,1)} %get-tuple-element.56), channel_id=1, source_target_pairs={{0,4},{4,0},{8,12},{12,8},{1,5},{5,1},{9,13},{13,9},{2,6},{6,2},{1... | collective-permute-start | bytes 786440 | tf_op jit(solution)/shard_map/ppermute | solution.py:640
  73.4 32.5 %collective-permute-start.12 = (bf16[2,8,64,128]{3,2,1,0:T(8,128)(2,1)}, bf16[2,8,64,128]{3,2,1,0:T(8,128)(2,1)}, u32[]{:S(2)}, u32[]{:S(2)}) collective-permute-start(bf16[2,8,64,128]{3,2,1,0:T(8,128)(2,1)} %get-tuple-element.57), channel_id=1, source_target_pairs={{0,8},{4,12},{8,0},{12,4},{1,9},{5,13},{9,1},{13,5},{2,10},{6,14},... | collective-permute-start | bytes 786440 | tf_op jit(solution)/shard_map/ppermute | solution.py:640
  74.5 31.5 %collective-permute-start.13 = (bf16[2,8,64,128]{3,2,1,0:T(8,128)(2,1)}, bf16[2,8,64,128]{3,2,1,0:T(8,128)(2,1)}, u32[]{:S(2)}, u32[]{:S(2)}) collective-permute-start(bf16[2,8,64,128]{3,2,1,0:T(8,128)(2,1)} %get-tuple-element.58), channel_id=1, source_target_pairs={{0,12},{4,8},{8,4},{12,0},{1,13},{5,9},{9,5},{13,1},{2,14},{6,10},... | collective-permute-start | bytes 786440 | tf_op jit(solution)/shard_map/ppermute | solution.py:640
  80.1 25.9 %collective-permute-start.14 = (bf16[4,8,64,128]{3,2,1,0:T(8,128)(2,1)S(1)}, bf16[4,8,64,128]{3,2,1,0:T(8,128)(2,1)S(1)}, u32[]{:S(2)}, u32[]{:S(2)}) collective-permute-start(bf16[4,8,64,128]{3,2,1,0:T(8,128)(2,1)S(1)} %get-tuple-element.50.refs_8_), channel_id=1, source_target_pairs={{0,1},{1,0},{2,3},{3,2},{4,5},{5,4},{6,7},{7,6},{8,9},{9,8},{10,11... | collective-permute-start | bytes 1572872 | tf_op jit(solution)/shard_map/ppermute | solution.py:593
  84.0 17.9 %collective-permute-start = (f32[4,1,12416]{2,1,0:T(1,128)}, f32[4,1,12416]{2,1,0:T(1,128)S(1)}, u32[]{:S(2)}, u32[]{:S(2)}) collective-permute-start(f32[4,1,12416]{2,1,0:T(1,128)} %get-tuple-element.40), channel_id=1, source_target_pairs={{0,1},{1,0},{2,3},{3,2},{4,5},{5,4},{6,7},{7,6},{8,9},{9,8},{10,11... | collective-permute-start | bytes 595976 | tf_op jit(solution)/shard_map/ppermute | solution.py:593
  107.8 17.9 %collective-permute-start.15 = (bf16[4,8,64,128]{3,2,1,0:T(8,128)(2,1)S(1)}, bf16[4,8,64,128]{3,2,1,0:T(8,128)(2,1)S(1)}, u32[]{:S(2)}, u32[]{:S(2)}) collective-permute-start(bf16[4,8,64,128]{3,2,1,0:T(8,128)(2,1)S(1)} %get-tuple-element.61), channel_id=1, source_target_pairs={{0,1},{1,0},{2,3},{3,2},{4,5},{5,4},{6,7},{7,6},{8,9},{9,8},{10,11... | collective-permute-start | bytes 1572872 | tf_op jit(solution)/shard_map/ppermute | solution.py:593
  111.6 19.4 %copy-start.2 = (f32[4,1,12416]{2,1,0:T(1,128)S(1)}, f32[4,1,12416]{2,1,0:T(1,128)}, u32[]{:S(2)}) copy-start(f32[4,1,12416]{2,1,0:T(1,128)} %get-tuple-element.39.refs_0_.refs_1_.refs_2_.refs_3_.own) | copy-start | bytes 595972
  111.6 8.7 %collective-permute-start.10 = (bf16[2,8,64,128]{3,2,1,0:T(8,128)(2,1)S(1)}, bf16[2,8,64,128]{3,2,1,0:T(8,128)(2,1)S(1)}, u32[]{:S(2)}, u32[]{:S(2)}) collective-permute-start(bf16[2,8,64,128]{3,2,1,0:T(8,128)(2,1)S(1)} %get-tuple-element.54), channel_id=1, source_target_pairs={{0,12},{4,8},{8,4},{12,0},{1,13},{5,9},{9,5},{13,1},{2,14},{6,10},... | collective-permute-start | bytes 786440 | tf_op jit(solution)/shard_map/ppermute | solution.py:640
  112.2 8.1 %collective-permute-start.8 = (bf16[2,8,64,128]{3,2,1,0:T(8,128)(2,1)S(1)}, bf16[2,8,64,128]{3,2,1,0:T(8,128)(2,1)S(1)}, u32[]{:S(2)}, u32[]{:S(2)}) collective-permute-start(bf16[2,8,64,128]{3,2,1,0:T(8,128)(2,1)S(1)} %get-tuple-element.52), channel_id=1, source_target_pairs={{0,4},{4,0},{8,12},{12,8},{1,5},{5,1},{9,13},{13,9},{2,6},{6,2},{1... | collective-permute-start | bytes 786440 | tf_op jit(solution)/shard_map/ppermute | solution.py:640
  113.0 12.7 %collective-permute-start.9 = (bf16[2,8,64,128]{3,2,1,0:T(8,128)(2,1)S(1)}, bf16[2,8,64,128]{3,2,1,0:T(8,128)(2,1)S(1)}, u32[]{:S(2)}, u32[]{:S(2)}) collective-permute-start(bf16[2,8,64,128]{3,2,1,0:T(8,128)(2,1)S(1)} %get-tuple-element.53), channel_id=1, source_target_pairs={{0,8},{4,12},{8,0},{12,4},{1,9},{5,13},{9,1},{13,5},{2,10},{6,14},... | collective-permute-start | bytes 786440 | tf_op jit(solution)/shard_map/ppermute | solution.py:640
  126.6 14.0 %collective-permute-start.16 = (bf16[4,8,64,128]{3,2,1,0:T(8,128)(2,1)S(1)}, bf16[4,8,64,128]{3,2,1,0:T(8,128)(2,1)S(1)}, u32[]{:S(2)}, u32[]{:S(2)}) collective-permute-start(bf16[4,8,64,128]{3,2,1,0:T(8,128)(2,1)S(1)} %get-tuple-element.66), channel_id=1, source_target_pairs={{0,1},{1,0},{2,3},{3,2},{4,5},{5,4},{6,7},{7,6},{8,9},{9,8},{10,11... | collective-permute-start | bytes 1572872 | tf_op jit(solution)/shard_map/ppermute | solution.py:593
  (22 other events, 101.0 us)
Sparse Core Ops, SparseCore 0:
  69.5 23.5 reduce-scatter.1

commit v3 on v2

--- a/solution.py
+++ b/solution.py
@@ -14,10 +14,21 @@
 R_PF = 8
 PER_GROUP = H // G
 X_WIDTH = PER_GROUP * P_SIZE
-CHUNKS = 4
-AHEAD = 2
+CHUNKS = ((0, 2), (2, 2), (4, 2), (6, 2))
+UNITS = 8
+NEAR = 2
+ROWS = 2 * R_PF
+PARTS = 4
 LANES = 128
 VMEM_LIMIT = 48 * 1024 * 1024
+SCALE = 1.0
+
+
+def cost(microseconds):
+    return pl.CostEstimate(
+        flops=0, bytes_accessed=int(SCALE * 3.2e6 * microseconds), transcendentals=0
+    )
+
 
 ANY = pl.BlockSpec(memory_space=pl.ANY)
 
@@ -39,7 +50,9 @@
         self.split_place = self.slot_place + R_PF
         self.live = self.split_place + R_PF
         self.parity = self.live + 1
-        self.slot_row = self.parity + 1
+        self.req = self.parity + 1
+        self.head = self.req + 1
+        self.slot_row = self.head + 1
         self.size = self.slot_row + self.rows
 
 
@@ -49,6 +62,8 @@
     half = R_PF // 2
     out[plan.live] = counts[me]
     out[plan.parity] = parity
+    out[plan.req] = me
+    out[plan.head] = lax.axis_index("head")
     for place in range(plan.places):
         out[plan.row_of + place] = 0
 
@@ -84,6 +99,8 @@
         in_specs=[smem, smem],
         out_specs=smem,
         out_shape=jax.ShapeDtypeStruct((plan.size,), jnp.int32),
+        compiler_params=pltpu.CompilerParams(vmem_limit_bytes=VMEM_LIMIT),
+        cost_estimate=cost(1.6),
         name="plan",
     )(request_slot, counts)
 
@@ -101,7 +118,8 @@
     return jnp.dot(matrix, values, preferred_element_type=jnp.float32)
 
 
-def tokens_kernel(plan, table, xbc, z, dt, out):
+def tokens_kernel(plan, table, xbc, z, dt, *refs):
+    out = refs[-1]
     steps, groups = xbc.shape[:2]
     matrix = one_hot(
         (plan.places, R_PF), [(table[plan.slot_place + slot], slot) for slot in range(R_PF)]
@@ -125,7 +143,7 @@
         at += LANES
 
 
-def pack_tokens(plan, table, xbc, z, dt):
+def pack_tokens(plan, table, xbc, z, dt, after):
     steps, groups = xbc.shape[:2]
     size = steps * (groups * xbc.shape[3] + z.shape[2] + LANES)
     return pl.pallas_call(
@@ -133,12 +151,14 @@
         grid_spec=pltpu.PrefetchScalarGridSpec(
             num_scalar_prefetch=1,
             grid=(1,),
-            in_specs=[whole(xbc), whole(z), whole(dt)],
+            in_specs=[whole(xbc), whole(z), whole(dt)] + [ANY] * len(after),
             out_specs=pl.BlockSpec((plan.places // plan.cap, plan.cap, size), lambda i, t: (0, 0, 0)),
         ),
         out_shape=jax.ShapeDtypeStruct((plan.places // plan.cap, plan.cap, size), jnp.bfloat16),
+        compiler_params=pltpu.CompilerParams(vmem_limit_bytes=VMEM_LIMIT),
+        cost_estimate=cost(1.4),
         name="tokens",
-    )(table, xbc, z, dt)
+    )(table, xbc, z, dt, *after)
 
 
 def whole(array):
@@ -149,20 +169,25 @@
     return value / (1.0 + jnp.exp(-value))
 
 
-def rows_kernel(plan, table, tokens, conv, weight, bias, small, gain, state, *refs):
-    normed, packet, read, read_taps, acts, wide, gates, lines = refs
+def packet_places(groups, conv_width):
+    taps_at = 2 * groups * X_WIDTH
+    last_at = taps_at + 2 * groups * N
+    decay_at = last_at + groups * conv_width
+    return taps_at, last_at, decay_at, decay_at + LANES
+
+
+def rows_kernel(plan, table, tokens, conv, weight, bias, small, gain, *refs):
+    states = refs[:PARTS]
+    out, read, read_taps, acts, wide, gates, lines = refs[-7:]
     steps = 2
     taps, groups, conv_width = weight.shape
-    heads = state.shape[1]
+    heads = states[0].shape[1] * PARTS
     channels = groups * X_WIDTH
     index = pl.program_id(0)
     row_ids = lax.broadcasted_iota(jnp.int32, (R_PF, 1), 0)
     live = row_ids < table[plan.live]
     f32, bf16 = jnp.float32, jnp.bfloat16
-    update_at = 0
-    taps_at = update_at + steps * channels
-    last_at = taps_at + steps * groups * N
-    decay_at = last_at + groups * conv_width
+    taps_at, last_at, decay_at, _ = packet_places(groups, conv_width)
 
     @pl.when(index == 0)
     def _():
@@ -219,9 +244,10 @@
         for part in range(5):
             wide[part] = spread[part * R_PF : (part + 1) * R_PF]
 
-    for group in range(groups):
-        rows = state[0, group * PER_GROUP : (group + 1) * PER_GROUP].reshape(X_WIDTH, N)
-        state_high, state_low = split_bf16(rows)
+    for part, state in enumerate(states):
+        size = heads // PARTS * P_SIZE
+        group, start = part * size // X_WIDTH, part * size % X_WIDTH
+        state_high, state_low = split_bf16(state[0].reshape(size, N))
         dims = (((1,), (1,)), ((), ()))
         total = lax.dot_general(read_taps[group], state_high, dims, preferred_element_type=f32)
         rest = lax.dot_general(
@@ -229,8 +255,9 @@
         )
         total = total[: steps * R_PF] + total[steps * R_PF :] + rest
         for step in range(steps):
-            part = total[step * R_PF : (step + 1) * R_PF]
-            read[group, step] = jnp.where(row_ids == index, part, read[group, step])
+            now = total[step * R_PF : (step + 1) * R_PF]
+            span = slice(start, start + size)
+            read[group, step, :, span] = jnp.where(row_ids == index, now, read[group, step, :, span])
 
     @pl.when(index == R_PF - 1)
     def _():
@@ -259,22 +286,36 @@
                 gated = y[step] * gates[step, :, span]
                 scale = lax.rsqrt(jnp.mean(gated * gated, axis=1, keepdims=True) + 1e-05)
                 result.append(gated * scale * gain[0:1, span])
-            normed[:, span] = jnp.concatenate(result, axis=0).astype(bf16)
+            together = jnp.concatenate(result, axis=0).astype(bf16)
+            for target in range(out.shape[0]):
+                out[target, :ROWS, span] = together
             lines[:, span] = later
             lines[:, channels + group * X_WIDTH : channels + (group + 1) * X_WIDTH] = u[1]
             for step in range(steps):
                 start = taps_at + (step * groups + group) * N
                 lines[:, start : start + N] = b[step]
+        segments = lines.shape[1] // channels
+        values = [lines[:, part * channels : (part + 1) * channels] for part in range(segments)]
+        high = [value.astype(bf16).astype(f32) for value in values]
+        low = [value - near for value, near in zip(values, high)]
+        pairs = []
         for row in range(R_PF):
-            packet[table[plan.row_place + row]] = lines[row : row + 1]
-
-
-def run_rows(plan, table, tokens, conv, weight, bias, small, gain, ssm_state):
+            place = table[plan.row_place + row]
+            first = place // plan.cap * ROWS + place % plan.cap * 2 * segments
+            pairs += [(first + part, part * R_PF + row) for part in range(2 * segments)]
+        matrix = one_hot((out.shape[0] * ROWS, 2 * segments * R_PF), pairs)
+        placed = pick(matrix, jnp.concatenate(high + low, axis=0).astype(bf16)).astype(bf16)
+        for target in range(out.shape[0]):
+            out[target, ROWS:] = placed[target * ROWS : (target + 1) * ROWS]
+
+
+def run_rows(plan, table, tokens, conv, weight, bias, small, gain, ssm_state, after):
     taps, groups, conv_width = weight.shape
     steps = 2
     heads = ssm_state.shape[1]
+    sources = plan.places // plan.cap
     channels = groups * X_WIDTH
-    size = steps * channels + steps * groups * N + groups * conv_width + LANES
+    size = -(-packet_places(groups, conv_width)[-1] // channels) * channels
     f32 = jnp.float32
     return pl.pallas_call(
         functools.partial(rows_kernel, plan),
@@ -288,12 +329,16 @@
                 whole(bias),
                 whole(small),
                 whole(gain),
-                pl.BlockSpec((1, heads, P_SIZE, N), lambda i, t: (i, 0, 0, 0)),
-            ],
-            out_specs=[
-                pl.BlockSpec((steps * R_PF, channels), lambda i, t: (0, 0)),
-                pl.BlockSpec((plan.places, 1, size), lambda i, t: (0, 0, 0)),
-            ],
+            ]
+            + [
+                pl.BlockSpec(
+                    (1, heads // PARTS, P_SIZE, N),
+                    functools.partial(lambda i, t, part: (i, part, 0, 0), part=part),
+                )
+                for part in range(PARTS)
+            ]
+            + [ANY] * len(after),
+            out_specs=pl.BlockSpec((sources, 2 * ROWS, channels), lambda i, t: (0, 0, 0)),
             scratch_shapes=[
                 pltpu.VMEM((groups, steps, R_PF, X_WIDTH), f32),
                 pltpu.VMEM((groups, 2 * steps * R_PF, N), jnp.bfloat16),
@@ -303,20 +348,18 @@
                 pltpu.VMEM((R_PF, size), f32),
             ],
         ),
-        out_shape=[
-            jax.ShapeDtypeStruct((steps * R_PF, channels), jnp.bfloat16),
-            jax.ShapeDtypeStruct((plan.places, 1, size), f32),
-        ],
+        out_shape=jax.ShapeDtypeStruct((sources, 2 * ROWS, channels), jnp.bfloat16),
         compiler_params=pltpu.CompilerParams(vmem_limit_bytes=VMEM_LIMIT),
-        cost_estimate=pl.CostEstimate(
-            flops=64 * ssm_state.size, bytes_accessed=4 * ssm_state.size, transcendentals=0
-        ),
+        cost_estimate=cost(9),
         name="rows",
-    )(table, tokens, conv, weight, bias, small, gain, ssm_state)
-
-
-def project_kernel(plan, share, table, normed, weight, out, picked):
+    )(table, tokens, conv, weight, bias, small, gain, *([ssm_state] * PARTS), *after)
+
+
+def project_kernel(plan, share, table, *refs):
     steps = 2
+    targets = plan.rows // share
+    normed, weights = refs[0], refs[1 : 1 + PARTS]
+    own, out, picked = refs[-3:]
 
     @pl.when(pl.program_id(0) == 0)
     def _():
@@ -326,7 +369,7 @@
 
         def add(slot, total):
             row = table[plan.slot_row + slot]
-            target = (slot // share) * steps * share + slot % share
+            target = slot // share * steps * share + slot % share
             source = (row // R_PF) * steps * R_PF + row % R_PF
             for step in range(steps):
                 hit = (rows == target + step * share) & (columns == source + step * R_PF)
@@ -334,70 +377,131 @@
             return total
 
         matrix = lax.fori_loop(0, plan.rows, add, jnp.zeros(shape, jnp.float32), unroll=8)
-        picked[...] = pick(matrix.astype(jnp.bfloat16), normed[...]).astype(jnp.bfloat16)
-
-    out[...] = pick(picked[...], weight[...])
-
-
-def project(plan, share, table, normed, weight):
-    rows, depth = normed.shape
+        matrix = matrix.astype(jnp.bfloat16)
+        values = normed[...].reshape(picked.shape)
+        picked[...] = pick(matrix, values).astype(jnp.bfloat16)
+
+    depth = weights[0].shape[0]
+    total = sum(
+        pick(picked[:, part * depth : (part + 1) * depth], weights[part][...])
+        for part in range(PARTS)
+    )
+    for target in range(targets):
+        part = total[target * steps * share : (target + 1) * steps * share]
+        out[target] = part.astype(out.dtype)
+
+        @pl.when(table[plan.head] == target)
+        def _():
+            own[...] = part
+
+
+def project(plan, share, table, normed, weight, after):
+    depth = weight.shape[0]
     columns = weight.shape[1]
     block = min(512, columns)
+    rows = 2 * share
+    targets = plan.rows // share
     return pl.pallas_call(
         functools.partial(project_kernel, plan, share),
         grid_spec=pltpu.PrefetchScalarGridSpec(
             num_scalar_prefetch=1,
             grid=(columns // block,),
-            in_specs=[whole(normed), pl.BlockSpec((depth, block), lambda i, t: (0, i))],
-            out_specs=pl.BlockSpec((rows, block), lambda i, t: (0, i)),
-            scratch_shapes=[pltpu.VMEM((rows, depth), jnp.bfloat16)],
+            in_specs=[pl.BlockSpec((normed.shape[0], ROWS, depth), lambda i, t: (0, 0, 0))]
+            + [
+                pl.BlockSpec(
+                    (depth // PARTS, block), functools.partial(lambda i, t, part: (part, i), part=part)
+                )
+                for part in range(PARTS)
+            ]
+            + [ANY] * len(after),
+            out_specs=[
+                pl.BlockSpec((rows, block), lambda i, t: (0, i)),
+                pl.BlockSpec((targets, rows, block), lambda i, t: (0, 0, i)),
+            ],
+            scratch_shapes=[pltpu.VMEM((2 * plan.rows, depth), jnp.bfloat16)],
         ),
-        out_shape=jax.ShapeDtypeStruct((rows, columns), jnp.float32),
+        out_shape=[
+            jax.ShapeDtypeStruct((rows, columns), jnp.float32),
+            jax.ShapeDtypeStruct((targets, rows, columns), jnp.bfloat16),
+        ],
         compiler_params=pltpu.CompilerParams(vmem_limit_bytes=VMEM_LIMIT),
-        cost_estimate=pl.CostEstimate(
-            flops=2 * rows * weight.size, bytes_accessed=2 * weight.size, transcendentals=0
-        ),
+        cost_estimate=cost(6),
         name="project",
-    )(table, normed, weight)
-
-
-def slots_kernel(plan, table, packet, tokens, own, other):
+    )(table, normed, *([weight] * PARTS), *after)
+
+
+def slots_kernel(plan, decay_at, table, packets, xbc, *refs):
+    own, other = refs[-2:]
+    f32, bf16 = jnp.float32, jnp.bfloat16
+    steps, groups = xbc.shape[:2]
     half = R_PF // 2
-    size = packet.shape[2]
+    sources, _, channels = packets.shape
+    segments = (own.shape[1] - LANES - steps * groups * xbc.shape[3]) // channels
+    pairs, order = [], []
     for local in range(R_PF):
-        target = own if local < half else other
         slot = (local + table[plan.parity] * half) % R_PF
-        target[local % half, :, :size] = packet[table[plan.slot_place + slot]]
-        target[local % half, :, size:] = tokens[slot]
-
-
-def split_slots(plan, table, packet, tokens):
-    shape = (R_PF // 2, 1, packet.shape[2] + tokens.shape[2])
-    out = jax.ShapeDtypeStruct(shape, jnp.float32)
+        order.append((local, slot))
+        place = table[plan.slot_place + slot]
+        first = place // plan.cap * ROWS + place % plan.cap * 2 * segments
+        pairs += [(part * R_PF + local, first + part) for part in range(2 * segments)]
+    matrix = one_hot((2 * segments * R_PF, sources * ROWS), pairs)
+    order = one_hot((R_PF, R_PF), order)
+
+    def put(values, start):
+        size = values.shape[1]
+        own[:, start : start + size] = values[:half].astype(bf16)
+        other[:, start : start + size] = values[half:].astype(bf16)
+
+    picked = pick(matrix, packets[...].reshape(sources * ROWS, channels))
+    for part in range(segments):
+        high = picked[part * R_PF : (part + 1) * R_PF]
+        low = picked[(segments + part) * R_PF : (segments + part + 1) * R_PF]
+        put(high + low, part * channels)
+        if decay_at // channels == part:
+            span = slice(decay_at % channels, decay_at % channels + LANES)
+            put(low[:, span], segments * channels)
+    at = segments * channels + LANES
+    for step in range(steps):
+        for group in range(groups):
+            put(pick(order, xbc[step, group]), at)
+            at += xbc.shape[3]
+
+
+def split_slots(plan, table, packets, xbc, after):
+    steps, groups, _, conv_width = xbc.shape
+    sources, _, channels = packets.shape
+    decay_at, end = packet_places(groups, conv_width)[2:]
+    size = -(-end // channels) * channels + LANES + steps * groups * conv_width
+    out = jax.ShapeDtypeStruct((R_PF // 2, size), jnp.bfloat16)
     return pl.pallas_call(
-        functools.partial(slots_kernel, plan),
+        functools.partial(slots_kernel, plan, decay_at),
         grid_spec=pltpu.PrefetchScalarGridSpec(
             num_scalar_prefetch=1,
             grid=(1,),
-            in_specs=[whole(packet), whole(tokens)],
+            in_specs=[
+                pl.BlockSpec((sources, ROWS, channels), lambda i, t: (0, 1, 0)),
+                whole(xbc),
+            ]
+            + [ANY] * len(after),
             out_specs=[whole(out)] * 2,
         ),
         out_shape=[out, out],
+        compiler_params=pltpu.CompilerParams(vmem_limit_bytes=VMEM_LIMIT),
+        cost_estimate=cost(1),
         name="slots",
-    )(table, packet, tokens)
+    )(table, packets, xbc, *after)
 
 
 def windows_kernel(plan, groups, conv_width, starts, table, own, got, out):
     parity = table[plan.parity]
     for owner, packet in enumerate((own, got)):
         side = jnp.where(parity == owner, 0, groups)
-        for slot in range(R_PF // 2):
-            for row, start in enumerate(starts):
-                for group in range(groups):
-                    first = start + group * conv_width
-                    out[0, 0, slot, row, pl.ds(side + group, 1)] = packet[
-                        slot, :, first : first + conv_width
-                    ]
+        for row, start in enumerate(starts):
+            for group in range(groups):
+                first = start + group * conv_width
+                values = packet[:, first : first + conv_width].astype(jnp.float32)
+                for slot in range(R_PF // 2):
+                    out[0, 0, slot, row, pl.ds(side + group, 1)] = values[slot : slot + 1]
 
 
 def write_windows(plan, table, own, got, groups, conv_width, starts):
@@ -412,39 +516,47 @@
             out_specs=whole(out),
         ),
         out_shape=out,
+        compiler_params=pltpu.CompilerParams(vmem_limit_bytes=VMEM_LIMIT),
+        cost_estimate=cost(1.3),
         name="windows",
     )(table, own, got)
 
 
-def pack_kernel(count, cap, _rows, *refs):
+def pack_kernel(count, cap, _table, *refs):
     inputs, outputs = refs[:count], refs[-(count // cap) :]
     for place in range(count):
         outputs[place // cap][place % cap] = inputs[place][0].astype(jnp.bfloat16)
 
 
-def pack_chunk(plan, table, ssm_state, chunk, width, after):
-    count, cap = plan.places, plan.cap
-    block = (1, width, P_SIZE, N)
+def pack_rows(plan, table, ssm_state, shifts, first, width, cuts, after):
+    cap = plan.cap
+    places = [shift * cap + rank for shift in shifts for rank in range(cap)]
+    piece = width // cuts
+    start = first // piece
     specs = [
-        pl.BlockSpec(block, functools.partial(lambda i, rows, p: (rows[plan.row_of + p], chunk, 0, 0), p=p))
-        for p in range(count)
+        pl.BlockSpec(
+            (1, piece, P_SIZE, N),
+            functools.partial(
+                lambda i, rows, place: (rows[plan.row_of + place], start + i, 0, 0), place=place
+            ),
+        )
+        for place in places
     ]
-    shape = (cap, width, P_SIZE, N)
+    out = jax.ShapeDtypeStruct((cap, width, P_SIZE, N), jnp.bfloat16)
     return pl.pallas_call(
-        functools.partial(pack_kernel, count, cap),
+        functools.partial(pack_kernel, len(places), cap),
         grid_spec=pltpu.PrefetchScalarGridSpec(
             num_scalar_prefetch=1,
-            grid=(1,),
+            grid=(cuts,),
             in_specs=specs + [ANY] * len(after),
-            out_specs=[pl.BlockSpec(shape, lambda i, rows: (0, 0, 0, 0))] * (count // cap),
+            out_specs=[pl.BlockSpec((cap, piece, P_SIZE, N), lambda i, rows: (0, i, 0, 0))]
+            * len(shifts),
         ),
-        out_shape=[jax.ShapeDtypeStruct(shape, jnp.bfloat16)] * (count // cap),
+        out_shape=[out] * len(shifts),
         compiler_params=pltpu.CompilerParams(vmem_limit_bytes=VMEM_LIMIT),
-        cost_estimate=pl.CostEstimate(
-            flops=0, bytes_accessed=6 * count * width * P_SIZE * N, transcendentals=0
-        ),
-        name="pack",
-    )(table, *([ssm_state] * count), *after)
+        cost_estimate=cost(2.5),
+        name=f"pack_{first}_{width}",
+    )(table, *([ssm_state] * len(places)), *after)
 
 
 def route_kernel(plan, sources, table, *refs):
@@ -461,24 +573,24 @@
                 target[index % half] = arrived[source][place % cap]
 
 
-def route_chunk(plan, table, arrived, half, after):
-    shape = (half,) + arrived[0].shape[1:]
-    out = jax.ShapeDtypeStruct(shape, jnp.bfloat16)
+def route_chunk(plan, table, near, far, first, after):
+    width = far[0].shape[1]
+    half = R_PF // 2
+    out = jax.ShapeDtypeStruct((half, width, P_SIZE, N), jnp.bfloat16)
+    block = pl.BlockSpec((plan.cap, width, P_SIZE, N), lambda i, rows: (0, first // width - 1, 0, 0))
     return pl.pallas_call(
-        functools.partial(route_kernel, plan, len(arrived)),
+        functools.partial(route_kernel, plan, len(near) + len(far)),
         grid_spec=pltpu.PrefetchScalarGridSpec(
             num_scalar_prefetch=1,
             grid=(1,),
-            in_specs=[whole(one) for one in arrived] + [ANY] * len(after),
+            in_specs=[block] * len(near) + [whole(one) for one in far] + [ANY] * len(after),
             out_specs=[whole(out)] * 2,
         ),
         out_shape=[out, out],
         compiler_params=pltpu.CompilerParams(vmem_limit_bytes=VMEM_LIMIT),
-        cost_estimate=pl.CostEstimate(
-            flops=0, bytes_accessed=8 * half * arrived[0][0].size, transcendentals=0
-        ),
-        name="route",
-    )(table, *arrived, *after)
+        cost_estimate=cost(1),
+        name=f"route_{first}_{width}",
+    )(table, *near, *far, *after)
 
 
 def finish_kernel(plan, width, heads, base, table, decay, keep, got, *refs):
@@ -487,20 +599,20 @@
     slots = keep.shape[0]
     done[...] = jnp.zeros_like(done)
 
-    def stack(first, second, slot):
-        rows = jnp.concatenate([first[slot], second[slot]], axis=0)
-        high = rows.astype(jnp.bfloat16).astype(jnp.float32)
-        return high, rows - high
-
-    def fill(source, first_update, second_update, first_taps, second_taps):
+    def fill(source, *pieces):
+        first_update, second_update, first_taps, second_taps = [
+            piece[...].astype(jnp.float32) for piece in pieces
+        ]
+
+        def stack(first, second, slot):
+            blank = jnp.zeros((6, first.shape[1]), jnp.float32)
+            rows = [first[slot : slot + 1], second[slot : slot + 1], blank]
+            return jnp.concatenate(rows, axis=0).astype(jnp.bfloat16)
+
         for slot in range(slots):
-            update_high, update_low = stack(first_update, second_update, slot)
-            taps_high, taps_low = stack(first_taps, second_taps, slot)
-            updates = jnp.concatenate([update_high, update_low, update_high, update_low], axis=0)
-            taps = jnp.concatenate([taps_high, taps_high, taps_low, taps_low], axis=0)
             added = lax.dot_general(
-                updates.astype(jnp.bfloat16),
-                taps.astype(jnp.bfloat16),
+                stack(first_update, second_update, slot),
+                stack(first_taps, second_taps, slot),
                 (((0,), (0,)), ((), ())),
                 preferred_element_type=jnp.float32,
             ).reshape(width, P_SIZE, N)
@@ -514,19 +626,20 @@
     pl.when(owner == 1)(lambda: fill(got, *parts[4:]))
 
 
-def finish_chunk(plan, table, so_far, keep, got, decay, own, other, chunk, heads):
+def finish_chunk(plan, table, so_far, keep, got, decay, own, other, first, heads):
     slots, width = keep.shape[:2]
     per_half = heads // width
     span = width * P_SIZE
     channels = heads * P_SIZE
     groups = heads // PER_GROUP
-    group = chunk * width // PER_GROUP
+    group = first // PER_GROUP
+    chunk = first // width
     taps_at = 2 * channels // N
     out_shape = jax.ShapeDtypeStruct((1, 1, slots, 2 * heads, P_SIZE, N), jnp.float32)
     extra = [] if so_far is None else [so_far]
 
     def part(size, place):
-        return pl.BlockSpec((slots, 1, size), lambda o, t, d: (0, 0, place))
+        return pl.BlockSpec((slots, size), lambda o, t, d: (0, place))
 
     parts = [
         part(span, chunk),
@@ -536,7 +649,7 @@
     ]
     side = lambda o, t: (o + t[plan.parity]) % 2
     return pl.pallas_call(
-        functools.partial(finish_kernel, plan, width, heads, chunk * width),
+        functools.partial(finish_kernel, plan, width, heads, first),
         grid_spec=pltpu.PrefetchScalarGridSpec(
             num_scalar_prefetch=2,
             grid=(2,),
@@ -552,12 +665,8 @@
         out_shape=[out_shape, jax.ShapeDtypeStruct((8, 128), jnp.float32)],
         input_output_aliases={12: 0} if extra else {},
         compiler_params=pltpu.CompilerParams(vmem_limit_bytes=VMEM_LIMIT),
-        cost_estimate=pl.CostEstimate(
-            flops=64 * slots * width * P_SIZE * N,
-            bytes_accessed=12 * slots * width * P_SIZE * N,
-            transcendentals=0,
-        ),
-        name="finish",
+        cost_estimate=cost(2.4),
+        name=f"finish_{first}_{width}",
     )(table, decay, keep, got, *([own] * 4), *([other] * 4), *extra)
 
 
@@ -581,27 +690,55 @@
     req_count = lax.axis_size("req")
     head_count = lax.axis_size("head")
     plan = Plan(req_count)
-    slot_dev = R_PF // 2
     steps = token_xbc.shape[0]
     heads = ssm_state.shape[1]
     groups = conv_state.shape[2]
     conv_width = conv_state.shape[3]
-    width = heads // CHUNKS
     channels = groups * X_WIDTH
 
+    def shifted(value, axis, shift):
+        return lax.ppermute(value, axis, [(i, i ^ shift) for i in range(lax.axis_size(axis))])
+
     def swap(value):
-        return lax.ppermute(value, "head", [(i, i ^ 1) for i in range(head_count)])
-
-    def exchange(value):
-        return lax.all_to_all(value, "req", split_axis=0, concat_axis=0, tiled=True)
+        return shifted(value, "head", 1)
+
+    def exchange(value, axis):
+        return lax.all_to_all(value, axis, split_axis=0, concat_axis=0, tiled=True)
 
     table = make_plan(plan, request_slot, counts)
 
-    tokens = exchange(
-        pack_tokens(plan, table, jnp.swapaxes(token_xbc, 1, 2), token_z, token_dt)
+    unit = heads // UNITS
+    count = len(CHUNKS)
+    firsts = [start * unit for start, _ in CHUNKS]
+    far, sent = [None] * count, [None] * count
+    keeps, gives, gots = [None] * count, [None] * count, [None] * count
+
+    def send(chunk, shifts, after):
+        width = CHUNKS[chunk][1] * unit
+        packed = pack_rows(plan, table, ssm_state, shifts, firsts[chunk], width, 2, after)
+        sent[chunk] = packed[0]
+        return [shifted(part, "req", shift) if shift else part for part, shift in zip(packed, shifts)]
+
+    def route(chunk, near, far, after):
+        keeps[chunk], gives[chunk] = route_chunk(plan, table, near, far, firsts[chunk], after)
+        gots[chunk] = swap(gives[chunk])
+
+    xbc = jnp.swapaxes(token_xbc, 1, 2)
+    all_shifts, far_shifts = range(req_count), range(NEAR, req_count)
+    far[0] = send(0, all_shifts, [])
+    packed_tokens = pack_tokens(plan, table, xbc, token_z, token_dt, [sent[0]])
+    tokens = exchange(packed_tokens, "req")
+    far[1] = send(1, far_shifts, [packed_tokens])
+    route(0, [], far[0], [sent[1], tokens])
+    rest = UNITS - CHUNKS[0][1]
+    near = pack_rows(
+        plan, table, ssm_state, range(NEAR), CHUNKS[0][1] * unit, rest * unit, 3, [gives[0]]
     )
+    far[2] = send(2, far_shifts, [gives[0]])
+    near = [near[0]] + [shifted(near[shift], "req", shift) for shift in range(1, NEAR)]
+
     small = jnp.stack([a_log, dt_bias, d_skip]).astype(f32)
-    normed, packet = run_rows(
+    result = run_rows(
         plan,
         table,
         tokens,
@@ -611,42 +748,37 @@
         small,
         norm_gain.astype(f32)[None],
         ssm_state,
+        [gives[0]],
     )
+    route(1, near, far[1], [result, sent[2], gots[0]])
+    far[3] = send(3, far_shifts, [gives[1]])
+    result = exchange(result, "req")
+    route(2, near, far[2], [sent[3], result, gots[1]])
 
     share = plan.rows // head_count
-    projected = project(
-        plan, share, table, lax.all_gather(normed, "req", axis=0, tiled=True), out_weight
-    ).reshape(head_count, -1, out_weight.shape[1])
-    layer_out = lax.psum_scatter(projected, "head", scatter_dimension=0, tiled=True)
+    own_sum, sums = project(plan, share, table, result, out_weight, [gives[2]])
+    others = exchange(sums, "head").astype(f32)
+    is_mine = jnp.arange(head_count) == lax.axis_index("head")
+    layer_out = own_sum + jnp.sum(jnp.where(is_mine[:, None, None], 0.0, others), axis=0)
     layer_out = layer_out.astype(jnp.bfloat16).reshape(steps, share, -1)
 
-    local_tokens = jnp.swapaxes(token_xbc, 0, 1).reshape(R_PF, 1, -1).astype(f32)
-    own, other = split_slots(plan, table, exchange(packet), local_tokens)
-    other = swap(other)
-    taps_at = steps * channels
-    last_at = taps_at + steps * groups * N
-    decay_at = last_at + groups * conv_width
-    fresh_at = decay_at + LANES
+    own, give = split_slots(plan, table, result, xbc, [gives[2]])
+    other = swap(give)
+    _, last_at, decay_at, end = packet_places(groups, conv_width)
+    low_at = -(-end // channels) * channels
+    fresh_at = low_at + LANES
     starts = [last_at] + [fresh_at + step * groups * conv_width for step in range(steps)]
     out_conv = write_windows(plan, table, own, other, groups, conv_width, starts)
-    decay = jnp.stack([own, other])[:, :, 0, decay_at : decay_at + heads].reshape(-1)
-
-    gives, gots, dones, out_ssm = [], [], [], None
-    for chunk in range(CHUNKS):
-        packed = pack_chunk(plan, table, ssm_state, chunk, width, gives[: chunk - AHEAD + 1][-1:])
-        arrived = [packed[0]]
-        for shift in range(1, req_count):
-            pairs = [(i, i ^ shift) for i in range(req_count)]
-            arrived.append(lax.ppermute(packed[shift], "req", pairs))
-        keep, give = route_chunk(
-            plan, table, arrived, slot_dev, gots[-1:] + dones[: chunk - 1][-1:]
+    both = jnp.stack([own, other]).astype(f32)
+    decay = both[:, :, decay_at : decay_at + heads] + both[:, :, low_at : low_at + heads]
+    decay = decay.reshape(-1)
+    route(3, near, far[3], [gots[2], sums, give])
+
+    out_ssm = None
+    for chunk in range(count):
+        out_ssm, done = finish_chunk(
+            plan, table, out_ssm, keeps[chunk], gots[chunk], decay, own, other, firsts[chunk], heads
         )
-        gives.append(give)
-        gots.append(swap(give))
-        out_ssm, done = finish_chunk(
-            plan, table, out_ssm, keep, gots[-1], decay, own, other, chunk, heads
-        )
-        dones.append(done)
     return (layer_out, out_ssm, out_conv)
 
 

time: 151 us -> 126 us (0.83)
  between operations: 14.4 us -> 1.03 us
  waiting for transfers between devices: 44.2 us -> 34.9 us
  blocking collectives: 7.88 us -> 0 us
  local copies, waits for them, and re-layouts: 9.19 us -> 15.5 us
  starting transfers between devices: 22.7 us -> 24.8 us
  Pallas kernels: 49.2 us -> 47.4 us
    ppermute x17 -> x15, waiting for transfers between devices: 44.2 us -> 27.6 us  [shifted(): lax.ppermute(value, axis, [(i, i ^ shift) for i in range(lax.axis_size(ax...]
    all_gather x1 -> x0, blocking collectives: 7.88 us -> none  [on_device(): lax.all_gather(normed, 'req', axis=0, tiled=True)]
    all_to_all x2 -> x3, waiting for transfers between devices: 0.01 us -> 7.29 us  [exchange(): return lax.all_to_all(value, axis, split_axis=0, concat_axis=0, tiled=True)]
    unnamed x54 -> x68, local copies, waits for them, and re-layouts: 8.18 us -> 15.4 us
    all_to_all x2 -> x3, starting transfers between devices: 7.36 us -> 10.8 us  [exchange(): return lax.all_to_all(value, axis, split_axis=0, concat_axis=0, tiled=True)]
    ppermute x17 -> x15, starting transfers between devices: 15.3 us -> 14 us  [shifted(): lax.ppermute(value, axis, [(i, i ^ shift) for i in range(lax.axis_size(ax...]
    pallas_call x13 -> x14, Pallas kernels: 26.5 us -> 26.8 us  [the longest x5 11.5 us: pack_rows(): pl.pallas_call(functools.partial(pack_kernel, len(places), cap), grid_spe...]
  transfers between devices with their start and end apart: 20 -> 18, of which waited for: 6 -> 5; matrix products, arithmetic and copies ran while one was open for 3% -> 1% of each run, Pallas kernels for 28% -> 28%
where the time goes in v3:
time: 126 us; the launch traced here: 125 us
  Pallas kernels  47.4 us (38%)
  waiting for transfers between devices  34.9 us (28%)
  starting transfers between devices  24.8 us (20%)
  local copies, waits for them, and re-layouts  15.5 us (12%)
  other arithmetic  1.75 us (1%)
    ppermute x15, waiting for transfers between devices, shifted(): lax.ppermute(value, axis, [(i, i ^ shift) for i in range(lax.axis_size(ax...  27.6 us
    unnamed x68, local copies, waits for them, and re-layouts  15.4 us
    ppermute x15, starting transfers between devices, shifted(): lax.ppermute(value, axis, [(i, i ^ shift) for i in range(lax.axis_size(ax...  14 us
    pallas_call x5, Pallas kernels, pack_rows(): pl.pallas_call(functools.partial(pack_kernel, len(places), cap), grid_spe...  11.5 us
    all_to_all x3, starting transfers between devices, exchange(): return lax.all_to_all(value, axis, split_axis=0, concat_axis=0, tiled=True)  10.8 us
    pallas_call x1, Pallas kernels, run_rows(): pl.pallas_call(functools.partial(rows_kernel, plan), grid_spec=pltpu.Pref...  9.54 us
    pallas_call x4, Pallas kernels, finish_chunk(): pl.pallas_call(functools.partial(finish_kernel, plan, width, heads, first...  9.16 us
    all_to_all x3, waiting for transfers between devices, exchange(): return lax.all_to_all(value, axis, split_axis=0, concat_axis=0, tiled=True)  7.29 us
  transfers between devices with their start and end apart: 18, of which 5 were waited for; matrix products, arithmetic and copies ran while one was open for 1% of the time, Pallas kernels for 28%

profile of v3, /device:TPU:0, one launch (start us, length us, event | category | flops | bytes accessed | tf_op | source)
XLA Modules:
  0.0 125.4 jit_solution(12826122644218706630)
XLA Ops:
  3.6 2.4 %pack_0_8.1 = (bf16[2,8,64,128]{3,2,1,0:T(8,128)(2,1)S(1)}, bf16[2,8,64,128]{3,2,1,0:T(8,128)(2,1)S(1)}, bf16[2,8,64,128]{3,2,1,0:T(8,128)(2,1)S(1)}, bf16[2,8,64,128]{3,2,1,0:T(8,128)(2,1)S(1)}) custom-call(s32[68]{0:T(128)S(1)} %plan.1._table.table, f32[8,32,64,128]{3,2,1,0:T(8,128)} %refs_3_.12, f32[8,32,64,128]{3,2,1,0:T(8,128)} %refs_3_.12, ...), custom_call_target="tpu_custom_call" | custom-call | bytes 8000000 | tf_op jit(solution)/shard_map/pack_0_8/pallas_call | solution.py:546
  6.5 2.6 %collective-permute-start.1 = (bf16[2,8,64,128]{3,2,1,0:T(8,128)(2,1)S(1)}, bf16[2,8,64,128]{3,2,1,0:T(8,128)(2,1)S(1)}, u32[]{:S(2)}, u32[]{:S(2)}) collective-permute-start(bf16[2,8,64,128]{3,2,1,0:T(8,128)(2,1)S(1)} %get-tuple-element.33), channel_id=1, source_target_pairs={{0,8},{4,12},{8,0},{12,4},{1,9},{5,13},{9,1},{13,5},{2,10},{6,14},... | collective-permute-start | bytes 786440 | tf_op jit(solution)/shard_map/ppermute | solution.py:700
  10.7 3.3 %all-to-all-start = ((bf16[4,2,9472]{2,1,0:T(2,128)(2,1)}), bf16[4,2,9472]{2,1,0:T(2,128)(2,1)S(1)}, u32[]{:S(2)}, u32[]{:S(2)}) async-start(bf16[4,2,9472]{2,1,0:T(2,128)(2,1)} %tokens.1.refs_4_), calls=%async_computation | async-start | bytes 303104 | tf_op jit(solution)/shard_map/all_to_all | solution.py:706
  14.0 2.0 %pack_8_8.1 = (bf16[2,8,64,128]{3,2,1,0:T(8,128)(2,1)S(1)}, bf16[2,8,64,128]{3,2,1,0:T(8,128)(2,1)S(1)}) custom-call(s32[68]{0:T(128)S(1)} %plan.1._table.table, f32[8,32,64,128]{3,2,1,0:T(8,128)} %refs_3_.12, f32[8,32,64,128]{3,2,1,0:T(8,128)} %refs_3_.12, f32[8,32,64,128]{3,2,1,0:T(8,128)} %refs_3_.12, f32[8,32,64,128]{3,2,1,0:T(8,128)} %refs_3_.12, ...), custom_call_target="tpu_custom_call" | custom-call | bytes 8000000 | tf_op jit(solution)/shard_map/pack_8_8/pallas_call | solution.py:546
  16.0 7.3 %all-to-all-done.refs_5_.tokens = bf16[4,2,9472]{2,1,0:T(2,128)(2,1)S(1)} async-done(((bf16[4,2,9472]{2,1,0:T(2,128)(2,1)}), bf16[4,2,9472]{2,1,0:T(2,128)(2,1)S(1)}, u32[]{:S(2)}, u32[]{:S(2)}) %all-to-all-start) | async-done | bytes 151584 | tf_op jit(solution)/shard_map/all_to_all | solution.py:706
  24.9 3.2 %pack_8_24.1 = (bf16[2,24,64,128]{3,2,1,0:T(8,128)(2,1)S(1)}, bf16[2,24,64,128]{3,2,1,0:T(8,128)(2,1)S(1)}) custom-call(s32[68]{0:T(128)S(1)} %plan.1._table.table, f32[8,32,64,128]{3,2,1,0:T(8,128)} %refs_3_.12, f32[8,32,64,128]{3,2,1,0:T(8,128)} %refs_3_.12, f32[8,32,64,128]{3,2,1,0:T(8,128)} %refs_3_.12, f32[8,32,64,128]{3,2,1,0:T(8,128)} %refs_3_.12, ...), custom_call_target="tpu_custom_call" | custom-call | bytes 8000000 | tf_op jit(solution)/shard_map/pack_8_24/pallas_call | solution.py:546
  28.3 1.9 %collective-permute-start.8 = (bf16[4,8,64,128]{3,2,1,0:T(8,128)(2,1)S(1)}, bf16[4,8,64,128]{3,2,1,0:T(8,128)(2,1)S(1)}, u32[]{:S(2)}, u32[]{:S(2)}) collective-permute-start(bf16[4,8,64,128]{3,2,1,0:T(8,128)(2,1)S(1)} %get-tuple-element.36.refs_4_), channel_id=1, source_target_pairs={{0,1},{1,0},{2,3},{3,2},{4,5},{5,4},{6,7},{7,6},{8,9},{9,8},{10,11... | collective-permute-start | bytes 1572872 | tf_op jit(solution)/shard_map/ppermute | solution.py:700
  31.8 2.0 %pack_16_8.1 = (bf16[2,8,64,128]{3,2,1,0:T(8,128)(2,1)S(1)}, bf16[2,8,64,128]{3,2,1,0:T(8,128)(2,1)S(1)}) custom-call(s32[68]{0:T(128)S(1)} %plan.1._table.table, f32[8,32,64,128]{3,2,1,0:T(8,128)} %refs_3_.12, f32[8,32,64,128]{3,2,1,0:T(8,128)} %refs_3_.12, f32[8,32,64,128]{3,2,1,0:T(8,128)} %refs_3_.12, f32[8,32,64,128]{3,2,1,0:T(8,128)} %refs_3_.12, ...), custom_call_target="tpu_custom_call" | custom-call | bytes 8000000 | tf_op jit(solution)/shard_map/pack_16_8/pallas_call | solution.py:546
  34.5 9.5 %rows.1.refs_4_ = bf16[4,32,2048]{2,1,0:T(8,128)(2,1)} custom-call(s32[68]{0:T(128)S(1)} %plan.1._table.table, bf16[4,2,9472]{2,1,0:T(2,128)(2,1)S(1)} %all-to-all-done.refs_5_.tokens, f32[3,2,8,1280]{3,2,1,0:T(8,128)S(1)} %bitcast.16, bf16[4,2,1280]{2,1,0:T(2,128)(2,1)S(1)} %copy-done.20, bf16[2,1280]{1,0:T(2,128)(2,1)S(1)} %copy-done.21, ...), custom_call_target="tpu_custom_call" | custom-call | bytes 28800000 | tf_op jit(solution)/shard_map/rows/pallas_call | solution.py:320
  46.2 3.5 %all-to-all-start.1 = ((bf16[4,32,2048]{2,1,0:T(8,128)(2,1)}), bf16[4,32,2048]{2,1,0:T(8,128)(2,1)S(1)}, u32[]{:S(2)}, u32[]{:S(2)}) async-start(bf16[4,32,2048]{2,1,0:T(8,128)(2,1)} %rows.1.refs_4_), calls=%async_computation.1 | async-start | bytes 1048576 | tf_op jit(solution)/shard_map/all_to_all | solution.py:706
  49.7 2.0 %collective-permute-start.4 = (bf16[2,8,64,128]{3,2,1,0:T(8,128)(2,1)}, bf16[2,8,64,128]{3,2,1,0:T(8,128)(2,1)S(1)}, u32[]{:S(2)}, u32[]{:S(2)}) collective-permute-start(bf16[2,8,64,128]{3,2,1,0:T(8,128)(2,1)} %copy-done.12), channel_id=1, source_target_pairs={{0,8},{4,12},{8,0},{12,4},{1,9},{5,13},{9,1},{13,5},{2,10},{6,14},... | collective-permute-start | bytes 786440 | tf_op jit(solution)/shard_map/ppermute | solution.py:700
  51.7 1.9 %pack_24_8.1 = (bf16[2,8,64,128]{3,2,1,0:T(8,128)(2,1)S(1)}, bf16[2,8,64,128]{3,2,1,0:T(8,128)(2,1)S(1)}) custom-call(s32[68]{0:T(128)S(1)} %plan.1._table.table, f32[8,32,64,128]{3,2,1,0:T(8,128)} %refs_3_.12, f32[8,32,64,128]{3,2,1,0:T(8,128)} %refs_3_.12, f32[8,32,64,128]{3,2,1,0:T(8,128)} %refs_3_.12, f32[8,32,64,128]{3,2,1,0:T(8,128)} %refs_3_.12, ...), custom_call_target="tpu_custom_call" | custom-call | bytes 8000000 | tf_op jit(solution)/shard_map/pack_24_8/pallas_call | solution.py:546
  55.1 9.5 %collective-permute-done.4.refs_2_ = bf16[2,8,64,128]{3,2,1,0:T(8,128)(2,1)S(1)} collective-permute-done((bf16[2,8,64,128]{3,2,1,0:T(8,128)(2,1)}, bf16[2,8,64,128]{3,2,1,0:T(8,128)(2,1)S(1)}, u32[]{:S(2)}, u32[]{:S(2)}) %collective-permute-start.4) | collective-permute-done | bytes 262176 | tf_op jit(solution)/shard_map/ppermute | solution.py:700
  65.3 4.0 %collective-permute-done.5.refs_3_ = bf16[2,8,64,128]{3,2,1,0:T(8,128)(2,1)S(1)} collective-permute-done((bf16[2,8,64,128]{3,2,1,0:T(8,128)(2,1)}, bf16[2,8,64,128]{3,2,1,0:T(8,128)(2,1)S(1)}, u32[]{:S(2)}, u32[]{:S(2)}) %collective-permute-start.5) | collective-permute-done | bytes 262176 | tf_op jit(solution)/shard_map/ppermute | solution.py:700
  75.6 6.7 %project.1 = (f32[16,2048]{1,0:T(8,128)S(1)}, bf16[4,16,2048]{2,1,0:T(8,128)(2,1)}) custom-call(s32[68]{0:T(128)S(1)} %plan.1._table.table, bf16[4,32,2048]{2,1,0:T(8,128)(2,1)S(1)} %all-to-all-done.1.refs_5_.refs_0_.packets, bf16[2048,2048]{1,0:T(8,128)(2,1)} %refs_4_.3, bf16[2048,2048]{1,0:T(8,128)(2,1)} %refs_4_.3, bf16[2048,2048]{1,0:T(8,128)(2,1)} %refs_4_.3, ...), custom_call_target="tpu_custom_call" | custom-call | bytes 19200000 | tf_op jit(solution)/shard_map/project/pallas_call | solution.py:404
  82.3 4.0 %all-to-all-start.2 = ((bf16[4,16,2048]{2,1,0:T(8,128)(2,1)}), bf16[4,16,2048]{2,1,0:T(8,128)(2,1)}, u32[]{:S(2)}, u32[]{:S(2)}) async-start(bf16[4,16,2048]{2,1,0:T(8,128)(2,1)} %get-tuple-element.46.refs_5_), calls=%async_computation.2 | async-start | bytes 524288 | tf_op jit(solution)/shard_map/all_to_all | solution.py:706
  88.7 1.7 %collective-permute-start.10 = (bf16[4,13440]{1,0:T(4,128)(2,1)S(1)}, bf16[4,13440]{1,0:T(4,128)(2,1)S(1)}, u32[]{:S(2)}, u32[]{:S(2)}) collective-permute-start(bf16[4,13440]{1,0:T(4,128)(2,1)S(1)} %get-tuple-element.48.refs_6_), channel_id=1, source_target_pairs={{0,1},{1,0},{2,3},{3,2},{4,5},{5,4},{6,7},{7,6},{8,9},{9,8},{10,11... | collective-permute-start | bytes 322568 | tf_op jit(solution)/shard_map/ppermute | solution.py:700
  91.0 5.0 %collective-permute-done.10.refs_4_.refs_5_.refs_6_.refs_7_.got = bf16[4,13440]{1,0:T(4,128)(2,1)S(1)} collective-permute-done((bf16[4,13440]{1,0:T(4,128)(2,1)S(1)}, bf16[4,13440]{1,0:T(4,128)(2,1)S(1)}, u32[]{:S(2)}, u32[]{:S(2)}) %collective-permute-start.10) | collective-permute-done | bytes 107552 | tf_op jit(solution)/shard_map/ppermute | solution.py:700
  99.5 2.3 %finish_0_8.1 = (f32[1,1,4,64,64,128]{5,4,3,2,1,0:T(8,128)}, f32[8,128]{1,0:T(8,128)}) custom-call(s32[68]{0:T(128)S(1)} %plan.1._table.table, f32[256]{0:T(256)S(1)} %reshape.17.decay, bf16[4,8,64,128]{3,2,1,0:T(8,128)(2,1)S(1)} %copy-done.9, bf16[4,8,64,128]{3,2,1,0:T(8,128)(2,1)S(1)} %copy-done.3, ...), custom_call_target="tpu_custom_call" | custom-call | bytes 7680000 | tf_op jit(solution)/shard_map/finish_0_8/pallas_call | solution.py:651
  103.9 2.3 %finish_8_8.1 = (f32[1,1,4,64,64,128]{5,4,3,2,1,0:T(8,128)}, f32[8,128]{1,0:T(8,128)}) custom-call(s32[68]{0:T(128)S(1)} %plan.1._table.table, f32[256]{0:T(256)S(1)} %reshape.17.decay, bf16[4,8,64,128]{3,2,1,0:T(8,128)(2,1)S(1)} %copy-done.7, bf16[4,8,64,128]{3,2,1,0:T(8,128)(2,1)S(1)} %copy-done.1, ...), custom_call_target="tpu_custom_call", output_to_operand_aliasing={{0}: (12, {})} | custom-call | bytes 7680000 | tf_op jit(solution)/shard_map/finish_8_8/pallas_call | solution.py:651
  106.2 2.7 %route_24_8.1 = (bf16[4,8,64,128]{3,2,1,0:T(8,128)(2,1)S(1)}, bf16[4,8,64,128]{3,2,1,0:T(8,128)(2,1)}) custom-call(s32[68]{0:T(128)S(1)} %plan.1._table.table, bf16[2,24,64,128]{3,2,1,0:T(8,128)(2,1)S(1)} %get-tuple-element.37.refs_0_, bf16[2,24,64,128]{3,2,1,0:T(8,128)(2,1)S(1)} %collective-permute-done.3.refs_1_, ...), custom_call_target="tpu_custom_call" | custom-call | bytes 3200000 | tf_op jit(solution)/shard_map/route_24_8/pallas_call | solution.py:581
  111.7 2.3 %finish_16_8.1 = (f32[1,1,4,64,64,128]{5,4,3,2,1,0:T(8,128)}, f32[8,128]{1,0:T(8,128)}) custom-call(s32[68]{0:T(128)S(1)} %plan.1._table.table, f32[256]{0:T(256)S(1)} %reshape.17.decay, bf16[4,8,64,128]{3,2,1,0:T(8,128)(2,1)S(1)} %copy-done.5, bf16[4,8,64,128]{3,2,1,0:T(8,128)(2,1)S(1)} %collective-permute-done.13.refs_4_.got, ...), custom_call_target="tpu_custom_call", output_to_operand_aliasing={{0}: (12, {})} | custom-call | bytes 7680000 | tf_op jit(solution)/shard_map/finish_16_8/pallas_call | solution.py:651
  114.0 9.1 %collective-permute-done.14.got = bf16[4,8,64,128]{3,2,1,0:T(8,128)(2,1)S(1)} collective-permute-done((bf16[4,8,64,128]{3,2,1,0:T(8,128)(2,1)}, bf16[4,8,64,128]{3,2,1,0:T(8,128)(2,1)S(1)}, u32[]{:S(2)}, u32[]{:S(2)}) %collective-permute-start.14) | collective-permute-done | bytes 524320 | tf_op jit(solution)/shard_map/ppermute | solution.py:700
  123.1 2.3 %finish_24_8.1 = (f32[1,1,4,64,64,128]{5,4,3,2,1,0:T(8,128)}, f32[8,128]{1,0:T(8,128)}) custom-call(s32[68]{0:T(128)S(1)} %plan.1._table.table, f32[256]{0:T(256)S(1)} %reshape.17.decay, bf16[4,8,64,128]{3,2,1,0:T(8,128)(2,1)S(1)} %get-tuple-element.50.keep, ...), custom_call_target="tpu_custom_call", output_to_operand_aliasing={{0}: (12, {})} | custom-call | bytes 7680000 | tf_op jit(solution)/shard_map/finish_24_8/pallas_call | solution.py:651
  (106 shorter events, 30.9 us)
Async XLA Ops:
  6.0 17.2 %collective-permute-start = (bf16[2,8,64,128]{3,2,1,0:T(8,128)(2,1)S(1)}, bf16[2,8,64,128]{3,2,1,0:T(8,128)(2,1)S(1)}, u32[]{:S(2)}, u32[]{:S(2)}) collective-permute-start(bf16[2,8,64,128]{3,2,1,0:T(8,128)(2,1)S(1)} %get-tuple-element.32), channel_id=1, source_target_pairs={{0,4},{4,0},{8,12},{12,8},{1,5},{5,1},{9,13},{13,9},{2,6},{6,2},{1... | collective-permute-start | bytes 786440 | tf_op jit(solution)/shard_map/ppermute | solution.py:700
  6.5 16.7 %collective-permute-start.1 = (bf16[2,8,64,128]{3,2,1,0:T(8,128)(2,1)S(1)}, bf16[2,8,64,128]{3,2,1,0:T(8,128)(2,1)S(1)}, u32[]{:S(2)}, u32[]{:S(2)}) collective-permute-start(bf16[2,8,64,128]{3,2,1,0:T(8,128)(2,1)S(1)} %get-tuple-element.33), channel_id=1, source_target_pairs={{0,8},{4,12},{8,0},{12,4},{1,9},{5,13},{9,1},{13,5},{2,10},{6,14},... | collective-permute-start | bytes 786440 | tf_op jit(solution)/shard_map/ppermute | solution.py:700
  9.1 14.2 %collective-permute-start.2 = (bf16[2,8,64,128]{3,2,1,0:T(8,128)(2,1)S(1)}, bf16[2,8,64,128]{3,2,1,0:T(8,128)(2,1)S(1)}, u32[]{:S(2)}, u32[]{:S(2)}) collective-permute-start(bf16[2,8,64,128]{3,2,1,0:T(8,128)(2,1)S(1)} %get-tuple-element.34), channel_id=1, source_target_pairs={{0,12},{4,8},{8,4},{12,0},{1,13},{5,9},{9,5},{13,1},{2,14},{6,10},... | collective-permute-start | bytes 786440 | tf_op jit(solution)/shard_map/ppermute | solution.py:700
  10.7 12.6 %all-to-all-start = ((bf16[4,2,9472]{2,1,0:T(2,128)(2,1)}), bf16[4,2,9472]{2,1,0:T(2,128)(2,1)S(1)}, u32[]{:S(2)}, u32[]{:S(2)}) async-start(bf16[4,2,9472]{2,1,0:T(2,128)(2,1)} %tokens.1.refs_4_), calls=%async_computation | async-start | bytes 303104 | tf_op jit(solution)/shard_map/all_to_all | solution.py:706
  24.9 6.8 %copy-start.30 = (bf16[32]{0:T(256)(128)(2,1)S(1)}, bf16[32]{0:T(256)(128)(2,1)}, u32[]{:S(2)}) copy-start(bf16[32]{0:T(256)(128)(2,1)} %param.25) | copy-start | bytes 196
  24.9 6.8 %copy-start.31 = (bf16[32]{0:T(256)(128)(2,1)S(1)}, bf16[32]{0:T(256)(128)(2,1)}, u32[]{:S(2)}) copy-start(bf16[32]{0:T(256)(128)(2,1)} %param.24) | copy-start | bytes 196
  24.9 6.8 %copy-start.32 = (bf16[32]{0:T(256)(128)(2,1)S(1)}, bf16[32]{0:T(256)(128)(2,1)}, u32[]{:S(2)}) copy-start(bf16[32]{0:T(256)(128)(2,1)} %param.23) | copy-start | bytes 196
  28.2 15.9 %collective-permute-start.3 = (bf16[2,24,64,128]{3,2,1,0:T(8,128)(2,1)S(1)}, bf16[2,24,64,128]{3,2,1,0:T(8,128)(2,1)S(1)}, u32[]{:S(2)}, u32[]{:S(2)}) collective-permute-start(bf16[2,24,64,128]{3,2,1,0:T(8,128)(2,1)S(1)} %get-tuple-element.38), channel_id=1, source_target_pairs={{0,4},{4,0},{8,12},{12,8},{1,5},{5,1},{9,13},{13,9},{2,6},{6,2},{1... | collective-permute-start | bytes 2359304 | tf_op jit(solution)/shard_map/ppermute | solution.py:700
  28.3 15.8 %collective-permute-start.8 = (bf16[4,8,64,128]{3,2,1,0:T(8,128)(2,1)S(1)}, bf16[4,8,64,128]{3,2,1,0:T(8,128)(2,1)S(1)}, u32[]{:S(2)}, u32[]{:S(2)}) collective-permute-start(bf16[4,8,64,128]{3,2,1,0:T(8,128)(2,1)S(1)} %get-tuple-element.36.refs_4_), channel_id=1, source_target_pairs={{0,1},{1,0},{2,3},{3,2},{4,5},{5,4},{6,7},{7,6},{8,9},{9,8},{10,11... | collective-permute-start | bytes 1572872 | tf_op jit(solution)/shard_map/ppermute | solution.py:700
  30.2 13.9 %collective-permute-start.6 = (bf16[2,8,64,128]{3,2,1,0:T(8,128)(2,1)S(1)}, bf16[2,8,64,128]{3,2,1,0:T(8,128)(2,1)S(1)}, u32[]{:S(2)}, u32[]{:S(2)}) collective-permute-start(bf16[2,8,64,128]{3,2,1,0:T(8,128)(2,1)S(1)} %get-tuple-element.35.refs_4_), channel_id=1, source_target_pairs={{0,8},{4,12},{8,0},{12,4},{1,9},{5,13},{9,1},{13,5},{2,10},{6,14},... | collective-permute-start | bytes 786440 | tf_op jit(solution)/shard_map/ppermute | solution.py:700
  31.7 12.4 %collective-permute-start.7 = (bf16[2,8,64,128]{3,2,1,0:T(8,128)(2,1)S(1)}, bf16[2,8,64,128]{3,2,1,0:T(8,128)(2,1)S(1)}, u32[]{:S(2)}, u32[]{:S(2)}) collective-permute-start(bf16[2,8,64,128]{3,2,1,0:T(8,128)(2,1)S(1)} %get-tuple-element.41), channel_id=1, source_target_pairs={{0,12},{4,8},{8,4},{12,0},{1,13},{5,9},{9,5},{13,1},{2,14},{6,10},... | collective-permute-start | bytes 786440 | tf_op jit(solution)/shard_map/ppermute | solution.py:700
  34.5 9.6 %copy-start.12 = (bf16[2,8,64,128]{3,2,1,0:T(8,128)(2,1)}, bf16[2,8,64,128]{3,2,1,0:T(8,128)(2,1)S(1)}, u32[]{:S(2)}) copy-start(bf16[2,8,64,128]{3,2,1,0:T(8,128)(2,1)S(1)} %get-tuple-element.39.refs_5_) | copy-start | bytes 786436
  45.8 24.2 %collective-permute-start.9 = (bf16[4,8,64,128]{3,2,1,0:T(8,128)(2,1)S(1)}, bf16[4,8,64,128]{3,2,1,0:T(8,128)(2,1)S(1)}, u32[]{:S(2)}, u32[]{:S(2)}) collective-permute-start(bf16[4,8,64,128]{3,2,1,0:T(8,128)(2,1)S(1)} %get-tuple-element.42.refs_4_), channel_id=1, source_target_pairs={{0,1},{1,0},{2,3},{3,2},{4,5},{5,4},{6,7},{7,6},{8,9},{9,8},{10,11... | collective-permute-start | bytes 1572872 | tf_op jit(solution)/shard_map/ppermute | solution.py:700
  46.2 23.8 %all-to-all-start.1 = ((bf16[4,32,2048]{2,1,0:T(8,128)(2,1)}), bf16[4,32,2048]{2,1,0:T(8,128)(2,1)S(1)}, u32[]{:S(2)}, u32[]{:S(2)}) async-start(bf16[4,32,2048]{2,1,0:T(8,128)(2,1)} %rows.1.refs_4_), calls=%async_computation.1 | async-start | bytes 1048576 | tf_op jit(solution)/shard_map/all_to_all | solution.py:706
  49.7 14.9 %collective-permute-start.4 = (bf16[2,8,64,128]{3,2,1,0:T(8,128)(2,1)}, bf16[2,8,64,128]{3,2,1,0:T(8,128)(2,1)S(1)}, u32[]{:S(2)}, u32[]{:S(2)}) collective-permute-start(bf16[2,8,64,128]{3,2,1,0:T(8,128)(2,1)} %copy-done.12), channel_id=1, source_target_pairs={{0,8},{4,12},{8,0},{12,4},{1,9},{5,13},{9,1},{13,5},{2,10},{6,14},... | collective-permute-start | bytes 786440 | tf_op jit(solution)/shard_map/ppermute | solution.py:700
  51.7 17.6 %collective-permute-start.5 = (bf16[2,8,64,128]{3,2,1,0:T(8,128)(2,1)}, bf16[2,8,64,128]{3,2,1,0:T(8,128)(2,1)S(1)}, u32[]{:S(2)}, u32[]{:S(2)}) collective-permute-start(bf16[2,8,64,128]{3,2,1,0:T(8,128)(2,1)} %copy-done.24), channel_id=1, source_target_pairs={{0,12},{4,8},{8,4},{12,0},{1,13},{5,9},{9,5},{13,1},{2,14},{6,10},... | collective-permute-start | bytes 786440 | tf_op jit(solution)/shard_map/ppermute | solution.py:700
  73.9 8.4 %copy-start.4 = (bf16[4,8,64,128]{3,2,1,0:T(8,128)(2,1)}, bf16[4,8,64,128]{3,2,1,0:T(8,128)(2,1)S(1)}, u32[]{:S(2)}) copy-start(bf16[4,8,64,128]{3,2,1,0:T(8,128)(2,1)S(1)} %get-tuple-element.52.keep) | copy-start | bytes 1572868
  73.9 32.2 %collective-permute-start.13 = (bf16[4,8,64,128]{3,2,1,0:T(8,128)(2,1)S(1)}, bf16[4,8,64,128]{3,2,1,0:T(8,128)(2,1)S(1)}, u32[]{:S(2)}, u32[]{:S(2)}) collective-permute-start(bf16[4,8,64,128]{3,2,1,0:T(8,128)(2,1)S(1)} %get-tuple-element.44.refs_5_.refs_0_), channel_id=1, source_target_pairs={{0,1},{1,0},{2,3},{3,2},{4,5},{5,4},{6,7},{7,6},{8,9},{9,8},{10,11... | collective-permute-start | bytes 1572872 | tf_op jit(solution)/shard_map/ppermute | solution.py:700
  82.3 26.7 %all-to-all-start.2 = ((bf16[4,16,2048]{2,1,0:T(8,128)(2,1)}), bf16[4,16,2048]{2,1,0:T(8,128)(2,1)}, u32[]{:S(2)}, u32[]{:S(2)}) async-start(bf16[4,16,2048]{2,1,0:T(8,128)(2,1)} %get-tuple-element.46.refs_5_), calls=%async_computation.2 | async-start | bytes 524288 | tf_op jit(solution)/shard_map/all_to_all | solution.py:706
  86.3 19.8 %collective-permute-start.11 = (bf16[2,8,64,128]{3,2,1,0:T(8,128)(2,1)}, bf16[2,8,64,128]{3,2,1,0:T(8,128)(2,1)}, u32[]{:S(2)}, u32[]{:S(2)}) collective-permute-start(bf16[2,8,64,128]{3,2,1,0:T(8,128)(2,1)} %copy-done.10), channel_id=1, source_target_pairs={{0,8},{4,12},{8,0},{12,4},{1,9},{5,13},{9,1},{13,5},{2,10},{6,14},... | collective-permute-start | bytes 786440 | tf_op jit(solution)/shard_map/ppermute | solution.py:700
  87.0 19.1 %collective-permute-start.12 = (bf16[2,8,64,128]{3,2,1,0:T(8,128)(2,1)}, bf16[2,8,64,128]{3,2,1,0:T(8,128)(2,1)}, u32[]{:S(2)}, u32[]{:S(2)}) collective-permute-start(bf16[2,8,64,128]{3,2,1,0:T(8,128)(2,1)} %copy-done.23), channel_id=1, source_target_pairs={{0,12},{4,8},{8,4},{12,0},{1,13},{5,9},{9,5},{13,1},{2,14},{6,10},... | collective-permute-start | bytes 786440 | tf_op jit(solution)/shard_map/ppermute | solution.py:700
  88.7 7.4 %collective-permute-start.10 = (bf16[4,13440]{1,0:T(4,128)(2,1)S(1)}, bf16[4,13440]{1,0:T(4,128)(2,1)S(1)}, u32[]{:S(2)}, u32[]{:S(2)}) collective-permute-start(bf16[4,13440]{1,0:T(4,128)(2,1)S(1)} %get-tuple-element.48.refs_6_), channel_id=1, source_target_pairs={{0,1},{1,0},{2,3},{3,2},{4,5},{5,4},{6,7},{7,6},{8,9},{9,8},{10,11... | collective-permute-start | bytes 322568 | tf_op jit(solution)/shard_map/ppermute | solution.py:700
  91.0 15.2 %copy-start.18 = (bf16[4,13440]{1,0:T(4,128)(2,1)S(1)}, bf16[4,13440]{1,0:T(4,128)(2,1)}, u32[]{:S(2)}) copy-start(bf16[4,13440]{1,0:T(4,128)(2,1)} %copy-done.17) | copy-start | bytes 322564
  108.8 14.3 %collective-permute-start.14 = (bf16[4,8,64,128]{3,2,1,0:T(8,128)(2,1)}, bf16[4,8,64,128]{3,2,1,0:T(8,128)(2,1)S(1)}, u32[]{:S(2)}, u32[]{:S(2)}) collective-permute-start(bf16[4,8,64,128]{3,2,1,0:T(8,128)(2,1)} %get-tuple-element.51), channel_id=1, source_target_pairs={{0,1},{1,0},{2,3},{3,2},{4,5},{5,4},{6,7},{7,6},{8,9},{9,8},{10,11... | collective-permute-start | bytes 1572872 | tf_op jit(solution)/shard_map/ppermute | solution.py:700
  (27 other events, 56.0 us)

commit v4 on v3

--- a/solution.py
+++ b/solution.py
@@ -19,18 +19,12 @@
 NEAR = 2
 ROWS = 2 * R_PF
 PARTS = 4
+BLOCKS = 8
 LANES = 128
 VMEM_LIMIT = 48 * 1024 * 1024
-SCALE = 1.0
-
-
-def cost(microseconds):
-    return pl.CostEstimate(
-        flops=0, bytes_accessed=int(SCALE * 3.2e6 * microseconds), transcendentals=0
-    )
-
-
+VMEM_LARGE = 48 * 1024 * 1024
 ANY = pl.BlockSpec(memory_space=pl.ANY)
+HBM = pl.BlockSpec(memory_space=pltpu.HBM)
 
 
 def split_bf16(value):
@@ -100,7 +94,6 @@
         out_specs=smem,
         out_shape=jax.ShapeDtypeStruct((plan.size,), jnp.int32),
         compiler_params=pltpu.CompilerParams(vmem_limit_bytes=VMEM_LIMIT),
-        cost_estimate=cost(1.6),
         name="plan",
     )(request_slot, counts)
 
@@ -156,7 +149,6 @@
         ),
         out_shape=jax.ShapeDtypeStruct((plan.places // plan.cap, plan.cap, size), jnp.bfloat16),
         compiler_params=pltpu.CompilerParams(vmem_limit_bytes=VMEM_LIMIT),
-        cost_estimate=cost(1.4),
         name="tokens",
     )(table, xbc, z, dt, *after)
 
@@ -176,137 +168,149 @@
     return taps_at, last_at, decay_at, decay_at + LANES
 
 
-def rows_kernel(plan, table, tokens, conv, weight, bias, small, gain, *refs):
-    states = refs[:PARTS]
-    out, read, read_taps, acts, wide, gates, lines = refs[-7:]
+def rows_kernel(plan, table, tokens, conv, weight, bias, small, gain, state, *refs):
+    out, states, sems, read, read_taps, acts, wide, gates, lines = refs[-9:]
     steps = 2
     taps, groups, conv_width = weight.shape
-    heads = states[0].shape[1] * PARTS
+    heads = state.shape[1]
     channels = groups * X_WIDTH
-    index = pl.program_id(0)
     row_ids = lax.broadcasted_iota(jnp.int32, (R_PF, 1), 0)
     live = row_ids < table[plan.live]
     f32, bf16 = jnp.float32, jnp.bfloat16
     taps_at, last_at, decay_at, _ = packet_places(groups, conv_width)
 
-    @pl.when(index == 0)
-    def _():
-        matrix = one_hot(
-            (R_PF, plan.places), [(row, table[plan.row_place + row]) for row in range(R_PF)]
+    share = heads // PARTS
+
+    def copy(row, part):
+        span = pl.ds(part * share, share)
+        return pltpu.make_async_copy(
+            state.at[row, span], states.at[row, span], sems.at[row * PARTS + part]
         )
-        stride = tokens.shape[2] // steps
-
-        def rows_of(start, size):
-            parts = [tokens[source, :, start : start + size] for source in range(tokens.shape[0])]
-            parts = jnp.concatenate([part.astype(f32) for part in parts], axis=0)
-            return pick(matrix, parts.astype(bf16))
-
-        for group in range(groups):
-            window = [
-                jnp.where(live, conv[tap, group], 0.0) for tap in range(taps - 1)
-            ] + [
-                rows_of(step * stride + group * conv_width, conv_width) for step in range(steps)
-            ]
-            kernel = [weight[tap].astype(f32)[group : group + 1] for tap in range(taps)]
-            offset = bias[...].astype(f32)[group : group + 1]
-            parts = []
+
+    for row in range(R_PF):
+        for part in range(PARTS):
+            copy(row, part).start()
+
+    matrix = one_hot(
+        (R_PF, plan.places), [(row, table[plan.row_place + row]) for row in range(R_PF)]
+    )
+    stride = tokens.shape[2] // steps
+
+    def rows_of(start, size):
+        parts = [tokens[source, :, start : start + size] for source in range(tokens.shape[0])]
+        parts = jnp.concatenate([part.astype(f32) for part in parts], axis=0)
+        return pick(matrix, parts.astype(bf16))
+
+    for group in range(groups):
+        window = [
+            jnp.where(live, conv[tap, group], 0.0) for tap in range(taps - 1)
+        ] + [
+            rows_of(step * stride + group * conv_width, conv_width) for step in range(steps)
+        ]
+        kernel = [weight[tap].astype(f32)[group : group + 1] for tap in range(taps)]
+        offset = bias[...].astype(f32)[group : group + 1]
+        parts = []
+        for step in range(steps):
+            total = sum(window[step + tap] * kernel[tap] for tap in range(taps)) + offset
+            act = silu(total)
+            acts[step, group] = act
+            parts.append(act[:, X_WIDTH + N :])
+        high = [part.astype(bf16).astype(f32) for part in parts]
+        low = [part - near for part, near in zip(parts, high)]
+        read_taps[group] = jnp.concatenate(high + low, axis=0).astype(bf16)
+        start = last_at + group * conv_width
+        lines[:, start : start + conv_width] = window[taps - 2]
+
+    dts, decays = [], []
+    rate = jnp.exp(small[0:1, :heads])
+    for step in range(steps):
+        base = step * stride + groups * conv_width
+        gates[step] = silu(rows_of(base, channels))
+        raw = rows_of(base + channels, LANES)[:, :heads] + small[1:2, :heads]
+        dts.append(jnp.maximum(raw, 0.0) + jnp.log1p(jnp.exp(-jnp.abs(raw))))
+        decays.append(jnp.exp(-dts[-1] * rate))
+    lines[:, decay_at : decay_at + LANES] = jnp.concatenate(
+        [jnp.where(live, decays[0] * decays[1], 0.0), jnp.zeros((R_PF, LANES - heads), f32)],
+        axis=1,
+    )
+    skip = jnp.broadcast_to(small[2:3, :heads], (R_PF, heads))
+    narrow = jnp.concatenate(dts + decays + [skip], axis=0)
+    high = narrow.astype(bf16).astype(f32)
+    middle = (narrow - high).astype(bf16).astype(f32)
+    narrow = jnp.concatenate([high, middle, narrow - high - middle], axis=1).astype(bf16)
+    head_ids = lax.broadcasted_iota(jnp.int32, (3 * heads, channels), 0) % heads
+    channel_ids = lax.broadcasted_iota(jnp.int32, (3 * heads, channels), 1) // P_SIZE
+    spread = pick(narrow, (head_ids == channel_ids).astype(bf16))
+    for part in range(5):
+        wide[part] = spread[part * R_PF : (part + 1) * R_PF]
+
+    @pl.loop(0, R_PF)
+    def _(index):
+        for part in range(PARTS):
+            copy(index, part).wait()
+            size = share * P_SIZE
+            group, start = part * size // X_WIDTH, part * size % X_WIDTH
+            rows = states[index, part * share : (part + 1) * share].reshape(size, N)
+            state_high, state_low = split_bf16(rows)
+            dims = (((1,), (1,)), ((), ()))
+            total = lax.dot_general(read_taps[group], state_high, dims, preferred_element_type=f32)
+            rest = lax.dot_general(
+                read_taps[group, : steps * R_PF], state_low, dims, preferred_element_type=f32
+            )
+            total = total[: steps * R_PF] + total[steps * R_PF :] + rest
             for step in range(steps):
-                total = sum(window[step + tap] * kernel[tap] for tap in range(taps)) + offset
-                act = silu(total)
-                acts[step, group] = act
-                parts.append(act[:, X_WIDTH + N :])
-            high = [part.astype(bf16).astype(f32) for part in parts]
-            low = [part - near for part, near in zip(parts, high)]
-            read_taps[group] = jnp.concatenate(high + low, axis=0).astype(bf16)
-            start = last_at + group * conv_width
-            lines[:, start : start + conv_width] = window[taps - 2]
-
-        dts, decays = [], []
-        rate = jnp.exp(small[0:1, :heads])
+                now = total[step * R_PF : (step + 1) * R_PF]
+                span = slice(start, start + size)
+                read[group, step, :, span] = jnp.where(
+                    row_ids == index, now, read[group, step, :, span]
+                )
+
+    for group in range(groups):
+        span = slice(group * X_WIDTH, (group + 1) * X_WIDTH)
+        x = [acts[step, group, :, :X_WIDTH] for step in range(steps)]
+        b = [acts[step, group, :, X_WIDTH : X_WIDTH + N] for step in range(steps)]
+        c = [acts[step, group, :, X_WIDTH + N :] for step in range(steps)]
+        u = [wide[step, :, span] * x[step] for step in range(steps)]
+        first_decay, second_decay, skip = wide[2, :, span], wide[3, :, span], wide[4, :, span]
+        held = [jnp.where(live, read[group, step], 0.0) for step in range(steps)]
+
+        def pair_sum(one, two):
+            return jnp.sum(one * two, axis=1, keepdims=True)
+
+        later = second_decay * u[0]
+        y = [
+            first_decay * held[0] + pair_sum(b[0], c[0]) * u[0] + skip * x[0],
+            second_decay * first_decay * held[1]
+            + pair_sum(b[0], c[1]) * later
+            + pair_sum(b[1], c[1]) * u[1]
+            + skip * x[1],
+        ]
+        result = []
         for step in range(steps):
-            base = step * stride + groups * conv_width
-            gates[step] = silu(rows_of(base, channels))
-            raw = rows_of(base + channels, LANES)[:, :heads] + small[1:2, :heads]
-            dts.append(jnp.maximum(raw, 0.0) + jnp.log1p(jnp.exp(-jnp.abs(raw))))
-            decays.append(jnp.exp(-dts[-1] * rate))
-        lines[:, decay_at : decay_at + LANES] = jnp.concatenate(
-            [jnp.where(live, decays[0] * decays[1], 0.0), jnp.zeros((R_PF, LANES - heads), f32)],
-            axis=1,
-        )
-        skip = jnp.broadcast_to(small[2:3, :heads], (R_PF, heads))
-        narrow = jnp.concatenate(dts + decays + [skip], axis=0)
-        high = narrow.astype(bf16).astype(f32)
-        middle = (narrow - high).astype(bf16).astype(f32)
-        narrow = jnp.concatenate([high, middle, narrow - high - middle], axis=1).astype(bf16)
-        head_ids = lax.broadcasted_iota(jnp.int32, (3 * heads, channels), 0) % heads
-        channel_ids = lax.broadcasted_iota(jnp.int32, (3 * heads, channels), 1) // P_SIZE
-        spread = pick(narrow, (head_ids == channel_ids).astype(bf16))
-        for part in range(5):
-            wide[part] = spread[part * R_PF : (part + 1) * R_PF]
-
-    for part, state in enumerate(states):
-        size = heads // PARTS * P_SIZE
-        group, start = part * size // X_WIDTH, part * size % X_WIDTH
-        state_high, state_low = split_bf16(state[0].reshape(size, N))
-        dims = (((1,), (1,)), ((), ()))
-        total = lax.dot_general(read_taps[group], state_high, dims, preferred_element_type=f32)
-        rest = lax.dot_general(
-            read_taps[group, : steps * R_PF], state_low, dims, preferred_element_type=f32
-        )
-        total = total[: steps * R_PF] + total[steps * R_PF :] + rest
+            gated = y[step] * gates[step, :, span]
+            scale = lax.rsqrt(jnp.mean(gated * gated, axis=1, keepdims=True) + 1e-05)
+            result.append(gated * scale * gain[0:1, span])
+        together = jnp.concatenate(result, axis=0).astype(bf16)
+        for target in range(out.shape[0]):
+            out[target, :ROWS, span] = together
+        lines[:, span] = later
+        lines[:, channels + group * X_WIDTH : channels + (group + 1) * X_WIDTH] = u[1]
         for step in range(steps):
-            now = total[step * R_PF : (step + 1) * R_PF]
-            span = slice(start, start + size)
-            read[group, step, :, span] = jnp.where(row_ids == index, now, read[group, step, :, span])
-
-    @pl.when(index == R_PF - 1)
-    def _():
-        for group in range(groups):
-            span = slice(group * X_WIDTH, (group + 1) * X_WIDTH)
-            x = [acts[step, group, :, :X_WIDTH] for step in range(steps)]
-            b = [acts[step, group, :, X_WIDTH : X_WIDTH + N] for step in range(steps)]
-            c = [acts[step, group, :, X_WIDTH + N :] for step in range(steps)]
-            u = [wide[step, :, span] * x[step] for step in range(steps)]
-            first_decay, second_decay, skip = wide[2, :, span], wide[3, :, span], wide[4, :, span]
-            held = [jnp.where(live, read[group, step], 0.0) for step in range(steps)]
-
-            def pair_sum(one, two):
-                return jnp.sum(one * two, axis=1, keepdims=True)
-
-            later = second_decay * u[0]
-            y = [
-                first_decay * held[0] + pair_sum(b[0], c[0]) * u[0] + skip * x[0],
-                second_decay * first_decay * held[1]
-                + pair_sum(b[0], c[1]) * later
-                + pair_sum(b[1], c[1]) * u[1]
-                + skip * x[1],
-            ]
-            result = []
-            for step in range(steps):
-                gated = y[step] * gates[step, :, span]
-                scale = lax.rsqrt(jnp.mean(gated * gated, axis=1, keepdims=True) + 1e-05)
-                result.append(gated * scale * gain[0:1, span])
-            together = jnp.concatenate(result, axis=0).astype(bf16)
-            for target in range(out.shape[0]):
-                out[target, :ROWS, span] = together
-            lines[:, span] = later
-            lines[:, channels + group * X_WIDTH : channels + (group + 1) * X_WIDTH] = u[1]
-            for step in range(steps):
-                start = taps_at + (step * groups + group) * N
-                lines[:, start : start + N] = b[step]
-        segments = lines.shape[1] // channels
-        values = [lines[:, part * channels : (part + 1) * channels] for part in range(segments)]
-        high = [value.astype(bf16).astype(f32) for value in values]
-        low = [value - near for value, near in zip(values, high)]
-        pairs = []
-        for row in range(R_PF):
-            place = table[plan.row_place + row]
-            first = place // plan.cap * ROWS + place % plan.cap * 2 * segments
-            pairs += [(first + part, part * R_PF + row) for part in range(2 * segments)]
-        matrix = one_hot((out.shape[0] * ROWS, 2 * segments * R_PF), pairs)
-        placed = pick(matrix, jnp.concatenate(high + low, axis=0).astype(bf16)).astype(bf16)
-        for target in range(out.shape[0]):
-            out[target, ROWS:] = placed[target * ROWS : (target + 1) * ROWS]
+            start = taps_at + (step * groups + group) * N
+            lines[:, start : start + N] = b[step]
+    segments = lines.shape[1] // channels
+    values = [lines[:, part * channels : (part + 1) * channels] for part in range(segments)]
+    high = [value.astype(bf16).astype(f32) for value in values]
+    low = [value - near for value, near in zip(values, high)]
+    pairs = []
+    for row in range(R_PF):
+        place = table[plan.row_place + row]
+        first = place // plan.cap * ROWS + place % plan.cap * 2 * segments
+        pairs += [(first + part, part * R_PF + row) for part in range(2 * segments)]
+    matrix = one_hot((out.shape[0] * ROWS, 2 * segments * R_PF), pairs)
+    placed = pick(matrix, jnp.concatenate(high + low, axis=0).astype(bf16)).astype(bf16)
+    for target in range(out.shape[0]):
+        out[target, ROWS:] = placed[target * ROWS : (target + 1) * ROWS]
 
 
 def run_rows(plan, table, tokens, conv, weight, bias, small, gain, ssm_state, after):
@@ -321,7 +325,7 @@
         functools.partial(rows_kernel, plan),
         grid_spec=pltpu.PrefetchScalarGridSpec(
             num_scalar_prefetch=1,
-            grid=(R_PF,),
+            grid=(1,),
             in_specs=[
                 whole(tokens),
                 whole(conv),
@@ -329,17 +333,13 @@
                 whole(bias),
                 whole(small),
                 whole(gain),
-            ]
-            + [
-                pl.BlockSpec(
-                    (1, heads // PARTS, P_SIZE, N),
-                    functools.partial(lambda i, t, part: (i, part, 0, 0), part=part),
-                )
-                for part in range(PARTS)
+                HBM,
             ]
             + [ANY] * len(after),
             out_specs=pl.BlockSpec((sources, 2 * ROWS, channels), lambda i, t: (0, 0, 0)),
             scratch_shapes=[
+                pltpu.VMEM((R_PF, heads, P_SIZE, N), f32),
+                pltpu.SemaphoreType.DMA((R_PF * PARTS,)),
                 pltpu.VMEM((groups, steps, R_PF, X_WIDTH), f32),
                 pltpu.VMEM((groups, 2 * steps * R_PF, N), jnp.bfloat16),
                 pltpu.VMEM((steps, groups, R_PF, conv_width), f32),
@@ -349,43 +349,46 @@
             ],
         ),
         out_shape=jax.ShapeDtypeStruct((sources, 2 * ROWS, channels), jnp.bfloat16),
-        compiler_params=pltpu.CompilerParams(vmem_limit_bytes=VMEM_LIMIT),
-        cost_estimate=cost(9),
+        compiler_params=pltpu.CompilerParams(vmem_limit_bytes=VMEM_LARGE),
         name="rows",
-    )(table, tokens, conv, weight, bias, small, gain, *([ssm_state] * PARTS), *after)
-
-
-def project_kernel(plan, share, table, *refs):
+    )(table, tokens, conv, weight, bias, small, gain, ssm_state, *after)
+
+
+def project_kernel(plan, share, table, normed, weight, *refs):
     steps = 2
     targets = plan.rows // share
-    normed, weights = refs[0], refs[1 : 1 + PARTS]
-    own, out, picked = refs[-3:]
-
-    @pl.when(pl.program_id(0) == 0)
-    def _():
-        shape = (steps * plan.rows, steps * plan.rows)
-        rows = lax.broadcasted_iota(jnp.int32, shape, 0)
-        columns = lax.broadcasted_iota(jnp.int32, shape, 1)
-
-        def add(slot, total):
-            row = table[plan.slot_row + slot]
-            target = slot // share * steps * share + slot % share
-            source = (row // R_PF) * steps * R_PF + row % R_PF
-            for step in range(steps):
-                hit = (rows == target + step * share) & (columns == source + step * R_PF)
-                total = jnp.where(hit, 1.0, total)
-            return total
-
-        matrix = lax.fori_loop(0, plan.rows, add, jnp.zeros(shape, jnp.float32), unroll=8)
-        matrix = matrix.astype(jnp.bfloat16)
-        values = normed[...].reshape(picked.shape)
-        picked[...] = pick(matrix, values).astype(jnp.bfloat16)
-
-    depth = weights[0].shape[0]
-    total = sum(
-        pick(picked[:, part * depth : (part + 1) * depth], weights[part][...])
-        for part in range(PARTS)
-    )
+    own, out, held, total, picked, sems = refs[-6:]
+    depth = weight.shape[0]
+    piece = depth // BLOCKS
+
+    def copy(block):
+        span = pl.ds(block * piece, piece)
+        return pltpu.make_async_copy(weight.at[span], held.at[span], sems.at[block])
+
+    for block in range(BLOCKS):
+        copy(block).start()
+
+    shape = (steps * plan.rows, steps * plan.rows)
+    rows = lax.broadcasted_iota(jnp.int32, shape, 0)
+    columns = lax.broadcasted_iota(jnp.int32, shape, 1)
+
+    def add(slot, matrix):
+        row = table[plan.slot_row + slot]
+        target = slot // share * steps * share + slot % share
+        source = (row // R_PF) * steps * R_PF + row % R_PF
+        for step in range(steps):
+            hit = (rows == target + step * share) & (columns == source + step * R_PF)
+            matrix = jnp.where(hit, 1.0, matrix)
+        return matrix
+
+    matrix = lax.fori_loop(0, plan.rows, add, jnp.zeros(shape, jnp.float32), unroll=8)
+    values = normed[...].reshape(picked.shape)
+    picked[...] = pick(matrix.astype(jnp.bfloat16), values).astype(jnp.bfloat16)
+    for block in range(BLOCKS):
+        copy(block).wait()
+        span = slice(block * piece, (block + 1) * piece)
+        part = pick(picked[:, span], held[span])
+        total[...] = part if block == 0 else total[...] + part
     for target in range(targets):
         part = total[target * steps * share : (target + 1) * steps * share]
         out[target] = part.astype(out.dtype)
@@ -396,38 +399,30 @@
 
 
 def project(plan, share, table, normed, weight, after):
-    depth = weight.shape[0]
-    columns = weight.shape[1]
-    block = min(512, columns)
+    depth, columns = weight.shape
     rows = 2 * share
     targets = plan.rows // share
+    own = jax.ShapeDtypeStruct((rows, columns), jnp.float32)
+    out = jax.ShapeDtypeStruct((targets, rows, columns), jnp.bfloat16)
     return pl.pallas_call(
         functools.partial(project_kernel, plan, share),
         grid_spec=pltpu.PrefetchScalarGridSpec(
             num_scalar_prefetch=1,
-            grid=(columns // block,),
-            in_specs=[pl.BlockSpec((normed.shape[0], ROWS, depth), lambda i, t: (0, 0, 0))]
-            + [
-                pl.BlockSpec(
-                    (depth // PARTS, block), functools.partial(lambda i, t, part: (part, i), part=part)
-                )
-                for part in range(PARTS)
-            ]
+            grid=(1,),
+            in_specs=[pl.BlockSpec((normed.shape[0], ROWS, depth), lambda i, t: (0, 0, 0)), HBM]
             + [ANY] * len(after),
-            out_specs=[
-                pl.BlockSpec((rows, block), lambda i, t: (0, i)),
-                pl.BlockSpec((targets, rows, block), lambda i, t: (0, 0, i)),
+            out_specs=[whole(own), whole(out)],
+            scratch_shapes=[
+                pltpu.VMEM(weight.shape, jnp.bfloat16),
+                pltpu.VMEM((2 * plan.rows, columns), jnp.float32),
+                pltpu.VMEM((2 * plan.rows, depth), jnp.bfloat16),
+                pltpu.SemaphoreType.DMA((BLOCKS,)),
             ],
-            scratch_shapes=[pltpu.VMEM((2 * plan.rows, depth), jnp.bfloat16)],
         ),
-        out_shape=[
-            jax.ShapeDtypeStruct((rows, columns), jnp.float32),
-            jax.ShapeDtypeStruct((targets, rows, columns), jnp.bfloat16),
-        ],
-        compiler_params=pltpu.CompilerParams(vmem_limit_bytes=VMEM_LIMIT),
-        cost_estimate=cost(6),
+        out_shape=[own, out],
+        compiler_params=pltpu.CompilerParams(vmem_limit_bytes=VMEM_LARGE),
         name="project",
-    )(table, normed, *([weight] * PARTS), *after)
+    )(table, normed, weight, *after)
 
 
 def slots_kernel(plan, decay_at, table, packets, xbc, *refs):
@@ -487,12 +482,12 @@
         ),
         out_shape=[out, out],
         compiler_params=pltpu.CompilerParams(vmem_limit_bytes=VMEM_LIMIT),
-        cost_estimate=cost(1),
         name="slots",
     )(table, packets, xbc, *after)
 
 
-def windows_kernel(plan, groups, conv_width, starts, table, own, got, out):
+def windows_kernel(plan, groups, conv_width, starts, table, own, got, *refs):
+    out = refs[-1]
     parity = table[plan.parity]
     for owner, packet in enumerate((own, got)):
         side = jnp.where(parity == owner, 0, groups)
@@ -504,7 +499,7 @@
                     out[0, 0, slot, row, pl.ds(side + group, 1)] = values[slot : slot + 1]
 
 
-def write_windows(plan, table, own, got, groups, conv_width, starts):
+def write_windows(plan, table, own, got, groups, conv_width, starts, after):
     shape = (1, 1, R_PF // 2, len(starts), 2 * groups, conv_width)
     out = jax.ShapeDtypeStruct(shape, jnp.float32)
     return pl.pallas_call(
@@ -512,51 +507,53 @@
         grid_spec=pltpu.PrefetchScalarGridSpec(
             num_scalar_prefetch=1,
             grid=(1,),
-            in_specs=[whole(own), whole(got)],
+            in_specs=[whole(own), whole(got)] + [ANY] * len(after),
             out_specs=whole(out),
         ),
         out_shape=out,
         compiler_params=pltpu.CompilerParams(vmem_limit_bytes=VMEM_LIMIT),
-        cost_estimate=cost(1.3),
         name="windows",
-    )(table, own, got)
-
-
-def pack_kernel(count, cap, _table, *refs):
-    inputs, outputs = refs[:count], refs[-(count // cap) :]
-    for place in range(count):
-        outputs[place // cap][place % cap] = inputs[place][0].astype(jnp.bfloat16)
-
-
-def pack_rows(plan, table, ssm_state, shifts, first, width, cuts, after):
+    )(table, own, got, *after)
+
+
+def pack_kernel(plan, places, first, table, state, *refs):
+    rows, sems = refs[-2:]
+    outputs = refs[-2 - len(places) // plan.cap : -2]
+    width = rows.shape[1]
+
+    def copy(index):
+        row = table[plan.row_of + places[index]]
+        return pltpu.make_async_copy(
+            state.at[row, pl.ds(first, width)], rows.at[index], sems.at[index]
+        )
+
+    for index in range(len(places)):
+        copy(index).start()
+    for index in range(len(places)):
+        copy(index).wait()
+        outputs[index // plan.cap][index % plan.cap] = rows[index].astype(jnp.bfloat16)
+
+
+def pack_rows(plan, table, ssm_state, shifts, first, width, after):
     cap = plan.cap
     places = [shift * cap + rank for shift in shifts for rank in range(cap)]
-    piece = width // cuts
-    start = first // piece
-    specs = [
-        pl.BlockSpec(
-            (1, piece, P_SIZE, N),
-            functools.partial(
-                lambda i, rows, place: (rows[plan.row_of + place], start + i, 0, 0), place=place
-            ),
-        )
-        for place in places
-    ]
     out = jax.ShapeDtypeStruct((cap, width, P_SIZE, N), jnp.bfloat16)
     return pl.pallas_call(
-        functools.partial(pack_kernel, len(places), cap),
+        functools.partial(pack_kernel, plan, places, first),
         grid_spec=pltpu.PrefetchScalarGridSpec(
             num_scalar_prefetch=1,
-            grid=(cuts,),
-            in_specs=specs + [ANY] * len(after),
-            out_specs=[pl.BlockSpec((cap, piece, P_SIZE, N), lambda i, rows: (0, i, 0, 0))]
-            * len(shifts),
+            grid=(1,),
+            in_specs=[HBM] + [ANY] * len(after),
+            out_specs=[whole(out)] * len(shifts),
+            scratch_shapes=[
+                pltpu.VMEM((len(places), width, P_SIZE, N), jnp.float32),
+                pltpu.SemaphoreType.DMA((len(places),)),
+            ],
         ),
         out_shape=[out] * len(shifts),
         compiler_params=pltpu.CompilerParams(vmem_limit_bytes=VMEM_LIMIT),
-        cost_estimate=cost(2.5),
         name=f"pack_{first}_{width}",
-    )(table, *([ssm_state] * len(places)), *after)
+    )(table, ssm_state, *after)
 
 
 def route_kernel(plan, sources, table, *refs):
@@ -588,7 +585,6 @@
         ),
         out_shape=[out, out],
         compiler_params=pltpu.CompilerParams(vmem_limit_bytes=VMEM_LIMIT),
-        cost_estimate=cost(1),
         name=f"route_{first}_{width}",
     )(table, *near, *far, *after)
 
@@ -636,7 +632,7 @@
     chunk = first // width
     taps_at = 2 * channels // N
     out_shape = jax.ShapeDtypeStruct((1, 1, slots, 2 * heads, P_SIZE, N), jnp.float32)
-    extra = [] if so_far is None else [so_far]
+    extra = [so_far]
 
     def part(size, place):
         return pl.BlockSpec((slots, size), lambda o, t, d: (0, place))
@@ -663,9 +659,8 @@
             ],
         ),
         out_shape=[out_shape, jax.ShapeDtypeStruct((8, 128), jnp.float32)],
-        input_output_aliases={12: 0} if extra else {},
+        input_output_aliases={12: 0} if so_far.shape == out_shape.shape else {},
         compiler_params=pltpu.CompilerParams(vmem_limit_bytes=VMEM_LIMIT),
-        cost_estimate=cost(2.4),
         name=f"finish_{first}_{width}",
     )(table, decay, keep, got, *([own] * 4), *([other] * 4), *extra)
 
@@ -715,7 +710,7 @@
 
     def send(chunk, shifts, after):
         width = CHUNKS[chunk][1] * unit
-        packed = pack_rows(plan, table, ssm_state, shifts, firsts[chunk], width, 2, after)
+        packed = pack_rows(plan, table, ssm_state, shifts, firsts[chunk], width, after)
         sent[chunk] = packed[0]
         return [shifted(part, "req", shift) if shift else part for part, shift in zip(packed, shifts)]
 
@@ -732,7 +727,7 @@
     route(0, [], far[0], [sent[1], tokens])
     rest = UNITS - CHUNKS[0][1]
     near = pack_rows(
-        plan, table, ssm_state, range(NEAR), CHUNKS[0][1] * unit, rest * unit, 3, [gives[0]]
+        plan, table, ssm_state, range(NEAR), CHUNKS[0][1] * unit, rest * unit, [sent[1]]
     )
     far[2] = send(2, far_shifts, [gives[0]])
     near = [near[0]] + [shifted(near[shift], "req", shift) for shift in range(1, NEAR)]
@@ -753,28 +748,30 @@
     route(1, near, far[1], [result, sent[2], gots[0]])
     far[3] = send(3, far_shifts, [gives[1]])
     result = exchange(result, "req")
-    route(2, near, far[2], [sent[3], result, gots[1]])
 
     share = plan.rows // head_count
-    own_sum, sums = project(plan, share, table, result, out_weight, [gives[2]])
+    own_sum, sums = project(plan, share, table, result, out_weight, [sent[3]])
     others = exchange(sums, "head").astype(f32)
     is_mine = jnp.arange(head_count) == lax.axis_index("head")
     layer_out = own_sum + jnp.sum(jnp.where(is_mine[:, None, None], 0.0, others), axis=0)
     layer_out = layer_out.astype(jnp.bfloat16).reshape(steps, share, -1)
 
-    own, give = split_slots(plan, table, result, xbc, [gives[2]])
+    own, give = split_slots(plan, table, result, xbc, [sent[3]])
+    route(2, near, far[2], [sums, give, gots[1]])
     other = swap(give)
     _, last_at, decay_at, end = packet_places(groups, conv_width)
     low_at = -(-end // channels) * channels
     fresh_at = low_at + LANES
     starts = [last_at] + [fresh_at + step * groups * conv_width for step in range(steps)]
-    out_conv = write_windows(plan, table, own, other, groups, conv_width, starts)
     both = jnp.stack([own, other]).astype(f32)
     decay = both[:, :, decay_at : decay_at + heads] + both[:, :, low_at : low_at + heads]
     decay = decay.reshape(-1)
-    route(3, near, far[3], [gots[2], sums, give])
-
-    out_ssm = None
+    route(3, near, far[3], [gots[2]])
+    out_conv = write_windows(
+        plan, table, own, other, groups, conv_width, starts, [gives[3]]
+    )
+
+    out_ssm = gives[-1]
     for chunk in range(count):
         out_ssm, done = finish_chunk(
             plan, table, out_ssm, keeps[chunk], gots[chunk], decay, own, other, firsts[chunk], heads

time: 126 us -> 114 us (0.905)
  waiting for transfers between devices: 34.9 us -> 21.1 us
  blocking collectives: 0 us -> 8.69 us
  local copies, waits for them, and re-layouts: 15.5 us -> 10.9 us
  starting transfers between devices: 24.8 us -> 22.8 us
    ppermute x15, waiting for transfers between devices: 27.6 us -> 16.5 us  [shifted(): lax.ppermute(value, axis, [(i, i ^ shift) for i in range(lax.axis_size(ax...]
    all_to_all x0 -> x1, blocking collectives: none -> 8.69 us  [exchange(): return lax.all_to_all(value, axis, split_axis=0, concat_axis=0, tiled=True)]
    unnamed x68 -> x62, local copies, waits for them, and re-layouts: 15.4 us -> 10.8 us
    all_to_all x3 -> x2, starting transfers between devices: 10.8 us -> 7.5 us  [exchange(): return lax.all_to_all(value, axis, split_axis=0, concat_axis=0, tiled=True)]
    all_to_all x3 -> x2, waiting for transfers between devices: 7.29 us -> 4.66 us  [exchange(): return lax.all_to_all(value, axis, split_axis=0, concat_axis=0, tiled=True)]
    pallas_call x1, Pallas kernels: 6.72 us -> 4.34 us  [project(): pl.pallas_call(functools.partial(project_kernel, plan, share), grid_spec=...]
    pallas_call x4, Pallas kernels: 5.24 us -> 7.02 us  [route_chunk(): pl.pallas_call(functools.partial(route_kernel, plan, len(near) + len(far)...]
    ppermute x15, starting transfers between devices: 14 us -> 15.3 us  [shifted(): lax.ppermute(value, axis, [(i, i ^ shift) for i in range(lax.axis_size(ax...]
  transfers between devices with their start and end apart: 18 -> 17, of which waited for: 5 -> 4; matrix products, arithmetic and copies ran while one was open for 1% -> 3% of each run, Pallas kernels for 28% -> 31%
where the time goes in v4:
time: 114 us; the launch traced here: 113 us
  Pallas kernels  46.2 us (41%)
  starting transfers between devices  22.8 us (20%)
  waiting for transfers between devices  21.1 us (19%)
  local copies, waits for them, and re-layouts  10.9 us (10%)
  blocking collectives  8.69 us (8%)
  other arithmetic  2.72 us (2%)
    ppermute x15, waiting for transfers between devices, shifted(): lax.ppermute(value, axis, [(i, i ^ shift) for i in range(lax.axis_size(ax...  16.5 us
    ppermute x15, starting transfers between devices, shifted(): lax.ppermute(value, axis, [(i, i ^ shift) for i in range(lax.axis_size(ax...  15.3 us
    unnamed x62, local copies, waits for them, and re-layouts  10.8 us
    pallas_call x5, Pallas kernels, pack_rows(): pl.pallas_call(functools.partial(pack_kernel, plan, places, first), grid_...  10.7 us
    pallas_call x4, Pallas kernels, finish_chunk(): pl.pallas_call(functools.partial(finish_kernel, plan, width, heads, first...  10.2 us
    pallas_call x1, Pallas kernels, run_rows(): pl.pallas_call(functools.partial(rows_kernel, plan), grid_spec=pltpu.Pref...  9.37 us
    all_to_all x1, blocking collectives, exchange(): return lax.all_to_all(value, axis, split_axis=0, concat_axis=0, tiled=True)  8.69 us
    all_to_all x2, starting transfers between devices, exchange(): return lax.all_to_all(value, axis, split_axis=0, concat_axis=0, tiled=True)  7.5 us
  transfers between devices with their start and end apart: 17, of which 4 were waited for; matrix products, arithmetic and copies ran while one was open for 3% of the time, Pallas kernels for 31%

profile of v4, /device:TPU:0, one launch (start us, length us, event | category | flops | bytes accessed | tf_op | source)
XLA Modules:
  0.0 113.4 jit_solution(8106493926897158112)
XLA Ops:
  3.6 2.1 %pack_0_8.1 = (bf16[2,8,64,128]{3,2,1,0:T(8,128)(2,1)S(1)}, bf16[2,8,64,128]{3,2,1,0:T(8,128)(2,1)S(1)}, bf16[2,8,64,128]{3,2,1,0:T(8,128)(2,1)S(1)}, bf16[2,8,64,128]{3,2,1,0:T(8,128)(2,1)S(1)}) custom-call(s32[68]{0:T(128)S(1)} %plan.1.table, f32[8,32,64,128]{3,2,1,0:T(8,128)} %state.11), custom_call_target="tpu_custom_call" | custom-call | tf_op jit(solution)/shard_map/pack_0_8/pallas_call | solution.py:541
  6.3 2.6 %collective-permute-start.1 = (bf16[2,8,64,128]{3,2,1,0:T(8,128)(2,1)S(1)}, bf16[2,8,64,128]{3,2,1,0:T(8,128)(2,1)S(1)}, u32[]{:S(2)}, u32[]{:S(2)}) collective-permute-start(bf16[2,8,64,128]{3,2,1,0:T(8,128)(2,1)S(1)} %get-tuple-element.33), channel_id=1, source_target_pairs={{0,8},{4,12},{8,0},{12,4},{1,9},{5,13},{9,1},{13,5},{2,10},{6,14},... | collective-permute-start | bytes 786440 | tf_op jit(solution)/shard_map/ppermute | solution.py:695
  9.8 1.8 %pack_8_8.1 = (bf16[2,8,64,128]{3,2,1,0:T(8,128)(2,1)S(1)}, bf16[2,8,64,128]{3,2,1,0:T(8,128)(2,1)S(1)}) custom-call(s32[68]{0:T(128)S(1)} %plan.1.table, f32[8,32,64,128]{3,2,1,0:T(8,128)} %state.11, bf16[4,2,9472]{2,1,0:T(2,128)(2,1)S(1)} %tokens.1.refs_0_), custom_call_target="tpu_custom_call" | custom-call | tf_op jit(solution)/shard_map/pack_8_8/pallas_call | solution.py:541
  11.6 2.5 %pack_8_24.1 = (bf16[2,24,64,128]{3,2,1,0:T(8,128)(2,1)S(1)}, bf16[2,24,64,128]{3,2,1,0:T(8,128)(2,1)S(1)}) custom-call(s32[68]{0:T(128)S(1)} %plan.1.table, f32[8,32,64,128]{3,2,1,0:T(8,128)} %state.11, bf16[2,8,64,128]{3,2,1,0:T(8,128)(2,1)S(1)} %get-tuple-element.35.refs_4_.refs_0_), custom_call_target="tpu_custom_call" | custom-call | tf_op jit(solution)/shard_map/pack_8_24/pallas_call | solution.py:541
  14.3 8.7 %all_to_all.15.refs_5_.tokens = bf16[4,2,9472]{2,1,0:T(2,128)(2,1)S(1)} all-to-all(bf16[4,2,9472]{2,1,0:T(2,128)(2,1)S(1)} %tokens.1.refs_0_), channel_id=1, replica_groups=mesh['groups'=2,'req'=4,'head'=4] {'req'}, dimensions={0} | all-to-all | bytes 303104 | tf_op jit(solution)/shard_map/all_to_all | solution.py:701
  24.7 1.8 %collective-permute-start.6 = (bf16[4,8,64,128]{3,2,1,0:T(8,128)(2,1)S(1)}, bf16[4,8,64,128]{3,2,1,0:T(8,128)(2,1)S(1)}, u32[]{:S(2)}, u32[]{:S(2)}) collective-permute-start(bf16[4,8,64,128]{3,2,1,0:T(8,128)(2,1)S(1)} %get-tuple-element.36.refs_0_), channel_id=1, source_target_pairs={{0,1},{1,0},{2,3},{3,2},{4,5},{5,4},{6,7},{7,6},{8,9},{9,8},{10,11... | collective-permute-start | bytes 1572872 | tf_op jit(solution)/shard_map/ppermute | solution.py:695
  28.1 2.6 %pack_16_8.1 = (bf16[2,8,64,128]{3,2,1,0:T(8,128)(2,1)}, bf16[2,8,64,128]{3,2,1,0:T(8,128)(2,1)}) custom-call(s32[68]{0:T(128)S(1)} %plan.1.table, f32[8,32,64,128]{3,2,1,0:T(8,128)} %state.11, bf16[4,8,64,128]{3,2,1,0:T(8,128)(2,1)S(1)} %get-tuple-element.36.refs_0_), custom_call_target="tpu_custom_call" | custom-call | tf_op jit(solution)/shard_map/pack_16_8/pallas_call | solution.py:541
  30.7 9.4 %rows.1.refs_4_ = bf16[4,32,2048]{2,1,0:T(8,128)(2,1)} custom-call(s32[68]{0:T(128)S(1)} %plan.1.table, bf16[4,2,9472]{2,1,0:T(2,128)(2,1)S(1)} %all_to_all.15.refs_5_.tokens, f32[3,2,8,1280]{3,2,1,0:T(8,128)S(1)} %bitcast.16, bf16[4,2,1280]{2,1,0:T(2,128)(2,1)S(1)} %copy-done.18, bf16[2,1280]{1,0:T(2,128)(2,1)S(1)} %copy-done.19, ...), custom_call_target="tpu_custom_call" | custom-call | tf_op jit(solution)/shard_map/rows/pallas_call | solution.py:324
  43.4 3.5 %all-to-all-start.1 = ((bf16[4,32,2048]{2,1,0:T(8,128)(2,1)}), bf16[4,32,2048]{2,1,0:T(8,128)(2,1)S(1)}, u32[]{:S(2)}, u32[]{:S(2)}) async-start(bf16[4,32,2048]{2,1,0:T(8,128)(2,1)} %rows.1.refs_4_), calls=%async_computation.1 | async-start | bytes 1048576 | tf_op jit(solution)/shard_map/all_to_all | solution.py:701
  46.9 1.7 %collective-permute-start.11 = (bf16[2,8,64,128]{3,2,1,0:T(8,128)(2,1)}, bf16[2,8,64,128]{3,2,1,0:T(8,128)(2,1)}, u32[]{:S(2)}, u32[]{:S(2)}) collective-permute-start(bf16[2,8,64,128]{3,2,1,0:T(8,128)(2,1)} %get-tuple-element.48), channel_id=1, source_target_pairs={{0,12},{4,8},{8,4},{12,0},{1,13},{5,9},{9,5},{13,1},{2,14},{6,10},... | collective-permute-start | bytes 786440 | tf_op jit(solution)/shard_map/ppermute | solution.py:695
  49.0 1.8 %pack_24_8.1 = (bf16[2,8,64,128]{3,2,1,0:T(8,128)(2,1)S(1)}, bf16[2,8,64,128]{3,2,1,0:T(8,128)(2,1)S(1)}) custom-call(s32[68]{0:T(128)S(1)} %plan.1.table, f32[8,32,64,128]{3,2,1,0:T(8,128)} %state.11, bf16[4,8,64,128]{3,2,1,0:T(8,128)(2,1)} %get-tuple-element.41.refs_0_), custom_call_target="tpu_custom_call" | custom-call | tf_op jit(solution)/shard_map/pack_24_8/pallas_call | solution.py:541
  51.5 4.7 %all-to-all-done.1.normed.packets = bf16[4,32,2048]{2,1,0:T(8,128)(2,1)S(1)} async-done(((bf16[4,32,2048]{2,1,0:T(8,128)(2,1)}), bf16[4,32,2048]{2,1,0:T(8,128)(2,1)S(1)}, u32[]{:S(2)}, u32[]{:S(2)}) %all-to-all-start.1) | async-done | bytes 524320 | tf_op jit(solution)/shard_map/all_to_all | solution.py:701
  57.9 4.3 %project.1 = (f32[16,2048]{1,0:T(8,128)S(1)}, bf16[4,16,2048]{2,1,0:T(8,128)(2,1)S(1)}) custom-call(s32[68]{0:T(128)S(1)} %plan.1.table, bf16[4,32,2048]{2,1,0:T(8,128)(2,1)S(1)} %all-to-all-done.1.normed.packets, bf16[2048,2048]{1,0:T(8,128)(2,1)} %weight.3, bf16[2,8,64,128]{3,2,1,0:T(8,128)(2,1)S(1)} %get-tuple-element.42.refs_0_), custom_call_target="tpu_custom_call" | custom-call | tf_op jit(solution)/shard_map/project/pallas_call | solution.py:407
  63.0 4.1 %collective-permute-done.10.refs_2_ = bf16[2,8,64,128]{3,2,1,0:T(8,128)(2,1)} collective-permute-done((bf16[2,8,64,128]{3,2,1,0:T(8,128)(2,1)}, bf16[2,8,64,128]{3,2,1,0:T(8,128)(2,1)}, u32[]{:S(2)}, u32[]{:S(2)}) %collective-permute-start.10) | collective-permute-done | bytes 262176 | tf_op jit(solution)/shard_map/ppermute | solution.py:695
  67.0 2.7 %route_16_8.1 = (bf16[4,8,64,128]{3,2,1,0:T(8,128)(2,1)S(1)}, bf16[4,8,64,128]{3,2,1,0:T(8,128)(2,1)}) custom-call(s32[68]{0:T(128)S(1)} %plan.1.table, bf16[2,24,64,128]{3,2,1,0:T(8,128)(2,1)S(1)} %get-tuple-element.37.refs_0_, bf16[2,24,64,128]{3,2,1,0:T(8,128)(2,1)S(1)} %collective-permute-done.3.refs_1_, ...), custom_call_target="tpu_custom_call" | custom-call | tf_op jit(solution)/shard_map/route_16_8/pallas_call | solution.py:578
  70.5 1.8 %collective-permute-start.13 = (bf16[4,8,64,128]{3,2,1,0:T(8,128)(2,1)}, bf16[4,8,64,128]{3,2,1,0:T(8,128)(2,1)S(1)}, u32[]{:S(2)}, u32[]{:S(2)}) collective-permute-start(bf16[4,8,64,128]{3,2,1,0:T(8,128)(2,1)} %get-tuple-element.49), channel_id=1, source_target_pairs={{0,1},{1,0},{2,3},{3,2},{4,5},{5,4},{6,7},{7,6},{8,9},{9,8},{10,11... | collective-permute-start | bytes 1572872 | tf_op jit(solution)/shard_map/ppermute | solution.py:695
  72.3 4.0 %all-to-all-start.2 = ((bf16[4,16,2048]{2,1,0:T(8,128)(2,1)}), bf16[4,16,2048]{2,1,0:T(8,128)(2,1)}, u32[]{:S(2)}, u32[]{:S(2)}) async-start(bf16[4,16,2048]{2,1,0:T(8,128)(2,1)} %copy-done.4), calls=%async_computation.2 | async-start | bytes 524288 | tf_op jit(solution)/shard_map/all_to_all | solution.py:701
  79.1 11.7 %collective-permute-done.7.refs_4_.refs_5_.refs_6_.refs_7_.got = bf16[4,13440]{1,0:T(4,128)(2,1)S(1)} collective-permute-done((bf16[4,13440]{1,0:T(4,128)(2,1)}, bf16[4,13440]{1,0:T(4,128)(2,1)S(1)}, u32[]{:S(2)}, u32[]{:S(2)}) %collective-permute-start.7) | collective-permute-done | bytes 107552 | tf_op jit(solution)/shard_map/ppermute | solution.py:695
  92.7 1.9 %route_24_8.1 = (bf16[4,8,64,128]{3,2,1,0:T(8,128)(2,1)S(1)}, bf16[4,8,64,128]{3,2,1,0:T(8,128)(2,1)S(1)}) custom-call(s32[68]{0:T(128)S(1)} %plan.1.table, bf16[2,24,64,128]{3,2,1,0:T(8,128)(2,1)S(1)} %get-tuple-element.37.refs_0_, bf16[2,24,64,128]{3,2,1,0:T(8,128)(2,1)S(1)} %collective-permute-done.3.refs_1_, ...), custom_call_target="tpu_custom_call" | custom-call | tf_op jit(solution)/shard_map/route_24_8/pallas_call | solution.py:578
  95.4 1.7 %collective-permute-start.14 = (bf16[4,8,64,128]{3,2,1,0:T(8,128)(2,1)S(1)}, bf16[4,8,64,128]{3,2,1,0:T(8,128)(2,1)}, u32[]{:S(2)}, u32[]{:S(2)}) collective-permute-start(bf16[4,8,64,128]{3,2,1,0:T(8,128)(2,1)S(1)} %get-tuple-element.51.refs_8_.refs_0_), channel_id=1, source_target_pairs={{0,1},{1,0},{2,3},{3,2},{4,5},{5,4},{6,7},{7,6},{8,9},{9,8},{10,11... | collective-permute-start | bytes 1572872 | tf_op jit(solution)/shard_map/ppermute | solution.py:695
  102.2 2.3 %finish_0_8.1 = (f32[1,1,4,64,64,128]{5,4,3,2,1,0:T(8,128)}, f32[8,128]{1,0:T(8,128)}) custom-call(s32[68]{0:T(128)S(1)} %plan.1.table, f32[256]{0:T(256)S(1)} %reshape.17.decay, bf16[4,8,64,128]{3,2,1,0:T(8,128)(2,1)S(1)} %copy-done.8, bf16[4,8,64,128]{3,2,1,0:T(8,128)(2,1)S(1)} %collective-permute-done.6.refs_6_.got, ...), custom_call_target="tpu_custom_call" | custom-call | tf_op jit(solution)/shard_map/finish_0_8/pallas_call | solution.py:647
  105.5 2.3 %finish_8_8.1 = (f32[1,1,4,64,64,128]{5,4,3,2,1,0:T(8,128)}, f32[8,128]{1,0:T(8,128)}) custom-call(s32[68]{0:T(128)S(1)} %plan.1.table, f32[256]{0:T(256)S(1)} %reshape.17.decay, bf16[4,8,64,128]{3,2,1,0:T(8,128)(2,1)S(1)} %copy-done.10, bf16[4,8,64,128]{3,2,1,0:T(8,128)(2,1)S(1)} %collective-permute-done.12.refs_6_.got, ...), custom_call_target="tpu_custom_call", output_to_operand_aliasing={{0}: (12, {})} | custom-call | tf_op jit(solution)/shard_map/finish_8_8/pallas_call | solution.py:647
  107.8 2.3 %finish_16_8.1 = (f32[1,1,4,64,64,128]{5,4,3,2,1,0:T(8,128)}, f32[8,128]{1,0:T(8,128)}) custom-call(s32[68]{0:T(128)S(1)} %plan.1.table, f32[256]{0:T(256)S(1)} %reshape.17.decay, bf16[4,8,64,128]{3,2,1,0:T(8,128)(2,1)S(1)} %copy-done.12, bf16[4,8,64,128]{3,2,1,0:T(8,128)(2,1)S(1)} %copy-done.2, ...), custom_call_target="tpu_custom_call", output_to_operand_aliasing={{0}: (12, {})} | custom-call | tf_op jit(solution)/shard_map/finish_16_8/pallas_call | solution.py:647
  110.1 3.3 %finish_24_8.1 = (f32[1,1,4,64,64,128]{5,4,3,2,1,0:T(8,128)}, f32[8,128]{1,0:T(8,128)}) custom-call(s32[68]{0:T(128)S(1)} %plan.1.table, f32[256]{0:T(256)S(1)} %reshape.17.decay, bf16[4,8,64,128]{3,2,1,0:T(8,128)(2,1)S(1)} %copy-done.14, bf16[4,8,64,128]{3,2,1,0:T(8,128)(2,1)} %collective-permute-done.14.got, ...), custom_call_target="tpu_custom_call", output_to_operand_aliasing={{0}: (12, {})} | custom-call | tf_op jit(solution)/shard_map/finish_24_8/pallas_call | solution.py:647
  (99 shorter events, 26.9 us)
Async XLA Ops:
  5.8 17.2 %collective-permute-start = (bf16[2,8,64,128]{3,2,1,0:T(8,128)(2,1)S(1)}, bf16[2,8,64,128]{3,2,1,0:T(8,128)(2,1)S(1)}, u32[]{:S(2)}, u32[]{:S(2)}) collective-permute-start(bf16[2,8,64,128]{3,2,1,0:T(8,128)(2,1)S(1)} %get-tuple-element.32), channel_id=1, source_target_pairs={{0,4},{4,0},{8,12},{12,8},{1,5},{5,1},{9,13},{13,9},{2,6},{6,2},{1... | collective-permute-start | bytes 786440 | tf_op jit(solution)/shard_map/ppermute | solution.py:695
  6.3 16.7 %collective-permute-start.1 = (bf16[2,8,64,128]{3,2,1,0:T(8,128)(2,1)S(1)}, bf16[2,8,64,128]{3,2,1,0:T(8,128)(2,1)S(1)}, u32[]{:S(2)}, u32[]{:S(2)}) collective-permute-start(bf16[2,8,64,128]{3,2,1,0:T(8,128)(2,1)S(1)} %get-tuple-element.33), channel_id=1, source_target_pairs={{0,8},{4,12},{8,0},{12,4},{1,9},{5,13},{9,1},{13,5},{2,10},{6,14},... | collective-permute-start | bytes 786440 | tf_op jit(solution)/shard_map/ppermute | solution.py:695
  8.9 14.2 %collective-permute-start.2 = (bf16[2,8,64,128]{3,2,1,0:T(8,128)(2,1)S(1)}, bf16[2,8,64,128]{3,2,1,0:T(8,128)(2,1)S(1)}, u32[]{:S(2)}, u32[]{:S(2)}) collective-permute-start(bf16[2,8,64,128]{3,2,1,0:T(8,128)(2,1)S(1)} %get-tuple-element.34), channel_id=1, source_target_pairs={{0,12},{4,8},{8,4},{12,0},{1,13},{5,9},{9,5},{13,1},{2,14},{6,10},... | collective-permute-start | bytes 786440 | tf_op jit(solution)/shard_map/ppermute | solution.py:695
  9.7 18.3 %copy-start.26 = (bf16[2048]{0:T(1024)(128)(2,1)S(1)}, bf16[2048]{0:T(1024)(128)(2,1)}, u32[]{:S(2)}) copy-start(bf16[2048]{0:T(1024)(128)(2,1)} %param.26) | copy-start | bytes 12292
  9.8 18.3 %copy-start.24 = (f32[8,3,2,1280]{3,2,1,0:T(2,128)S(1)}, f32[8,3,2,1280]{3,2,1,0:T(2,128)}, u32[]{:S(2)}) copy-start(f32[8,3,2,1280]{3,2,1,0:T(2,128)} %param.15) | copy-start | bytes 737284
  9.8 18.3 %copy-start.27 = (bf16[32]{0:T(256)(128)(2,1)S(1)}, bf16[32]{0:T(256)(128)(2,1)}, u32[]{:S(2)}) copy-start(bf16[32]{0:T(256)(128)(2,1)} %param.25) | copy-start | bytes 196
  9.8 18.3 %copy-start.28 = (bf16[32]{0:T(256)(128)(2,1)S(1)}, bf16[32]{0:T(256)(128)(2,1)}, u32[]{:S(2)}) copy-start(bf16[32]{0:T(256)(128)(2,1)} %param.24) | copy-start | bytes 196
  9.8 18.3 %copy-start.29 = (bf16[32]{0:T(256)(128)(2,1)S(1)}, bf16[32]{0:T(256)(128)(2,1)}, u32[]{:S(2)}) copy-start(bf16[32]{0:T(256)(128)(2,1)} %param.23) | copy-start | bytes 196
  11.6 19.1 %copy-start.18 = (bf16[4,2,1280]{2,1,0:T(2,128)(2,1)S(1)}, bf16[4,2,1280]{2,1,0:T(2,128)(2,1)}, u32[]{:S(2)}) copy-start(bf16[4,2,1280]{2,1,0:T(2,128)(2,1)} %weight.2) | copy-start | bytes 61444
  11.6 19.1 %copy-start.19 = (bf16[2,1280]{1,0:T(2,128)(2,1)S(1)}, bf16[2,1280]{1,0:T(2,128)(2,1)}, u32[]{:S(2)}) copy-start(bf16[2,1280]{1,0:T(2,128)(2,1)} %bias.1) | copy-start | bytes 15364
  14.1 26.7 %collective-permute-start.3 = (bf16[2,24,64,128]{3,2,1,0:T(8,128)(2,1)S(1)}, bf16[2,24,64,128]{3,2,1,0:T(8,128)(2,1)S(1)}, u32[]{:S(2)}, u32[]{:S(2)}) collective-permute-start(bf16[2,24,64,128]{3,2,1,0:T(8,128)(2,1)S(1)} %get-tuple-element.38), channel_id=1, source_target_pairs={{0,4},{4,0},{8,12},{12,8},{1,5},{5,1},{9,13},{13,9},{2,6},{6,2},{1... | collective-permute-start | bytes 2359304 | tf_op jit(solution)/shard_map/ppermute | solution.py:695
  24.7 16.1 %collective-permute-start.6 = (bf16[4,8,64,128]{3,2,1,0:T(8,128)(2,1)S(1)}, bf16[4,8,64,128]{3,2,1,0:T(8,128)(2,1)S(1)}, u32[]{:S(2)}, u32[]{:S(2)}) collective-permute-start(bf16[4,8,64,128]{3,2,1,0:T(8,128)(2,1)S(1)} %get-tuple-element.36.refs_0_), channel_id=1, source_target_pairs={{0,1},{1,0},{2,3},{3,2},{4,5},{5,4},{6,7},{7,6},{8,9},{9,8},{10,11... | collective-permute-start | bytes 1572872 | tf_op jit(solution)/shard_map/ppermute | solution.py:695
  26.5 13.6 %collective-permute-start.5 = (bf16[2,8,64,128]{3,2,1,0:T(8,128)(2,1)S(1)}, bf16[2,8,64,128]{3,2,1,0:T(8,128)(2,1)S(1)}, u32[]{:S(2)}, u32[]{:S(2)}) collective-permute-start(bf16[2,8,64,128]{3,2,1,0:T(8,128)(2,1)S(1)} %get-tuple-element.39), channel_id=1, source_target_pairs={{0,12},{4,8},{8,4},{12,0},{1,13},{5,9},{9,5},{13,1},{2,14},{6,10},... | collective-permute-start | bytes 786440 | tf_op jit(solution)/shard_map/ppermute | solution.py:695
  27.3 13.4 %collective-permute-start.4 = (bf16[2,8,64,128]{3,2,1,0:T(8,128)(2,1)S(1)}, bf16[2,8,64,128]{3,2,1,0:T(8,128)(2,1)S(1)}, u32[]{:S(2)}, u32[]{:S(2)}) collective-permute-start(bf16[2,8,64,128]{3,2,1,0:T(8,128)(2,1)S(1)} %get-tuple-element.35.refs_4_.refs_0_), channel_id=1, source_target_pairs={{0,8},{4,12},{8,0},{12,4},{1,9},{5,13},{9,1},{13,5},{2,10},{6,14},... | collective-permute-start | bytes 786440 | tf_op jit(solution)/shard_map/ppermute | solution.py:695
  43.2 23.8 %collective-permute-start.12 = (bf16[4,8,64,128]{3,2,1,0:T(8,128)(2,1)}, bf16[4,8,64,128]{3,2,1,0:T(8,128)(2,1)S(1)}, u32[]{:S(2)}, u32[]{:S(2)}) collective-permute-start(bf16[4,8,64,128]{3,2,1,0:T(8,128)(2,1)} %get-tuple-element.41.refs_0_), channel_id=1, source_target_pairs={{0,1},{1,0},{2,3},{3,2},{4,5},{5,4},{6,7},{7,6},{8,9},{9,8},{10,11... | collective-permute-start | bytes 1572872 | tf_op jit(solution)/shard_map/ppermute | solution.py:695
  43.4 12.8 %all-to-all-start.1 = ((bf16[4,32,2048]{2,1,0:T(8,128)(2,1)}), bf16[4,32,2048]{2,1,0:T(8,128)(2,1)S(1)}, u32[]{:S(2)}, u32[]{:S(2)}) async-start(bf16[4,32,2048]{2,1,0:T(8,128)(2,1)} %rows.1.refs_4_), calls=%async_computation.1 | async-start | bytes 1048576 | tf_op jit(solution)/shard_map/all_to_all | solution.py:701
  46.9 16.1 %collective-permute-start.11 = (bf16[2,8,64,128]{3,2,1,0:T(8,128)(2,1)}, bf16[2,8,64,128]{3,2,1,0:T(8,128)(2,1)}, u32[]{:S(2)}, u32[]{:S(2)}) collective-permute-start(bf16[2,8,64,128]{3,2,1,0:T(8,128)(2,1)} %get-tuple-element.48), channel_id=1, source_target_pairs={{0,12},{4,8},{8,4},{12,0},{1,13},{5,9},{9,5},{13,1},{2,14},{6,10},... | collective-permute-start | bytes 786440 | tf_op jit(solution)/shard_map/ppermute | solution.py:695
  48.6 18.4 %collective-permute-start.10 = (bf16[2,8,64,128]{3,2,1,0:T(8,128)(2,1)}, bf16[2,8,64,128]{3,2,1,0:T(8,128)(2,1)}, u32[]{:S(2)}, u32[]{:S(2)}) collective-permute-start(bf16[2,8,64,128]{3,2,1,0:T(8,128)(2,1)} %get-tuple-element.40.refs_5_), channel_id=1, source_target_pairs={{0,8},{4,12},{8,0},{12,4},{1,9},{5,13},{9,1},{13,5},{2,10},{6,14},... | collective-permute-start | bytes 786440 | tf_op jit(solution)/shard_map/ppermute | solution.py:695
  70.5 20.4 %collective-permute-start.13 = (bf16[4,8,64,128]{3,2,1,0:T(8,128)(2,1)}, bf16[4,8,64,128]{3,2,1,0:T(8,128)(2,1)S(1)}, u32[]{:S(2)}, u32[]{:S(2)}) collective-permute-start(bf16[4,8,64,128]{3,2,1,0:T(8,128)(2,1)} %get-tuple-element.49), channel_id=1, source_target_pairs={{0,1},{1,0},{2,3},{3,2},{4,5},{5,4},{6,7},{7,6},{8,9},{9,8},{10,11... | collective-permute-start | bytes 1572872 | tf_op jit(solution)/shard_map/ppermute | solution.py:695
  72.3 24.8 %all-to-all-start.2 = ((bf16[4,16,2048]{2,1,0:T(8,128)(2,1)}), bf16[4,16,2048]{2,1,0:T(8,128)(2,1)}, u32[]{:S(2)}, u32[]{:S(2)}) async-start(bf16[4,16,2048]{2,1,0:T(8,128)(2,1)} %copy-done.4), calls=%async_computation.2 | async-start | bytes 524288 | tf_op jit(solution)/shard_map/all_to_all | solution.py:701
  76.4 14.5 %collective-permute-start.9 = (bf16[2,8,64,128]{3,2,1,0:T(8,128)(2,1)}, bf16[2,8,64,128]{3,2,1,0:T(8,128)(2,1)}, u32[]{:S(2)}, u32[]{:S(2)}) collective-permute-start(bf16[2,8,64,128]{3,2,1,0:T(8,128)(2,1)} %copy-done.21), channel_id=1, source_target_pairs={{0,12},{4,8},{8,4},{12,0},{1,13},{5,9},{9,5},{13,1},{2,14},{6,10},... | collective-permute-start | bytes 786440 | tf_op jit(solution)/shard_map/ppermute | solution.py:695
  76.5 14.4 %collective-permute-start.8 = (bf16[2,8,64,128]{3,2,1,0:T(8,128)(2,1)}, bf16[2,8,64,128]{3,2,1,0:T(8,128)(2,1)}, u32[]{:S(2)}, u32[]{:S(2)}) collective-permute-start(bf16[2,8,64,128]{3,2,1,0:T(8,128)(2,1)} %copy-done.3), channel_id=1, source_target_pairs={{0,8},{4,12},{8,0},{12,4},{1,9},{5,13},{9,1},{13,5},{2,10},{6,14},... | collective-permute-start | bytes 786440 | tf_op jit(solution)/shard_map/ppermute | solution.py:695
  77.4 13.4 %collective-permute-start.7 = (bf16[4,13440]{1,0:T(4,128)(2,1)}, bf16[4,13440]{1,0:T(4,128)(2,1)S(1)}, u32[]{:S(2)}, u32[]{:S(2)}) collective-permute-start(bf16[4,13440]{1,0:T(4,128)(2,1)} %copy-done.16), channel_id=1, source_target_pairs={{0,1},{1,0},{2,3},{3,2},{4,5},{5,4},{6,7},{7,6},{8,9},{9,8},{10,11... | collective-permute-start | bytes 322568 | tf_op jit(solution)/shard_map/ppermute | solution.py:695
  95.4 14.7 %collective-permute-start.14 = (bf16[4,8,64,128]{3,2,1,0:T(8,128)(2,1)S(1)}, bf16[4,8,64,128]{3,2,1,0:T(8,128)(2,1)}, u32[]{:S(2)}, u32[]{:S(2)}) collective-permute-start(bf16[4,8,64,128]{3,2,1,0:T(8,128)(2,1)S(1)} %get-tuple-element.51.refs_8_.refs_0_), channel_id=1, source_target_pairs={{0,1},{1,0},{2,3},{3,2},{4,5},{5,4},{6,7},{7,6},{8,9},{9,8},{10,11... | collective-permute-start | bytes 1572872 | tf_op jit(solution)/shard_map/ppermute | solution.py:695
  (23 other events, 102.9 us)

commit v5 on v4

--- a/solution.py
+++ b/solution.py
@@ -14,7 +14,7 @@
 R_PF = 8
 PER_GROUP = H // G
 X_WIDTH = PER_GROUP * P_SIZE
-CHUNKS = ((0, 2), (2, 2), (4, 2), (6, 2))
+CHUNKS = ((0, 2), (4, 4), (2, 2))
 UNITS = 8
 NEAR = 2
 ROWS = 2 * R_PF
@@ -556,7 +556,7 @@
     )(table, ssm_state, *after)
 
 
-def route_kernel(plan, sources, table, *refs):
+def route_kernel(plan, sources, nears, offset, table, *refs):
     cap = plan.cap
     arrived, keep, give = refs[:sources], refs[-2], refs[-1]
     half = keep.shape[0]
@@ -567,20 +567,23 @@
 
             @pl.when(place // cap == source)
             def _():
-                target[index % half] = arrived[source][place % cap]
-
-
-def route_chunk(plan, table, near, far, first, after):
+                if source < nears:
+                    span = pl.ds(offset, target.shape[1])
+                    target[index % half] = arrived[source][place % cap, span]
+                else:
+                    target[index % half] = arrived[source][place % cap]
+
+
+def route_chunk(plan, table, near, far, first, offset, after):
     width = far[0].shape[1]
     half = R_PF // 2
     out = jax.ShapeDtypeStruct((half, width, P_SIZE, N), jnp.bfloat16)
-    block = pl.BlockSpec((plan.cap, width, P_SIZE, N), lambda i, rows: (0, first // width - 1, 0, 0))
     return pl.pallas_call(
-        functools.partial(route_kernel, plan, len(near) + len(far)),
+        functools.partial(route_kernel, plan, len(near) + len(far), len(near), offset),
         grid_spec=pltpu.PrefetchScalarGridSpec(
             num_scalar_prefetch=1,
             grid=(1,),
-            in_specs=[block] * len(near) + [whole(one) for one in far] + [ANY] * len(after),
+            in_specs=[whole(one) for one in [*near, *far]] + [ANY] * len(after),
             out_specs=[whole(out)] * 2,
         ),
         out_shape=[out, out],
@@ -715,7 +718,9 @@
         return [shifted(part, "req", shift) if shift else part for part, shift in zip(packed, shifts)]
 
     def route(chunk, near, far, after):
-        keeps[chunk], gives[chunk] = route_chunk(plan, table, near, far, firsts[chunk], after)
+        keeps[chunk], gives[chunk] = route_chunk(
+            plan, table, near, far, firsts[chunk], firsts[chunk] - CHUNKS[0][1] * unit, after
+        )
         gots[chunk] = swap(gives[chunk])
 
     xbc = jnp.swapaxes(token_xbc, 1, 2)
@@ -745,20 +750,18 @@
         ssm_state,
         [gives[0]],
     )
-    route(1, near, far[1], [result, sent[2], gots[0]])
-    far[3] = send(3, far_shifts, [gives[1]])
+    route(1, near, far[1], [sent[2], gots[0], result])
     result = exchange(result, "req")
-
     share = plan.rows // head_count
-    own_sum, sums = project(plan, share, table, result, out_weight, [sent[3]])
+    own_sum, sums = project(plan, share, table, result, out_weight, [gives[1]])
     others = exchange(sums, "head").astype(f32)
     is_mine = jnp.arange(head_count) == lax.axis_index("head")
     layer_out = own_sum + jnp.sum(jnp.where(is_mine[:, None, None], 0.0, others), axis=0)
     layer_out = layer_out.astype(jnp.bfloat16).reshape(steps, share, -1)
 
-    own, give = split_slots(plan, table, result, xbc, [sent[3]])
-    route(2, near, far[2], [sums, give, gots[1]])
+    own, give = split_slots(plan, table, result, xbc, far[2])
     other = swap(give)
+    route(2, near, far[2], [sums, other, gots[1]])
     _, last_at, decay_at, end = packet_places(groups, conv_width)
     low_at = -(-end // channels) * channels
     fresh_at = low_at + LANES
@@ -766,9 +769,8 @@
     both = jnp.stack([own, other]).astype(f32)
     decay = both[:, :, decay_at : decay_at + heads] + both[:, :, low_at : low_at + heads]
     decay = decay.reshape(-1)
-    route(3, near, far[3], [gots[2]])
     out_conv = write_windows(
-        plan, table, own, other, groups, conv_width, starts, [gives[3]]
+        plan, table, own, other, groups, conv_width, starts, [gives[2]]
     )
 
     out_ssm = gives[-1]

time: 114 us -> 108 us (0.947)
  blocking collectives: 8.69 us -> 0 us
  waiting for transfers between devices: 21.1 us -> 22.7 us
    all_to_all x1 -> x0, blocking collectives: 8.69 us -> none  [exchange(): return lax.all_to_all(value, axis, split_axis=0, concat_axis=0, tiled=True)]
    all_to_all x2 -> x3, waiting for transfers between devices: 4.66 us -> 10.4 us  [exchange(): return lax.all_to_all(value, axis, split_axis=0, concat_axis=0, tiled=True)]
    ppermute x15 -> x12, waiting for transfers between devices: 16.5 us -> 12.3 us  [shifted(): lax.ppermute(value, axis, [(i, i ^ shift) for i in range(lax.axis_size(ax...]
    all_to_all x2 -> x3, starting transfers between devices: 7.5 us -> 10.9 us  [exchange(): return lax.all_to_all(value, axis, split_axis=0, concat_axis=0, tiled=True)]
    ppermute x15 -> x12, starting transfers between devices: 15.3 us -> 12.7 us  [shifted(): lax.ppermute(value, axis, [(i, i ^ shift) for i in range(lax.axis_size(ax...]
    pallas_call x4 -> x3, Pallas kernels: 10.2 us -> 8.72 us  [finish_chunk(): pl.pallas_call(functools.partial(finish_kernel, plan, width, heads, first...]
    unnamed x62 -> x52, local copies, waits for them, and re-layouts: 10.8 us -> 11.2 us
    pallas_call x5 -> x4, Pallas kernels: 10.7 us -> 10.3 us  [pack_rows(): pl.pallas_call(functools.partial(pack_kernel, plan, places, first), grid_...]
  transfers between devices with their start and end apart: 17 -> 15, of which waited for: 4 -> 6; matrix products, arithmetic and copies ran while one was open for 3% -> 3% of each run, Pallas kernels for 31% -> 33%
where the time goes in v5:
time: 108 us; the launch traced here: 107 us
  Pallas kernels  45.9 us (42%)
  starting transfers between devices  23.5 us (22%)
  waiting for transfers between devices  22.7 us (21%)
  local copies, waits for them, and re-layouts  11.3 us (10%)
  other arithmetic  2.67 us (2%)
    ppermute x12, starting transfers between devices, shifted(): lax.ppermute(value, axis, [(i, i ^ shift) for i in range(lax.axis_size(ax...  12.7 us
    ppermute x12, waiting for transfers between devices, shifted(): lax.ppermute(value, axis, [(i, i ^ shift) for i in range(lax.axis_size(ax...  12.3 us
    unnamed x52, local copies, waits for them, and re-layouts  11.2 us
    all_to_all x3, starting transfers between devices, exchange(): return lax.all_to_all(value, axis, split_axis=0, concat_axis=0, tiled=True)  10.9 us
    all_to_all x3, waiting for transfers between devices, exchange(): return lax.all_to_all(value, axis, split_axis=0, concat_axis=0, tiled=True)  10.4 us
    pallas_call x4, Pallas kernels, pack_rows(): pl.pallas_call(functools.partial(pack_kernel, plan, places, first), grid_...  10.3 us
    pallas_call x1, Pallas kernels, run_rows(): pl.pallas_call(functools.partial(rows_kernel, plan), grid_spec=pltpu.Pref...  9.36 us
    pallas_call x3, Pallas kernels, finish_chunk(): pl.pallas_call(functools.partial(finish_kernel, plan, width, heads, first...  8.72 us
  transfers between devices with their start and end apart: 15, of which 6 were waited for; matrix products, arithmetic and copies ran while one was open for 3% of the time, Pallas kernels for 33%

profile of v5, /device:TPU:0, one launch (start us, length us, event | category | flops | bytes accessed | tf_op | source)
XLA Modules:
  0.0 107.1 jit_solution(10652068886927538463)
XLA Ops:
  3.6 3.0 %pack_0_8.1 = (bf16[2,8,64,128]{3,2,1,0:T(8,128)(2,1)S(1)}, bf16[2,8,64,128]{3,2,1,0:T(8,128)(2,1)}, bf16[2,8,64,128]{3,2,1,0:T(8,128)(2,1)}, bf16[2,8,64,128]{3,2,1,0:T(8,128)(2,1)}) custom-call(s32[68]{0:T(128)S(1)} %plan.1.table, f32[8,32,64,128]{3,2,1,0:T(8,128)} %state.9), custom_call_target="tpu_custom_call" | custom-call | tf_op jit(solution)/shard_map/pack_0_8/pallas_call | solution.py:541
  7.2 2.6 %collective-permute-start.1 = (bf16[2,8,64,128]{3,2,1,0:T(8,128)(2,1)}, bf16[2,8,64,128]{3,2,1,0:T(8,128)(2,1)}, u32[]{:S(2)}, u32[]{:S(2)}) collective-permute-start(bf16[2,8,64,128]{3,2,1,0:T(8,128)(2,1)} %get-tuple-element.28), channel_id=1, source_target_pairs={{0,8},{4,12},{8,0},{12,4},{1,9},{5,13},{9,1},{13,5},{2,10},{6,14},... | collective-permute-start | bytes 786440 | tf_op jit(solution)/shard_map/ppermute | solution.py:698
  12.0 2.1 %pack_16_16.1 = (bf16[2,16,64,128]{3,2,1,0:T(8,128)(2,1)S(1)}, bf16[2,16,64,128]{3,2,1,0:T(8,128)(2,1)S(1)}) custom-call(s32[68]{0:T(128)S(1)} %plan.1.table, f32[8,32,64,128]{3,2,1,0:T(8,128)} %state.9, bf16[4,2,9472]{2,1,0:T(2,128)(2,1)} %tokens.1.refs_0_), custom_call_target="tpu_custom_call" | custom-call | tf_op jit(solution)/shard_map/pack_16_16/pallas_call | solution.py:541
  14.9 3.3 %pack_8_24.1 = (bf16[2,24,64,128]{3,2,1,0:T(8,128)(2,1)S(1)}, bf16[2,24,64,128]{3,2,1,0:T(8,128)(2,1)}) custom-call(s32[68]{0:T(128)S(1)} %plan.1.table, f32[8,32,64,128]{3,2,1,0:T(8,128)} %state.9, bf16[2,16,64,128]{3,2,1,0:T(8,128)(2,1)S(1)} %get-tuple-element.30.refs_4_.refs_0_), custom_call_target="tpu_custom_call" | custom-call | tf_op jit(solution)/shard_map/pack_8_24/pallas_call | solution.py:541
  18.4 3.3 %all-to-all-start = ((bf16[4,2,9472]{2,1,0:T(2,128)(2,1)}), bf16[4,2,9472]{2,1,0:T(2,128)(2,1)S(1)}, u32[]{:S(2)}, u32[]{:S(2)}) async-start(bf16[4,2,9472]{2,1,0:T(2,128)(2,1)} %tokens.1.refs_0_), calls=%async_computation | async-start | bytes 303104 | tf_op jit(solution)/shard_map/all_to_all | solution.py:704
  21.8 2.0 %collective-permute-start.4 = (bf16[2,16,64,128]{3,2,1,0:T(8,128)(2,1)S(1)}, bf16[2,16,64,128]{3,2,1,0:T(8,128)(2,1)S(1)}, u32[]{:S(2)}, u32[]{:S(2)}) collective-permute-start(bf16[2,16,64,128]{3,2,1,0:T(8,128)(2,1)S(1)} %get-tuple-element.30.refs_4_.refs_0_), channel_id=1, source_target_pairs={{0,8},{4,12},{8,0},{12,4},{1,9},{5,13},{9,1},{13,5},{2,10},{6,14},... | collective-permute-start | bytes 1572872 | tf_op jit(solution)/shard_map/ppermute | solution.py:698
  23.8 3.3 %all-to-all-done.refs_5_.tokens = bf16[4,2,9472]{2,1,0:T(2,128)(2,1)S(1)} async-done(((bf16[4,2,9472]{2,1,0:T(2,128)(2,1)}), bf16[4,2,9472]{2,1,0:T(2,128)(2,1)S(1)}, u32[]{:S(2)}, u32[]{:S(2)}) %all-to-all-start) | async-done | bytes 151584 | tf_op jit(solution)/shard_map/all_to_all | solution.py:704
  27.1 1.8 %route_0_8.1 = (bf16[4,8,64,128]{3,2,1,0:T(8,128)(2,1)S(1)}, bf16[4,8,64,128]{3,2,1,0:T(8,128)(2,1)S(1)}) custom-call(s32[68]{0:T(128)S(1)} %plan.1.table, bf16[2,8,64,128]{3,2,1,0:T(8,128)(2,1)S(1)} %get-tuple-element.26.refs_0_, bf16[2,8,64,128]{3,2,1,0:T(8,128)(2,1)S(1)} %collective-permute-done.refs_1_, ...), custom_call_target="tpu_custom_call" | custom-call | tf_op jit(solution)/shard_map/route_0_8/pallas_call | solution.py:581
  29.7 2.0 %collective-permute-start.6 = (bf16[4,8,64,128]{3,2,1,0:T(8,128)(2,1)S(1)}, bf16[4,8,64,128]{3,2,1,0:T(8,128)(2,1)S(1)}, u32[]{:S(2)}, u32[]{:S(2)}) collective-permute-start(bf16[4,8,64,128]{3,2,1,0:T(8,128)(2,1)S(1)} %get-tuple-element.31.refs_0_), channel_id=1, source_target_pairs={{0,1},{1,0},{2,3},{3,2},{4,5},{5,4},{6,7},{7,6},{8,9},{9,8},{10,11... | collective-permute-start | bytes 1572872 | tf_op jit(solution)/shard_map/ppermute | solution.py:698
  32.8 1.8 %pack_8_8.1 = (bf16[2,8,64,128]{3,2,1,0:T(8,128)(2,1)S(1)}, bf16[2,8,64,128]{3,2,1,0:T(8,128)(2,1)S(1)}) custom-call(s32[68]{0:T(128)S(1)} %plan.1.table, f32[8,32,64,128]{3,2,1,0:T(8,128)} %state.9, bf16[4,8,64,128]{3,2,1,0:T(8,128)(2,1)S(1)} %get-tuple-element.31.refs_0_), custom_call_target="tpu_custom_call" | custom-call | tf_op jit(solution)/shard_map/pack_8_8/pallas_call | solution.py:541
  34.6 9.4 %rows.1.refs_6_ = bf16[4,32,2048]{2,1,0:T(8,128)(2,1)} custom-call(s32[68]{0:T(128)S(1)} %plan.1.table, bf16[4,2,9472]{2,1,0:T(2,128)(2,1)S(1)} %all-to-all-done.refs_5_.tokens, f32[3,2,8,1280]{3,2,1,0:T(8,128)S(1)} %bitcast.16, bf16[4,2,1280]{2,1,0:T(2,128)(2,1)S(1)} %copy-done.13, bf16[2,1280]{1,0:T(2,128)(2,1)S(1)} %copy-done.14, ...), custom_call_target="tpu_custom_call" | custom-call | tf_op jit(solution)/shard_map/rows/pallas_call | solution.py:324
  44.0 4.7 %collective-permute-done.5.refs_3_ = bf16[2,16,64,128]{3,2,1,0:T(8,128)(2,1)} collective-permute-done((bf16[2,16,64,128]{3,2,1,0:T(8,128)(2,1)}, bf16[2,16,64,128]{3,2,1,0:T(8,128)(2,1)}, u32[]{:S(2)}, u32[]{:S(2)}) %collective-permute-start.5) | collective-permute-done | bytes 524320 | tf_op jit(solution)/shard_map/ppermute | solution.py:698
  48.7 2.9 %route_16_16.1 = (bf16[4,16,64,128]{3,2,1,0:T(8,128)(2,1)S(1)}, bf16[4,16,64,128]{3,2,1,0:T(8,128)(2,1)}) custom-call(s32[68]{0:T(128)S(1)} %plan.1.table, bf16[2,24,64,128]{3,2,1,0:T(8,128)(2,1)S(1)} %get-tuple-element.32.refs_0_, bf16[2,24,64,128]{3,2,1,0:T(8,128)(2,1)S(1)} %collective-permute-done.3.refs_1_, ...), custom_call_target="tpu_custom_call" | custom-call | tf_op jit(solution)/shard_map/route_16_16/pallas_call | solution.py:581
  52.6 2.0 %collective-permute-start.10 = (bf16[4,16,64,128]{3,2,1,0:T(8,128)(2,1)}, bf16[4,16,64,128]{3,2,1,0:T(8,128)(2,1)S(1)}, u32[]{:S(2)}, u32[]{:S(2)}) collective-permute-start(bf16[4,16,64,128]{3,2,1,0:T(8,128)(2,1)} %get-tuple-element.36.refs_0_), channel_id=1, source_target_pairs={{0,1},{1,0},{2,3},{3,2},{4,5},{5,4},{6,7},{7,6},{8,9},{9,8},{10,11... | collective-permute-start | bytes 3145736 | tf_op jit(solution)/shard_map/ppermute | solution.py:698
  54.7 3.5 %all-to-all-start.1 = ((bf16[4,32,2048]{2,1,0:T(8,128)(2,1)}), bf16[4,32,2048]{2,1,0:T(8,128)(2,1)S(1)}, u32[]{:S(2)}, u32[]{:S(2)}) async-start(bf16[4,32,2048]{2,1,0:T(8,128)(2,1)} %rows.1.refs_6_), calls=%async_computation.1 | async-start | bytes 1048576 | tf_op jit(solution)/shard_map/all_to_all | solution.py:704
  58.1 1.7 %collective-permute-start.8 = (bf16[2,8,64,128]{3,2,1,0:T(8,128)(2,1)}, bf16[2,8,64,128]{3,2,1,0:T(8,128)(2,1)S(1)}, u32[]{:S(2)}, u32[]{:S(2)}) collective-permute-start(bf16[2,8,64,128]{3,2,1,0:T(8,128)(2,1)} %copy-done.17), channel_id=1, source_target_pairs={{0,12},{4,8},{8,4},{12,0},{1,13},{5,9},{9,5},{13,1},{2,14},{6,10},... | collective-permute-start | bytes 786440 | tf_op jit(solution)/shard_map/ppermute | solution.py:698
  60.3 7.2 %all-to-all-done.1.normed.packets = bf16[4,32,2048]{2,1,0:T(8,128)(2,1)S(1)} async-done(((bf16[4,32,2048]{2,1,0:T(8,128)(2,1)}), bf16[4,32,2048]{2,1,0:T(8,128)(2,1)S(1)}, u32[]{:S(2)}, u32[]{:S(2)}) %all-to-all-start.1) | async-done | bytes 524320 | tf_op jit(solution)/shard_map/all_to_all | solution.py:704
  67.4 5.1 %project.1 = (f32[16,2048]{1,0:T(8,128)S(1)}, bf16[4,16,2048]{2,1,0:T(8,128)(2,1)}) custom-call(s32[68]{0:T(128)S(1)} %plan.1.table, bf16[4,32,2048]{2,1,0:T(8,128)(2,1)S(1)} %all-to-all-done.1.normed.packets, bf16[2048,2048]{1,0:T(8,128)(2,1)} %weight.3, bf16[4,16,64,128]{3,2,1,0:T(8,128)(2,1)} %get-tuple-element.36.refs_0_), custom_call_target="tpu_custom_call" | custom-call | tf_op jit(solution)/shard_map/project/pallas_call | solution.py:407
  73.1 4.0 %all-to-all-start.2 = ((bf16[4,16,2048]{2,1,0:T(8,128)(2,1)}), bf16[4,16,2048]{2,1,0:T(8,128)(2,1)}, u32[]{:S(2)}, u32[]{:S(2)}) async-start(bf16[4,16,2048]{2,1,0:T(8,128)(2,1)} %get-tuple-element.38.refs_4_), calls=%async_computation.2 | async-start | bytes 524288 | tf_op jit(solution)/shard_map/all_to_all | solution.py:704
  81.0 5.5 %collective-permute-done.9.refs_5_.refs_4_.refs_6_.refs_7_.got = bf16[4,13440]{1,0:T(4,128)(2,1)S(1)} collective-permute-done((bf16[4,13440]{1,0:T(4,128)(2,1)S(1)}, bf16[4,13440]{1,0:T(4,128)(2,1)S(1)}, u32[]{:S(2)}, u32[]{:S(2)}) %collective-permute-start.9) | collective-permute-done | bytes 107552 | tf_op jit(solution)/shard_map/ppermute | solution.py:698
  86.6 2.5 %route_8_8.1 = (bf16[4,8,64,128]{3,2,1,0:T(8,128)(2,1)S(1)}, bf16[4,8,64,128]{3,2,1,0:T(8,128)(2,1)}) custom-call(s32[68]{0:T(128)S(1)} %plan.1.table, bf16[2,24,64,128]{3,2,1,0:T(8,128)(2,1)S(1)} %get-tuple-element.32.refs_0_, bf16[2,24,64,128]{3,2,1,0:T(8,128)(2,1)S(1)} %collective-permute-done.3.refs_1_, ...), custom_call_target="tpu_custom_call" | custom-call | tf_op jit(solution)/shard_map/route_8_8/pallas_call | solution.py:581
  96.2 2.3 %finish_0_8.1 = (f32[1,1,4,64,64,128]{5,4,3,2,1,0:T(8,128)}, f32[8,128]{1,0:T(8,128)}) custom-call(s32[68]{0:T(128)S(1)} %plan.1.table, f32[256]{0:T(256)S(1)} %reshape.17.decay, bf16[4,8,64,128]{3,2,1,0:T(8,128)(2,1)S(1)} %copy-done.7, bf16[4,8,64,128]{3,2,1,0:T(8,128)(2,1)S(1)} %copy-done.1, ...), custom_call_target="tpu_custom_call" | custom-call | tf_op jit(solution)/shard_map/finish_0_8/pallas_call | solution.py:650
  99.7 3.1 %finish_16_16.1 = (f32[1,1,4,64,64,128]{5,4,3,2,1,0:T(8,128)}, f32[8,128]{1,0:T(8,128)}) custom-call(s32[68]{0:T(128)S(1)} %plan.1.table, f32[256]{0:T(256)S(1)} %reshape.17.decay, bf16[4,16,64,128]{3,2,1,0:T(8,128)(2,1)S(1)} %copy-done.3, bf16[4,16,64,128]{3,2,1,0:T(8,128)(2,1)S(1)} %collective-permute-done.10.refs_6_.got, ...), custom_call_target="tpu_custom_call", output_to_operand_aliasing={{0}: (12, {})} | custom-call | tf_op jit(solution)/shard_map/finish_16_16/pallas_call | solution.py:650
  103.7 3.3 %finish_8_8.1 = (f32[1,1,4,64,64,128]{5,4,3,2,1,0:T(8,128)}, f32[8,128]{1,0:T(8,128)}) custom-call(s32[68]{0:T(128)S(1)} %plan.1.table, f32[256]{0:T(256)S(1)} %reshape.17.decay, bf16[4,8,64,128]{3,2,1,0:T(8,128)(2,1)S(1)} %copy-done.9, bf16[4,8,64,128]{3,2,1,0:T(8,128)(2,1)} %collective-permute-done.11.got, ...), custom_call_target="tpu_custom_call", output_to_operand_aliasing={{0}: (12, {})} | custom-call | tf_op jit(solution)/shard_map/finish_8_8/pallas_call | solution.py:650
  (81 shorter events, 23.6 us)
Async XLA Ops:
  6.7 17.1 %collective-permute-start = (bf16[2,8,64,128]{3,2,1,0:T(8,128)(2,1)}, bf16[2,8,64,128]{3,2,1,0:T(8,128)(2,1)S(1)}, u32[]{:S(2)}, u32[]{:S(2)}) collective-permute-start(bf16[2,8,64,128]{3,2,1,0:T(8,128)(2,1)} %get-tuple-element.27), channel_id=1, source_target_pairs={{0,4},{4,0},{8,12},{12,8},{1,5},{5,1},{9,13},{13,9},{2,6},{6,2},{1... | collective-permute-start | bytes 786440 | tf_op jit(solution)/shard_map/ppermute | solution.py:698
  7.2 19.9 %collective-permute-start.1 = (bf16[2,8,64,128]{3,2,1,0:T(8,128)(2,1)}, bf16[2,8,64,128]{3,2,1,0:T(8,128)(2,1)}, u32[]{:S(2)}, u32[]{:S(2)}) collective-permute-start(bf16[2,8,64,128]{3,2,1,0:T(8,128)(2,1)} %get-tuple-element.28), channel_id=1, source_target_pairs={{0,8},{4,12},{8,0},{12,4},{1,9},{5,13},{9,1},{13,5},{2,10},{6,14},... | collective-permute-start | bytes 786440 | tf_op jit(solution)/shard_map/ppermute | solution.py:698
  9.8 17.3 %collective-permute-start.2 = (bf16[2,8,64,128]{3,2,1,0:T(8,128)(2,1)}, bf16[2,8,64,128]{3,2,1,0:T(8,128)(2,1)}, u32[]{:S(2)}, u32[]{:S(2)}) collective-permute-start(bf16[2,8,64,128]{3,2,1,0:T(8,128)(2,1)} %get-tuple-element.29), channel_id=1, source_target_pairs={{0,12},{4,8},{8,4},{12,0},{1,13},{5,9},{9,5},{13,1},{2,14},{6,10},... | collective-permute-start | bytes 786440 | tf_op jit(solution)/shard_map/ppermute | solution.py:698
  11.9 19.8 %copy-start.21 = (bf16[2048]{0:T(1024)(128)(2,1)S(1)}, bf16[2048]{0:T(1024)(128)(2,1)}, u32[]{:S(2)}) copy-start(bf16[2048]{0:T(1024)(128)(2,1)} %param.26) | copy-start | bytes 12292
  11.9 20.8 %copy-start.22 = (bf16[32]{0:T(256)(128)(2,1)S(1)}, bf16[32]{0:T(256)(128)(2,1)}, u32[]{:S(2)}) copy-start(bf16[32]{0:T(256)(128)(2,1)} %param.25) | copy-start | bytes 196
  11.9 20.8 %copy-start.23 = (bf16[32]{0:T(256)(128)(2,1)S(1)}, bf16[32]{0:T(256)(128)(2,1)}, u32[]{:S(2)}) copy-start(bf16[32]{0:T(256)(128)(2,1)} %param.24) | copy-start | bytes 196
  11.9 20.8 %copy-start.24 = (bf16[32]{0:T(256)(128)(2,1)S(1)}, bf16[32]{0:T(256)(128)(2,1)}, u32[]{:S(2)}) copy-start(bf16[32]{0:T(256)(128)(2,1)} %param.23) | copy-start | bytes 196
  14.9 19.7 %copy-start.13 = (bf16[4,2,1280]{2,1,0:T(2,128)(2,1)S(1)}, bf16[4,2,1280]{2,1,0:T(2,128)(2,1)}, u32[]{:S(2)}) copy-start(bf16[4,2,1280]{2,1,0:T(2,128)(2,1)} %weight.2) | copy-start | bytes 61444
  14.9 19.7 %copy-start.14 = (bf16[2,1280]{1,0:T(2,128)(2,1)S(1)}, bf16[2,1280]{1,0:T(2,128)(2,1)}, u32[]{:S(2)}) copy-start(bf16[2,1280]{1,0:T(2,128)(2,1)} %bias.1) | copy-start | bytes 15364
  18.2 30.5 %collective-permute-start.3 = (bf16[2,24,64,128]{3,2,1,0:T(8,128)(2,1)}, bf16[2,24,64,128]{3,2,1,0:T(8,128)(2,1)S(1)}, u32[]{:S(2)}, u32[]{:S(2)}) collective-permute-start(bf16[2,24,64,128]{3,2,1,0:T(8,128)(2,1)} %get-tuple-element.33), channel_id=1, source_target_pairs={{0,4},{4,0},{8,12},{12,8},{1,5},{5,1},{9,13},{13,9},{2,6},{6,2},{1... | collective-permute-start | bytes 2359304 | tf_op jit(solution)/shard_map/ppermute | solution.py:698
  18.4 8.6 %all-to-all-start = ((bf16[4,2,9472]{2,1,0:T(2,128)(2,1)}), bf16[4,2,9472]{2,1,0:T(2,128)(2,1)S(1)}, u32[]{:S(2)}, u32[]{:S(2)}) async-start(bf16[4,2,9472]{2,1,0:T(2,128)(2,1)} %tokens.1.refs_0_), calls=%async_computation | async-start | bytes 303104 | tf_op jit(solution)/shard_map/all_to_all | solution.py:704
  21.8 26.9 %collective-permute-start.4 = (bf16[2,16,64,128]{3,2,1,0:T(8,128)(2,1)S(1)}, bf16[2,16,64,128]{3,2,1,0:T(8,128)(2,1)S(1)}, u32[]{:S(2)}, u32[]{:S(2)}) collective-permute-start(bf16[2,16,64,128]{3,2,1,0:T(8,128)(2,1)S(1)} %get-tuple-element.30.refs_4_.refs_0_), channel_id=1, source_target_pairs={{0,8},{4,12},{8,0},{12,4},{1,9},{5,13},{9,1},{13,5},{2,10},{6,14},... | collective-permute-start | bytes 1572872 | tf_op jit(solution)/shard_map/ppermute | solution.py:698
  23.8 24.9 %collective-permute-start.5 = (bf16[2,16,64,128]{3,2,1,0:T(8,128)(2,1)}, bf16[2,16,64,128]{3,2,1,0:T(8,128)(2,1)}, u32[]{:S(2)}, u32[]{:S(2)}) collective-permute-start(bf16[2,16,64,128]{3,2,1,0:T(8,128)(2,1)} %copy-done.16), channel_id=1, source_target_pairs={{0,12},{4,8},{8,4},{12,0},{1,13},{5,9},{9,5},{13,1},{2,14},{6,10},... | collective-permute-start | bytes 1572872 | tf_op jit(solution)/shard_map/ppermute | solution.py:698
  29.7 19.0 %collective-permute-start.6 = (bf16[4,8,64,128]{3,2,1,0:T(8,128)(2,1)S(1)}, bf16[4,8,64,128]{3,2,1,0:T(8,128)(2,1)S(1)}, u32[]{:S(2)}, u32[]{:S(2)}) collective-permute-start(bf16[4,8,64,128]{3,2,1,0:T(8,128)(2,1)S(1)} %get-tuple-element.31.refs_0_), channel_id=1, source_target_pairs={{0,1},{1,0},{2,3},{3,2},{4,5},{5,4},{6,7},{7,6},{8,9},{9,8},{10,11... | collective-permute-start | bytes 1572872 | tf_op jit(solution)/shard_map/ppermute | solution.py:698
  34.6 18.1 %copy-start.10 = (bf16[2,8,64,128]{3,2,1,0:T(8,128)(2,1)}, bf16[2,8,64,128]{3,2,1,0:T(8,128)(2,1)S(1)}, u32[]{:S(2)}) copy-start(bf16[2,8,64,128]{3,2,1,0:T(8,128)(2,1)S(1)} %get-tuple-element.35.refs_4_) | copy-start | bytes 786436
  34.6 20.1 %copy-start.17 = (bf16[2,8,64,128]{3,2,1,0:T(8,128)(2,1)}, bf16[2,8,64,128]{3,2,1,0:T(8,128)(2,1)S(1)}, u32[]{:S(2)}) copy-start(bf16[2,8,64,128]{3,2,1,0:T(8,128)(2,1)S(1)} %get-tuple-element.39) | copy-start | bytes 786436
  52.6 34.0 %collective-permute-start.10 = (bf16[4,16,64,128]{3,2,1,0:T(8,128)(2,1)}, bf16[4,16,64,128]{3,2,1,0:T(8,128)(2,1)S(1)}, u32[]{:S(2)}, u32[]{:S(2)}) collective-permute-start(bf16[4,16,64,128]{3,2,1,0:T(8,128)(2,1)} %get-tuple-element.36.refs_0_), channel_id=1, source_target_pairs={{0,1},{1,0},{2,3},{3,2},{4,5},{5,4},{6,7},{7,6},{8,9},{9,8},{10,11... | collective-permute-start | bytes 3145736 | tf_op jit(solution)/shard_map/ppermute | solution.py:698
  54.7 12.8 %all-to-all-start.1 = ((bf16[4,32,2048]{2,1,0:T(8,128)(2,1)}), bf16[4,32,2048]{2,1,0:T(8,128)(2,1)S(1)}, u32[]{:S(2)}, u32[]{:S(2)}) async-start(bf16[4,32,2048]{2,1,0:T(8,128)(2,1)} %rows.1.refs_6_), calls=%async_computation.1 | async-start | bytes 1048576 | tf_op jit(solution)/shard_map/all_to_all | solution.py:704
  58.1 19.1 %collective-permute-start.8 = (bf16[2,8,64,128]{3,2,1,0:T(8,128)(2,1)}, bf16[2,8,64,128]{3,2,1,0:T(8,128)(2,1)S(1)}, u32[]{:S(2)}, u32[]{:S(2)}) collective-permute-start(bf16[2,8,64,128]{3,2,1,0:T(8,128)(2,1)} %copy-done.17), channel_id=1, source_target_pairs={{0,12},{4,8},{8,4},{12,0},{1,13},{5,9},{9,5},{13,1},{2,14},{6,10},... | collective-permute-start | bytes 786440 | tf_op jit(solution)/shard_map/ppermute | solution.py:698
  59.9 18.4 %collective-permute-start.7 = (bf16[2,8,64,128]{3,2,1,0:T(8,128)(2,1)}, bf16[2,8,64,128]{3,2,1,0:T(8,128)(2,1)}, u32[]{:S(2)}, u32[]{:S(2)}) collective-permute-start(bf16[2,8,64,128]{3,2,1,0:T(8,128)(2,1)} %copy-done.10), channel_id=1, source_target_pairs={{0,8},{4,12},{8,0},{12,4},{1,9},{5,13},{9,1},{13,5},{2,10},{6,14},... | collective-permute-start | bytes 786440 | tf_op jit(solution)/shard_map/ppermute | solution.py:698
  73.1 17.0 %all-to-all-start.2 = ((bf16[4,16,2048]{2,1,0:T(8,128)(2,1)}), bf16[4,16,2048]{2,1,0:T(8,128)(2,1)}, u32[]{:S(2)}, u32[]{:S(2)}) async-start(bf16[4,16,2048]{2,1,0:T(8,128)(2,1)} %get-tuple-element.38.refs_4_), calls=%async_computation.2 | async-start | bytes 524288 | tf_op jit(solution)/shard_map/all_to_all | solution.py:704
  80.0 6.5 %collective-permute-start.9 = (bf16[4,13440]{1,0:T(4,128)(2,1)S(1)}, bf16[4,13440]{1,0:T(4,128)(2,1)S(1)}, u32[]{:S(2)}, u32[]{:S(2)}) collective-permute-start(bf16[4,13440]{1,0:T(4,128)(2,1)S(1)} %get-tuple-element.41), channel_id=1, source_target_pairs={{0,1},{1,0},{2,3},{3,2},{4,5},{5,4},{6,7},{7,6},{8,9},{9,8},{10,11... | collective-permute-start | bytes 322568 | tf_op jit(solution)/shard_map/ppermute | solution.py:698
  90.0 13.8 %copy-start.9 = (bf16[4,8,64,128]{3,2,1,0:T(8,128)(2,1)S(1)}, bf16[4,8,64,128]{3,2,1,0:T(8,128)(2,1)}, u32[]{:S(2)}) copy-start(bf16[4,8,64,128]{3,2,1,0:T(8,128)(2,1)} %copy-done.8) | copy-start | bytes 1572868
  90.0 13.8 %collective-permute-start.11 = (bf16[4,8,64,128]{3,2,1,0:T(8,128)(2,1)}, bf16[4,8,64,128]{3,2,1,0:T(8,128)(2,1)}, u32[]{:S(2)}, u32[]{:S(2)}) collective-permute-start(bf16[4,8,64,128]{3,2,1,0:T(8,128)(2,1)} %get-tuple-element.43.refs_8_.refs_0_), channel_id=1, source_target_pairs={{0,1},{1,0},{2,3},{3,2},{4,5},{5,4},{6,7},{7,6},{8,9},{9,8},{10,11... | collective-permute-start | bytes 1572872 | tf_op jit(solution)/shard_map/ppermute | solution.py:698
  (16 other events, 39.5 us)

commit v6 on v5

--- a/solution.py
+++ b/solution.py
@@ -21,8 +21,8 @@
 PARTS = 4
 BLOCKS = 8
 LANES = 128
-VMEM_LIMIT = 48 * 1024 * 1024
-VMEM_LARGE = 48 * 1024 * 1024
+VMEM_LIMIT = 53 * 1024 * 1024
+VMEM_LARGE = 53 * 1024 * 1024
 ANY = pl.BlockSpec(memory_space=pl.ANY)
 HBM = pl.BlockSpec(memory_space=pltpu.HBM)
 
@@ -761,7 +761,7 @@
 
     own, give = split_slots(plan, table, result, xbc, far[2])
     other = swap(give)
-    route(2, near, far[2], [sums, other, gots[1]])
+    route(2, near, far[2], [other, gots[1]])
     _, last_at, decay_at, end = packet_places(groups, conv_width)
     low_at = -(-end // channels) * channels
     fresh_at = low_at + LANES

time: 108 us -> 107 us (level)
  Pallas kernels: 45.9 us -> 51.8 us
  local copies, waits for them, and re-layouts: 11.3 us -> 5.66 us
  other arithmetic: 2.67 us -> 0.79 us
  waiting for transfers between devices: 22.7 us -> 23.9 us
    unnamed x52 -> x44, local copies, waits for them, and re-layouts: 11.2 us -> 5.58 us
    pallas_call x3, Pallas kernels: 8.72 us -> 11.3 us  [finish_chunk(): pl.pallas_call(functools.partial(finish_kernel, plan, width, heads, first...]
    pallas_call x3, Pallas kernels: 7.26 us -> 9.62 us  [route_chunk(): pl.pallas_call(functools.partial(route_kernel, plan, len(near) + len(far)...]
    ppermute x12, waiting for transfers between devices: 12.3 us -> 13.5 us  [shifted(): lax.ppermute(value, axis, [(i, i ^ shift) for i in range(lax.axis_size(ax...]
  transfers between devices with their start and end apart: 15 -> 15, of which waited for: 6 -> 6; matrix products, arithmetic and copies ran while one was open for 3% -> 1% of each run, Pallas kernels for 33% -> 38%
where the time goes in v6:
time: 107 us
  Pallas kernels  51.8 us (48%)
  waiting for transfers between devices  23.9 us (22%)
  starting transfers between devices  23.5 us (22%)
  local copies, waits for them, and re-layouts  5.66 us (5%)
    ppermute x12, waiting for transfers between devices, shifted(): lax.ppermute(value, axis, [(i, i ^ shift) for i in range(lax.axis_size(ax...  13.5 us
    ppermute x12, starting transfers between devices, shifted(): lax.ppermute(value, axis, [(i, i ^ shift) for i in range(lax.axis_size(ax...  12.8 us
    pallas_call x3, Pallas kernels, finish_chunk(): pl.pallas_call(functools.partial(finish_kernel, plan, width, heads, first...  11.3 us
    pallas_call x4, Pallas kernels, pack_rows(): pl.pallas_call(functools.partial(pack_kernel, plan, places, first), grid_...  11.1 us
    all_to_all x3, starting transfers between devices, exchange(): return lax.all_to_all(value, axis, split_axis=0, concat_axis=0, tiled=True)  10.7 us
    all_to_all x3, waiting for transfers between devices, exchange(): return lax.all_to_all(value, axis, split_axis=0, concat_axis=0, tiled=True)  10.4 us
    pallas_call x3, Pallas kernels, route_chunk(): pl.pallas_call(functools.partial(route_kernel, plan, len(near) + len(far)...  9.62 us
    pallas_call x1, Pallas kernels, run_rows(): pl.pallas_call(functools.partial(rows_kernel, plan), grid_spec=pltpu.Pref...  8.58 us
  transfers between devices with their start and end apart: 15, of which 6 were waited for; matrix products, arithmetic and copies ran while one was open for 1% of the time, Pallas kernels for 38%

profile of v6, /device:TPU:0, one launch (start us, length us, event | category | flops | bytes accessed | tf_op | source)
XLA Modules:
  0.0 106.6 jit_solution(4783167888250030352)
XLA Ops:
  3.6 2.8 %pack_0_8.1 = (bf16[2,8,64,128]{3,2,1,0:T(8,128)(2,1)S(1)}, bf16[2,8,64,128]{3,2,1,0:T(8,128)(2,1)S(1)}, bf16[2,8,64,128]{3,2,1,0:T(8,128)(2,1)S(1)}, bf16[2,8,64,128]{3,2,1,0:T(8,128)(2,1)}) custom-call(s32[68]{0:T(128)S(1)} %plan.1.table, f32[8,32,64,128]{3,2,1,0:T(8,128)} %state.9), custom_call_target="tpu_custom_call" | custom-call | tf_op jit(solution)/shard_map/pack_0_8/pallas_call | solution.py:541
  7.0 2.6 %collective-permute-start.1 = (bf16[2,8,64,128]{3,2,1,0:T(8,128)(2,1)S(1)}, bf16[2,8,64,128]{3,2,1,0:T(8,128)(2,1)S(1)}, u32[]{:S(2)}, u32[]{:S(2)}) collective-permute-start(bf16[2,8,64,128]{3,2,1,0:T(8,128)(2,1)S(1)} %get-tuple-element.28), channel_id=1, source_target_pairs={{0,8},{4,12},{8,0},{12,4},{1,9},{5,13},{9,1},{13,5},{2,10},{6,14},... | collective-permute-start | bytes 786440 | tf_op jit(solution)/shard_map/ppermute | solution.py:698
  11.1 2.9 %pack_16_16.1 = (bf16[2,16,64,128]{3,2,1,0:T(8,128)(2,1)S(1)}, bf16[2,16,64,128]{3,2,1,0:T(8,128)(2,1)}) custom-call(s32[68]{0:T(128)S(1)} %plan.1.table, f32[8,32,64,128]{3,2,1,0:T(8,128)} %state.9, bf16[4,2,9472]{2,1,0:T(2,128)(2,1)} %tokens.1.refs_0_), custom_call_target="tpu_custom_call" | custom-call | tf_op jit(solution)/shard_map/pack_16_16/pallas_call | solution.py:541
  14.1 3.6 %pack_8_24.1 = (bf16[2,24,64,128]{3,2,1,0:T(8,128)(2,1)}, bf16[2,24,64,128]{3,2,1,0:T(8,128)(2,1)}) custom-call(s32[68]{0:T(128)S(1)} %plan.1.table, f32[8,32,64,128]{3,2,1,0:T(8,128)} %state.9, bf16[2,16,64,128]{3,2,1,0:T(8,128)(2,1)S(1)} %get-tuple-element.30.refs_4_.refs_0_), custom_call_target="tpu_custom_call" | custom-call | tf_op jit(solution)/shard_map/pack_8_24/pallas_call | solution.py:541
  17.9 3.3 %all-to-all-start = ((bf16[4,2,9472]{2,1,0:T(2,128)(2,1)}), bf16[4,2,9472]{2,1,0:T(2,128)(2,1)S(1)}, u32[]{:S(2)}, u32[]{:S(2)}) async-start(bf16[4,2,9472]{2,1,0:T(2,128)(2,1)} %tokens.1.refs_0_), calls=%async_computation | async-start | bytes 303104 | tf_op jit(solution)/shard_map/all_to_all | solution.py:704
  21.2 2.0 %collective-permute-start.4 = (bf16[2,16,64,128]{3,2,1,0:T(8,128)(2,1)S(1)}, bf16[2,16,64,128]{3,2,1,0:T(8,128)(2,1)S(1)}, u32[]{:S(2)}, u32[]{:S(2)}) collective-permute-start(bf16[2,16,64,128]{3,2,1,0:T(8,128)(2,1)S(1)} %get-tuple-element.30.refs_4_.refs_0_), channel_id=1, source_target_pairs={{0,8},{4,12},{8,0},{12,4},{1,9},{5,13},{9,1},{13,5},{2,10},{6,14},... | collective-permute-start | bytes 1572872 | tf_op jit(solution)/shard_map/ppermute | solution.py:698
  23.2 3.3 %all-to-all-done.refs_5_.tokens = bf16[4,2,9472]{2,1,0:T(2,128)(2,1)S(1)} async-done(((bf16[4,2,9472]{2,1,0:T(2,128)(2,1)}), bf16[4,2,9472]{2,1,0:T(2,128)(2,1)S(1)}, u32[]{:S(2)}, u32[]{:S(2)}) %all-to-all-start) | async-done | bytes 151584 | tf_op jit(solution)/shard_map/all_to_all | solution.py:704
  27.2 2.7 %route_0_8.1 = (bf16[4,8,64,128]{3,2,1,0:T(8,128)(2,1)}, bf16[4,8,64,128]{3,2,1,0:T(8,128)(2,1)}) custom-call(s32[68]{0:T(128)S(1)} %plan.1.table, bf16[2,8,64,128]{3,2,1,0:T(8,128)(2,1)S(1)} %get-tuple-element.26.refs_0_, bf16[2,8,64,128]{3,2,1,0:T(8,128)(2,1)S(1)} %collective-permute-done.refs_1_, ...), custom_call_target="tpu_custom_call" | custom-call | tf_op jit(solution)/shard_map/route_0_8/pallas_call | solution.py:581
  30.0 2.0 %collective-permute-start.6 = (bf16[4,8,64,128]{3,2,1,0:T(8,128)(2,1)}, bf16[4,8,64,128]{3,2,1,0:T(8,128)(2,1)S(1)}, u32[]{:S(2)}, u32[]{:S(2)}) collective-permute-start(bf16[4,8,64,128]{3,2,1,0:T(8,128)(2,1)} %get-tuple-element.31.refs_0_), channel_id=1, source_target_pairs={{0,1},{1,0},{2,3},{3,2},{4,5},{5,4},{6,7},{7,6},{8,9},{9,8},{10,11... | collective-permute-start | bytes 1572872 | tf_op jit(solution)/shard_map/ppermute | solution.py:698
  33.9 8.6 %rows.1.refs_6_ = bf16[4,32,2048]{2,1,0:T(8,128)(2,1)S(1)} custom-call(s32[68]{0:T(128)S(1)} %plan.1.table, bf16[4,2,9472]{2,1,0:T(2,128)(2,1)S(1)} %all-to-all-done.refs_5_.tokens, f32[3,2,8,1280]{3,2,1,0:T(8,128)S(1)} %bitcast.16, bf16[4,2,1280]{2,1,0:T(2,128)(2,1)S(1)} %copy-done.7, bf16[2,1280]{1,0:T(2,128)(2,1)S(1)} %copy-done.8, ...), custom_call_target="tpu_custom_call" | custom-call | tf_op jit(solution)/shard_map/rows/pallas_call | solution.py:324
  43.3 4.9 %collective-permute-done.5.refs_3_ = bf16[2,16,64,128]{3,2,1,0:T(8,128)(2,1)} collective-permute-done((bf16[2,16,64,128]{3,2,1,0:T(8,128)(2,1)}, bf16[2,16,64,128]{3,2,1,0:T(8,128)(2,1)}, u32[]{:S(2)}, u32[]{:S(2)}) %collective-permute-start.5) | collective-permute-done | bytes 524320 | tf_op jit(solution)/shard_map/ppermute | solution.py:698
  48.9 3.7 %route_16_16.1 = (bf16[4,16,64,128]{3,2,1,0:T(8,128)(2,1)}, bf16[4,16,64,128]{3,2,1,0:T(8,128)(2,1)}) custom-call(s32[68]{0:T(128)S(1)} %plan.1.table, bf16[2,24,64,128]{3,2,1,0:T(8,128)(2,1)} %get-tuple-element.32.refs_0_, bf16[2,24,64,128]{3,2,1,0:T(8,128)(2,1)} %collective-permute-done.3.refs_1_, ...), custom_call_target="tpu_custom_call" | custom-call | tf_op jit(solution)/shard_map/route_16_16/pallas_call | solution.py:581
  52.7 2.0 %collective-permute-start.10 = (bf16[4,16,64,128]{3,2,1,0:T(8,128)(2,1)}, bf16[4,16,64,128]{3,2,1,0:T(8,128)(2,1)}, u32[]{:S(2)}, u32[]{:S(2)}) collective-permute-start(bf16[4,16,64,128]{3,2,1,0:T(8,128)(2,1)} %get-tuple-element.36.refs_0_), channel_id=1, source_target_pairs={{0,1},{1,0},{2,3},{3,2},{4,5},{5,4},{6,7},{7,6},{8,9},{9,8},{10,11... | collective-permute-start | bytes 3145736 | tf_op jit(solution)/shard_map/ppermute | solution.py:698
  54.7 3.5 %all-to-all-start.1 = ((bf16[4,32,2048]{2,1,0:T(8,128)(2,1)}), bf16[4,32,2048]{2,1,0:T(8,128)(2,1)S(1)}, u32[]{:S(2)}, u32[]{:S(2)}) async-start(bf16[4,32,2048]{2,1,0:T(8,128)(2,1)} %copy-done.1), calls=%async_computation.1 | async-start | bytes 1048576 | tf_op jit(solution)/shard_map/all_to_all | solution.py:704
  60.3 7.1 %all-to-all-done.1.normed.packets = bf16[4,32,2048]{2,1,0:T(8,128)(2,1)S(1)} async-done(((bf16[4,32,2048]{2,1,0:T(8,128)(2,1)}), bf16[4,32,2048]{2,1,0:T(8,128)(2,1)S(1)}, u32[]{:S(2)}, u32[]{:S(2)}) %all-to-all-start.1) | async-done | bytes 524320 | tf_op jit(solution)/shard_map/all_to_all | solution.py:704
  67.4 5.0 %project.1 = (f32[16,2048]{1,0:T(8,128)S(1)}, bf16[4,16,2048]{2,1,0:T(8,128)(2,1)}) custom-call(s32[68]{0:T(128)S(1)} %plan.1.table, bf16[4,32,2048]{2,1,0:T(8,128)(2,1)S(1)} %all-to-all-done.1.normed.packets, bf16[2048,2048]{1,0:T(8,128)(2,1)} %weight.3, bf16[4,16,64,128]{3,2,1,0:T(8,128)(2,1)} %get-tuple-element.36.refs_0_), custom_call_target="tpu_custom_call" | custom-call | tf_op jit(solution)/shard_map/project/pallas_call | solution.py:407
  72.5 3.9 %all-to-all-start.2 = ((bf16[4,16,2048]{2,1,0:T(8,128)(2,1)}), bf16[4,16,2048]{2,1,0:T(8,128)(2,1)S(1)}, u32[]{:S(2)}, u32[]{:S(2)}) async-start(bf16[4,16,2048]{2,1,0:T(8,128)(2,1)} %get-tuple-element.38), calls=%async_computation.2 | async-start | bytes 524288 | tf_op jit(solution)/shard_map/all_to_all | solution.py:704
  76.4 1.8 %collective-permute-done.7.refs_0_.refs_2_ = bf16[2,8,64,128]{3,2,1,0:T(8,128)(2,1)S(1)} collective-permute-done((bf16[2,8,64,128]{3,2,1,0:T(8,128)(2,1)S(1)}, bf16[2,8,64,128]{3,2,1,0:T(8,128)(2,1)S(1)}, u32[]{:S(2)}, u32[]{:S(2)}) %collective-permute-start.7) | collective-permute-done | bytes 262176 | tf_op jit(solution)/shard_map/ppermute | solution.py:698
  78.2 1.8 %slots.1 = (bf16[4,13440]{1,0:T(4,128)(2,1)S(1)}, bf16[4,13440]{1,0:T(4,128)(2,1)S(1)}) custom-call(s32[68]{0:T(128)S(1)} %plan.1.table, bf16[4,32,2048]{2,1,0:T(8,128)(2,1)} %copy-done, bf16[2,2,8,1280]{3,2,1,0:T(8,128)(2,1)S(1)} %bitcast.18, bf16[2,8,64,128]{3,2,1,0:T(8,128)(2,1)S(1)} %collective-permute-done.7.refs_0_.refs_2_, ...), custom_call_target="tpu_custom_call" | custom-call | tf_op jit(solution)/shard_map/slots/pallas_call | solution.py:471
  80.3 5.4 %collective-permute-done.9.refs_4_.refs_5_.refs_6_.refs_7_.got = bf16[4,13440]{1,0:T(4,128)(2,1)S(1)} collective-permute-done((bf16[4,13440]{1,0:T(4,128)(2,1)S(1)}, bf16[4,13440]{1,0:T(4,128)(2,1)S(1)}, u32[]{:S(2)}, u32[]{:S(2)}) %collective-permute-start.9) | collective-permute-done | bytes 107552 | tf_op jit(solution)/shard_map/ppermute | solution.py:698
  85.8 3.2 %route_8_8.1 = (bf16[4,8,64,128]{3,2,1,0:T(8,128)(2,1)}, bf16[4,8,64,128]{3,2,1,0:T(8,128)(2,1)}) custom-call(s32[68]{0:T(128)S(1)} %plan.1.table, bf16[2,24,64,128]{3,2,1,0:T(8,128)(2,1)} %get-tuple-element.32.refs_0_, bf16[2,24,64,128]{3,2,1,0:T(8,128)(2,1)} %collective-permute-done.3.refs_1_, ...), custom_call_target="tpu_custom_call" | custom-call | tf_op jit(solution)/shard_map/route_8_8/pallas_call | solution.py:581
  93.2 3.3 %finish_0_8.1 = (f32[1,1,4,64,64,128]{5,4,3,2,1,0:T(8,128)}, f32[8,128]{1,0:T(8,128)}) custom-call(s32[68]{0:T(128)S(1)} %plan.1.table, f32[256]{0:T(256)S(1)} %reshape.17.decay, bf16[4,8,64,128]{3,2,1,0:T(8,128)(2,1)S(1)} %copy-done.4, bf16[4,8,64,128]{3,2,1,0:T(8,128)(2,1)} %copy-done.12, ...), custom_call_target="tpu_custom_call" | custom-call | tf_op jit(solution)/shard_map/finish_0_8/pallas_call | solution.py:650
  96.5 4.6 %finish_16_16.1 = (f32[1,1,4,64,64,128]{5,4,3,2,1,0:T(8,128)}, f32[8,128]{1,0:T(8,128)}) custom-call(s32[68]{0:T(128)S(1)} %plan.1.table, f32[256]{0:T(256)S(1)} %reshape.17.decay, bf16[4,16,64,128]{3,2,1,0:T(8,128)(2,1)} %get-tuple-element.44.keep, bf16[4,16,64,128]{3,2,1,0:T(8,128)(2,1)} %collective-permute-done.10.refs_5_.got, ...), custom_call_target="tpu_custom_call", output_to_operand_aliasing={{0}: (12, {})} | custom-call | tf_op jit(solution)/shard_map/finish_16_16/pallas_call | solution.py:650
  103.3 3.3 %finish_8_8.1 = (f32[1,1,4,64,64,128]{5,4,3,2,1,0:T(8,128)}, f32[8,128]{1,0:T(8,128)}) custom-call(s32[68]{0:T(128)S(1)} %plan.1.table, f32[256]{0:T(256)S(1)} %reshape.17.decay, bf16[4,8,64,128]{3,2,1,0:T(8,128)(2,1)S(1)} %copy-done.5, bf16[4,8,64,128]{3,2,1,0:T(8,128)(2,1)} %copy-done.13, ...), custom_call_target="tpu_custom_call", output_to_operand_aliasing={{0}: (12, {})} | custom-call | tf_op jit(solution)/shard_map/finish_8_8/pallas_call | solution.py:650
  (73 shorter events, 18.2 us)
Async XLA Ops:
  6.5 16.7 %collective-permute-start = (bf16[2,8,64,128]{3,2,1,0:T(8,128)(2,1)S(1)}, bf16[2,8,64,128]{3,2,1,0:T(8,128)(2,1)S(1)}, u32[]{:S(2)}, u32[]{:S(2)}) collective-permute-start(bf16[2,8,64,128]{3,2,1,0:T(8,128)(2,1)S(1)} %get-tuple-element.27), channel_id=1, source_target_pairs={{0,4},{4,0},{8,12},{12,8},{1,5},{5,1},{9,13},{13,9},{2,6},{6,2},{1... | collective-permute-start | bytes 786440 | tf_op jit(solution)/shard_map/ppermute | solution.py:698
  7.0 19.5 %collective-permute-start.1 = (bf16[2,8,64,128]{3,2,1,0:T(8,128)(2,1)S(1)}, bf16[2,8,64,128]{3,2,1,0:T(8,128)(2,1)S(1)}, u32[]{:S(2)}, u32[]{:S(2)}) collective-permute-start(bf16[2,8,64,128]{3,2,1,0:T(8,128)(2,1)S(1)} %get-tuple-element.28), channel_id=1, source_target_pairs={{0,8},{4,12},{8,0},{12,4},{1,9},{5,13},{9,1},{13,5},{2,10},{6,14},... | collective-permute-start | bytes 786440 | tf_op jit(solution)/shard_map/ppermute | solution.py:698
  9.6 16.9 %collective-permute-start.2 = (bf16[2,8,64,128]{3,2,1,0:T(8,128)(2,1)}, bf16[2,8,64,128]{3,2,1,0:T(8,128)(2,1)S(1)}, u32[]{:S(2)}, u32[]{:S(2)}) collective-permute-start(bf16[2,8,64,128]{3,2,1,0:T(8,128)(2,1)} %get-tuple-element.29), channel_id=1, source_target_pairs={{0,12},{4,8},{8,4},{12,0},{1,13},{5,9},{9,5},{13,1},{2,14},{6,10},... | collective-permute-start | bytes 786440 | tf_op jit(solution)/shard_map/ppermute | solution.py:698
  11.1 20.9 %copy-start.17 = (bf16[2048]{0:T(1024)(128)(2,1)S(1)}, bf16[2048]{0:T(1024)(128)(2,1)}, u32[]{:S(2)}) copy-start(bf16[2048]{0:T(1024)(128)(2,1)} %param.26) | copy-start | bytes 12292
  11.1 20.9 %copy-start.15 = (f32[8,3,2,1280]{3,2,1,0:T(2,128)S(1)}, f32[8,3,2,1280]{3,2,1,0:T(2,128)}, u32[]{:S(2)}) copy-start(f32[8,3,2,1280]{3,2,1,0:T(2,128)} %param.15) | copy-start | bytes 737284
  11.1 20.9 %copy-start.18 = (bf16[32]{0:T(256)(128)(2,1)S(1)}, bf16[32]{0:T(256)(128)(2,1)}, u32[]{:S(2)}) copy-start(bf16[32]{0:T(256)(128)(2,1)} %param.25) | copy-start | bytes 196
  11.1 20.9 %copy-start.19 = (bf16[32]{0:T(256)(128)(2,1)S(1)}, bf16[32]{0:T(256)(128)(2,1)}, u32[]{:S(2)}) copy-start(bf16[32]{0:T(256)(128)(2,1)} %param.24) | copy-start | bytes 196
  11.1 20.9 %copy-start.20 = (bf16[32]{0:T(256)(128)(2,1)S(1)}, bf16[32]{0:T(256)(128)(2,1)}, u32[]{:S(2)}) copy-start(bf16[32]{0:T(256)(128)(2,1)} %param.23) | copy-start | bytes 196
  14.1 19.8 %copy-start.7 = (bf16[4,2,1280]{2,1,0:T(2,128)(2,1)S(1)}, bf16[4,2,1280]{2,1,0:T(2,128)(2,1)}, u32[]{:S(2)}) copy-start(bf16[4,2,1280]{2,1,0:T(2,128)(2,1)} %weight.2) | copy-start | bytes 61444
  14.1 19.8 %copy-start.8 = (bf16[2,1280]{1,0:T(2,128)(2,1)S(1)}, bf16[2,1280]{1,0:T(2,128)(2,1)}, u32[]{:S(2)}) copy-start(bf16[2,1280]{1,0:T(2,128)(2,1)} %bias.1) | copy-start | bytes 15364
  17.7 30.5 %collective-permute-start.3 = (bf16[2,24,64,128]{3,2,1,0:T(8,128)(2,1)}, bf16[2,24,64,128]{3,2,1,0:T(8,128)(2,1)}, u32[]{:S(2)}, u32[]{:S(2)}) collective-permute-start(bf16[2,24,64,128]{3,2,1,0:T(8,128)(2,1)} %get-tuple-element.33), channel_id=1, source_target_pairs={{0,4},{4,0},{8,12},{12,8},{1,5},{5,1},{9,13},{13,9},{2,6},{6,2},{1... | collective-permute-start | bytes 2359304 | tf_op jit(solution)/shard_map/ppermute | solution.py:698
  17.9 8.6 %all-to-all-start = ((bf16[4,2,9472]{2,1,0:T(2,128)(2,1)}), bf16[4,2,9472]{2,1,0:T(2,128)(2,1)S(1)}, u32[]{:S(2)}, u32[]{:S(2)}) async-start(bf16[4,2,9472]{2,1,0:T(2,128)(2,1)} %tokens.1.refs_0_), calls=%async_computation | async-start | bytes 303104 | tf_op jit(solution)/shard_map/all_to_all | solution.py:704
  21.2 26.9 %collective-permute-start.4 = (bf16[2,16,64,128]{3,2,1,0:T(8,128)(2,1)S(1)}, bf16[2,16,64,128]{3,2,1,0:T(8,128)(2,1)S(1)}, u32[]{:S(2)}, u32[]{:S(2)}) collective-permute-start(bf16[2,16,64,128]{3,2,1,0:T(8,128)(2,1)S(1)} %get-tuple-element.30.refs_4_.refs_0_), channel_id=1, source_target_pairs={{0,8},{4,12},{8,0},{12,4},{1,9},{5,13},{9,1},{13,5},{2,10},{6,14},... | collective-permute-start | bytes 1572872 | tf_op jit(solution)/shard_map/ppermute | solution.py:698
  23.2 24.9 %collective-permute-start.5 = (bf16[2,16,64,128]{3,2,1,0:T(8,128)(2,1)}, bf16[2,16,64,128]{3,2,1,0:T(8,128)(2,1)}, u32[]{:S(2)}, u32[]{:S(2)}) collective-permute-start(bf16[2,16,64,128]{3,2,1,0:T(8,128)(2,1)} %get-tuple-element.34), channel_id=1, source_target_pairs={{0,12},{4,8},{8,4},{12,0},{1,13},{5,9},{9,5},{13,1},{2,14},{6,10},... | collective-permute-start | bytes 1572872 | tf_op jit(solution)/shard_map/ppermute | solution.py:698
  30.0 18.2 %collective-permute-start.6 = (bf16[4,8,64,128]{3,2,1,0:T(8,128)(2,1)}, bf16[4,8,64,128]{3,2,1,0:T(8,128)(2,1)S(1)}, u32[]{:S(2)}, u32[]{:S(2)}) collective-permute-start(bf16[4,8,64,128]{3,2,1,0:T(8,128)(2,1)} %get-tuple-element.31.refs_0_), channel_id=1, source_target_pairs={{0,1},{1,0},{2,3},{3,2},{4,5},{5,4},{6,7},{7,6},{8,9},{9,8},{10,11... | collective-permute-start | bytes 1572872 | tf_op jit(solution)/shard_map/ppermute | solution.py:698
  52.7 33.2 %collective-permute-start.10 = (bf16[4,16,64,128]{3,2,1,0:T(8,128)(2,1)}, bf16[4,16,64,128]{3,2,1,0:T(8,128)(2,1)}, u32[]{:S(2)}, u32[]{:S(2)}) collective-permute-start(bf16[4,16,64,128]{3,2,1,0:T(8,128)(2,1)} %get-tuple-element.36.refs_0_), channel_id=1, source_target_pairs={{0,1},{1,0},{2,3},{3,2},{4,5},{5,4},{6,7},{7,6},{8,9},{9,8},{10,11... | collective-permute-start | bytes 3145736 | tf_op jit(solution)/shard_map/ppermute | solution.py:698
  54.7 12.8 %all-to-all-start.1 = ((bf16[4,32,2048]{2,1,0:T(8,128)(2,1)}), bf16[4,32,2048]{2,1,0:T(8,128)(2,1)S(1)}, u32[]{:S(2)}, u32[]{:S(2)}) async-start(bf16[4,32,2048]{2,1,0:T(8,128)(2,1)} %copy-done.1), calls=%async_computation.1 | async-start | bytes 1048576 | tf_op jit(solution)/shard_map/all_to_all | solution.py:704
  58.2 35.0 %copy-start.4 = (bf16[4,8,64,128]{3,2,1,0:T(8,128)(2,1)S(1)}, bf16[4,8,64,128]{3,2,1,0:T(8,128)(2,1)}, u32[]{:S(2)}) copy-start(bf16[4,8,64,128]{3,2,1,0:T(8,128)(2,1)} %get-tuple-element.45.keep) | copy-start | bytes 1572868
  58.2 18.2 %collective-permute-start.8 = (bf16[2,8,64,128]{3,2,1,0:T(8,128)(2,1)S(1)}, bf16[2,8,64,128]{3,2,1,0:T(8,128)(2,1)S(1)}, u32[]{:S(2)}, u32[]{:S(2)}) collective-permute-start(bf16[2,8,64,128]{3,2,1,0:T(8,128)(2,1)S(1)} %get-tuple-element.39), channel_id=1, source_target_pairs={{0,12},{4,8},{8,4},{12,0},{1,13},{5,9},{9,5},{13,1},{2,14},{6,10},... | collective-permute-start | bytes 786440 | tf_op jit(solution)/shard_map/ppermute | solution.py:698
  59.9 18.3 %collective-permute-start.7 = (bf16[2,8,64,128]{3,2,1,0:T(8,128)(2,1)S(1)}, bf16[2,8,64,128]{3,2,1,0:T(8,128)(2,1)S(1)}, u32[]{:S(2)}, u32[]{:S(2)}) collective-permute-start(bf16[2,8,64,128]{3,2,1,0:T(8,128)(2,1)S(1)} %get-tuple-element.35.refs_4_), channel_id=1, source_target_pairs={{0,8},{4,12},{8,0},{12,4},{1,9},{5,13},{9,1},{13,5},{2,10},{6,14},... | collective-permute-start | bytes 786440 | tf_op jit(solution)/shard_map/ppermute | solution.py:698
  72.5 17.6 %all-to-all-start.2 = ((bf16[4,16,2048]{2,1,0:T(8,128)(2,1)}), bf16[4,16,2048]{2,1,0:T(8,128)(2,1)S(1)}, u32[]{:S(2)}, u32[]{:S(2)}) async-start(bf16[4,16,2048]{2,1,0:T(8,128)(2,1)} %get-tuple-element.38), calls=%async_computation.2 | async-start | bytes 524288 | tf_op jit(solution)/shard_map/all_to_all | solution.py:704
  80.0 5.7 %collective-permute-start.9 = (bf16[4,13440]{1,0:T(4,128)(2,1)S(1)}, bf16[4,13440]{1,0:T(4,128)(2,1)S(1)}, u32[]{:S(2)}, u32[]{:S(2)}) collective-permute-start(bf16[4,13440]{1,0:T(4,128)(2,1)S(1)} %get-tuple-element.41), channel_id=1, source_target_pairs={{0,1},{1,0},{2,3},{3,2},{4,5},{5,4},{6,7},{7,6},{8,9},{9,8},{10,11... | collective-permute-start | bytes 322568 | tf_op jit(solution)/shard_map/ppermute | solution.py:698
  89.0 14.3 %copy-start.5 = (bf16[4,8,64,128]{3,2,1,0:T(8,128)(2,1)S(1)}, bf16[4,8,64,128]{3,2,1,0:T(8,128)(2,1)}, u32[]{:S(2)}) copy-start(bf16[4,8,64,128]{3,2,1,0:T(8,128)(2,1)} %get-tuple-element.42.keep) | copy-start | bytes 1572868
  89.0 13.5 %collective-permute-start.11 = (bf16[4,8,64,128]{3,2,1,0:T(8,128)(2,1)}, bf16[4,8,64,128]{3,2,1,0:T(8,128)(2,1)S(1)}, u32[]{:S(2)}, u32[]{:S(2)}) collective-permute-start(bf16[4,8,64,128]{3,2,1,0:T(8,128)(2,1)} %get-tuple-element.43.refs_8_.refs_0_), channel_id=1, source_target_pairs={{0,1},{1,0},{2,3},{3,2},{4,5},{5,4},{6,7},{7,6},{8,9},{9,8},{10,11... | collective-permute-start | bytes 1572872 | tf_op jit(solution)/shard_map/ppermute | solution.py:698
  (12 other events, 54.4 us)
